TPU v7x, 32 devices: a whole 2x2x4 slice. The times are simulated.
32 devices in a mesh: lat: 8 (over z, x), azim: 4 (over y, core).
Axes of the slice: x: 2, y: 2, z: 4, core: 2. Of those that a mesh axis runs over, the one named last changes fastest.
Arguments:
- magnetic: float32 [3, 32, 256, 2048], P(None, None, 'lat', 'azim'), may hold values from -6 to 6
- kept_modes: int32 [256], replicated, may hold values from 1 to 1024, as said below
Outputs:
- current_density: float32 [3, 32, 256, 2048], P(None, None, 'lat', 'azim')
Inputs may be any that keep to these rules, and one draw needn't show every extreme that they name: `kept_modes`: at latitude 256 // 2 all 1024 modes are kept.
All inputs are finite; a program needn't handle non-finite values.
Results may differ from a plain program's by a relative error of at most 0.000068.
Values sent between devices are 32-bit elements; how exact they have to be, the bound alone decides.
No kernel may reach another device: no remote copies, remote signals or barrier semaphores. Data moves between devices by JAX's collectives and lax.ppermute only.
A program may use at most 64 MiB of HBM per device.

v0:
```python
import math

import jax
import jax.numpy as jnp
from jax import lax
from jax.sharding import PartitionSpec as P

MB = 128


inner_radius = 0.7
stencil_coeffs = (-1.0 / 60.0, 3.0 / 20.0, -3.0 / 4.0, 0.0, 3.0 / 4.0, -3.0 / 20.0, 1.0 / 60.0)


def extended(value, sides, width):
    for axis, dim in sides:
        size, length = (lax.axis_size(axis), value.shape[dim])
        up = [(i, (i + 1) % size) for i in range(size - 1)]
        down = [(j, i) for i, j in up]
        last = lax.slice_in_dim(value, length - width, length, axis=dim)
        first = lax.slice_in_dim(value, 0, width, axis=dim)
        before = lax.ppermute(last, axis, up)
        after = lax.ppermute(first, axis, down)
        value = jnp.concatenate([before, value, after], axis=dim)
    return value


def stencil_sum(padded, split_axis, length):
    total = jnp.zeros(lax.slice_in_dim(padded, 3, 3 + length, axis=split_axis).shape, jnp.float32)
    for offset in range(-3, 4):
        if offset != 0:
            total = total + stencil_coeffs[offset + 3] * lax.slice_in_dim(
                padded, 3 + offset, 3 + offset + length, axis=split_axis
            )
    return total


def radial_diff(values):
    widths = [(0, 0)] * values.ndim
    widths[0] = (3, 3)
    return stencil_sum(jnp.pad(values, widths), 0, values.shape[0])


def row_counts(band_counts, row_lat):
    lat_ids = jnp.arange(band_counts.shape[0], dtype=jnp.int32)
    match = row_lat[:, None] == lat_ids[None, :]
    return jnp.sum(jnp.where(match, band_counts[None, :], 0), axis=1)


def base_tables(lon_total):
    columns = jnp.arange(lon_total, dtype=jnp.int32)
    mode_ids = jnp.arange(MB, dtype=jnp.int32)
    phase = (mode_ids[:, None] * columns[None, :] % lon_total).astype(jnp.float32) * (
        2.0 * math.pi / lon_total
    )
    return (jnp.cos(phase), jnp.sin(phase))


def spectral(row_data, row_kept, base_cos, base_sin):
    lon_total = row_data.shape[1]
    block_count = (jnp.max(row_kept) + MB - 1) // MB
    columns = jnp.arange(lon_total, dtype=jnp.int32)

    def block_step(block, total):
        mode_ids = block * MB + jnp.arange(MB, dtype=jnp.int32)
        offset_phase = (block * MB * columns % lon_total).astype(jnp.float32) * (
            2.0 * math.pi / lon_total
        )
        offset_cos = jnp.cos(offset_phase)[None, :]
        offset_sin = jnp.sin(offset_phase)[None, :]
        cos_rows = base_cos * offset_cos - base_sin * offset_sin
        sin_rows = base_sin * offset_cos + base_cos * offset_sin
        table = jnp.concatenate([cos_rows, sin_rows], axis=0)
        spectrum = lax.dot_general(
            row_data,
            table,
            (((1,), (1,)), ((), ())),
            precision=lax.Precision.HIGHEST,
            preferred_element_type=jnp.float32,
        )
        weight = jnp.where(mode_ids[None, :] < row_kept[:, None], mode_ids[None, :], 0).astype(
            jnp.float32
        ) * (2.0 / lon_total)
        scaled = jnp.concatenate([spectrum[:, MB:] * weight, -spectrum[:, :MB] * weight], axis=1)
        return total + jnp.dot(
            scaled, table, precision=lax.Precision.HIGHEST, preferred_element_type=jnp.float32
        )

    return lax.fori_loop(0, block_count, block_step, jnp.zeros_like(row_data))


def on_device(magnetic, kept_modes):
    radii_count, th_dev, ph_dev = (magnetic.shape[1], magnetic.shape[2], magnetic.shape[3])
    lat_size = lax.axis_size("lat")
    lat_id = lax.axis_index("lat")
    lat_total = th_dev * lat_size
    spacing = math.pi / lat_total
    band_start = lat_id * th_dev
    colatitude = (
        (band_start + jnp.arange(th_dev, dtype=jnp.int32)).astype(jnp.float32) + 0.5
    ) * spacing
    radius = (inner_radius + (jnp.arange(radii_count, dtype=jnp.float32) + 0.5) * spacing)[
        :, None, None
    ]
    inv_sin = (1.0 / jnp.sin(colatitude))[None, :, None]
    cotangent = (jnp.cos(colatitude) / jnp.sin(colatitude))[None, :, None]
    band_counts = lax.dynamic_slice_in_dim(kept_modes, band_start, th_dev)
    theta_pair = jnp.stack([magnetic[0], magnetic[2]])
    padded = extended(theta_pair, (("lat", 2),), 3)
    theta_diff = stencil_sum(padded, 2, th_dev)
    row_data = magnetic[:2].reshape(2 * radii_count * th_dev, ph_dev)
    lined = lax.all_to_all(row_data, "azim", split_axis=0, concat_axis=1, tiled=True)
    base_cos, base_sin = base_tables(lined.shape[1])
    rows_here = lined.shape[0]
    row_start = lax.axis_index("azim") * rows_here
    row_lat = (row_start + jnp.arange(rows_here, dtype=jnp.int32)) % th_dev
    row_kept = row_counts(band_counts, row_lat)
    azimuthal = spectral(lined, row_kept, base_cos, base_sin)
    flat_rows = lax.all_to_all(azimuthal, "azim", split_axis=1, concat_axis=0, tiled=True)
    azim_diff = flat_rows.reshape(2, radii_count, th_dev, ph_dev)
    b_polar = magnetic[1]
    b_azim = magnetic[2]
    j_radial = (
        theta_diff[1] + spacing * cotangent * b_azim - spacing * inv_sin * azim_diff[1]
    ) / radius
    j_polar = (spacing * inv_sin * azim_diff[0] - radial_diff(radius * b_azim)) / radius
    j_azim = (radial_diff(radius * b_polar) - theta_diff[0]) / radius
    return jnp.stack([j_radial, j_polar, j_azim])


def solution(mesh):
    placed = (P(None, None, "lat", "azim"), P())
    return jax.shard_map(
        on_device,
        mesh=mesh,
        in_specs=placed,
        out_specs=P(None, None, "lat", "azim"),
        check_vma=False,
    )
```

profile of v0, /device:TPU:16, one launch (start us, length us, event | category | flops | bytes accessed | tf_op | source)
XLA Modules:
  0.0 278.2 jit_solution(9503430380719873657)
XLA Ops:
  0.0 5.0 %slice.116 = f32[2,32,32,512]{3,2,1,0:T(8,128)} slice(f32[3,32,32,512]{3,2,1,0:T(8,128)} %param.4), slice={[0:2], [0:32], [0:32], [0:512]} | slice | bytes 8388608 | tf_op jit(solution)/shard_map/slice | solution.py:111
  5.0 5.0 %all-to-all-start = ((f32[4,512,512]{2,1,0:T(8,128)}), f32[4,512,512]{2,1,0:T(8,128)}, u32[]{:S(2)}, u32[]{:S(2)}) async-start(f32[4,512,512]{2,1,0:T(8,128)} %bitcast.34), calls=%async_computation | async-start | bytes 8388608 | tf_op jit(solution)/shard_map/all_to_all | solution.py:112
  10.2 0.7 reduce_max.9
  11.5 46.7 %all-to-all-done = f32[4,512,512]{2,1,0:T(8,128)} async-done(((f32[4,512,512]{2,1,0:T(8,128)}), f32[4,512,512]{2,1,0:T(8,128)}, u32[]{:S(2)}, u32[]{:S(2)}) %all-to-all-start) | async-done | bytes 4194336 | tf_op jit(solution)/shard_map/all_to_all | solution.py:112
  58.2 5.2 %copy.9 = f32[4,512,512]{1,2,0:T(8,128)} copy(f32[4,512,512]{2,1,0:T(8,128)} %all-to-all-done) | data formatting | bytes 8388608 | tf_op jit(solution)/shard_map/all_to_all | solution.py:112
  63.5 5.4 %copy.10 = f32[512,2048]{1,0:T(8,128)} copy(f32[512,2048]{0,1:T(8,128)} %bitcast.36) | data formatting | bytes 8388608
  68.8 2.5 broadcast_in_dim.23
  71.3 134.9 %while.14 = (s32[]{:T(128)}, f32[512,2048]{1,0:T(8,128)}, s32[]{:T(128)}, f32[512,2048]{1,0:T(8,128)}, s32[512]{0:T(512)S(1)}, /*index=5*/s32[]{:T(128)}, s32[]{:T(128)}) while((s32[]{:T(128)}, f32[512,2048]{1,0:T(8,128)}, s32[]{:T(128)}, f32[512,2048]{1,0:T(8,128)}, s32[512]{0:T(512)S(1)}, /*index=5*/s32[]{:T(128)}, ...), condition=%wide.region_3.4_spmd.clone.clone, body=%wide.region_2.3_spmd.clone.clone.sunk | while | flops 6450409472 | bytes 21007456 | solution.py:89
  71.4 4.3 %multiply_subtract_fusion.2 = (f32[128,2048]{1,0:T(8,128)S(1)}, f32[128,2048]{1,0:T(8,128)S(1)}) fusion(f32[2048]{0:T(1024)S(1)} %get-tuple-element.234, f32[2048]{0:T(1024)S(1)} %get-tuple-element.235), kind=kLoop, calls=%fused_computation.16.clone.1 | loop fusion | flops 5242880 | bytes 2113536 | tf_op jit(solution)/shard_map/while/body/sub | solution.py:71
  75.7 5.7 %fusion.78 = f32[512,256]{0,1:T(8,128)S(1)} fusion(f32[512,2048]{1,0:T(8,128)} %get-tuple-element.257, f32[128,2048]{1,0:T(8,128)S(1)} %get-tuple-element.236, f32[128,2048]{1,0:T(8,128)S(1)} %get-tuple-element.237), kind=kOutput, calls=%fused_computation.9.clone.1 | convolution fusion | flops 3221749760 | bytes 6815744 | tf_op jit(solution)/shard_map/while/body/dot_general | solution.py:74
  81.5 6.7 %convolution_add_fusion.2 = f32[512,2048]{1,0:T(8,128)} fusion(f32[512,2048]{1,0:T(8,128)} %get-tuple-element.248, f32[128,2048]{1,0:T(8,128)S(1)} %get-tuple-element.236, f32[128,2048]{1,0:T(8,128)S(1)} %get-tuple-element.237, f32[512,128]{0,1:T(8,128)S(1)} %get-tuple-element.238, f32[512,128]{0,1:T(8,128)S(1)} %get-tuple-element.239), kind=kOutput, calls=%fused_computation.3.clone.1 | convolution fusion | flops 3222929408 | bytes 11010048 | tf_op jit(solution)/shard_map/while/body/dot_general | solution.py:85
  88.3 4.3 %multiply_subtract_fusion.2 = (f32[128,2048]{1,0:T(8,128)S(1)}, f32[128,2048]{1,0:T(8,128)S(1)}) fusion(f32[2048]{0:T(1024)S(1)} %get-tuple-element.234, f32[2048]{0:T(1024)S(1)} %get-tuple-element.235), kind=kLoop, calls=%fused_computation.16.clone.1 | loop fusion | flops 5242880 | bytes 2113536 | tf_op jit(solution)/shard_map/while/body/sub | solution.py:71
  92.5 5.7 %fusion.78 = f32[512,256]{0,1:T(8,128)S(1)} fusion(f32[512,2048]{1,0:T(8,128)} %get-tuple-element.257, f32[128,2048]{1,0:T(8,128)S(1)} %get-tuple-element.236, f32[128,2048]{1,0:T(8,128)S(1)} %get-tuple-element.237), kind=kOutput, calls=%fused_computation.9.clone.1 | convolution fusion | flops 3221749760 | bytes 6815744 | tf_op jit(solution)/shard_map/while/body/dot_general | solution.py:74
  98.4 6.7 %convolution_add_fusion.2 = f32[512,2048]{1,0:T(8,128)} fusion(f32[512,2048]{1,0:T(8,128)} %get-tuple-element.248, f32[128,2048]{1,0:T(8,128)S(1)} %get-tuple-element.236, f32[128,2048]{1,0:T(8,128)S(1)} %get-tuple-element.237, f32[512,128]{0,1:T(8,128)S(1)} %get-tuple-element.238, f32[512,128]{0,1:T(8,128)S(1)} %get-tuple-element.239), kind=kOutput, calls=%fused_computation.3.clone.1 | convolution fusion | flops 3222929408 | bytes 11010048 | tf_op jit(solution)/shard_map/while/body/dot_general | solution.py:85
  105.1 4.3 %multiply_subtract_fusion.2 = (f32[128,2048]{1,0:T(8,128)S(1)}, f32[128,2048]{1,0:T(8,128)S(1)}) fusion(f32[2048]{0:T(1024)S(1)} %get-tuple-element.234, f32[2048]{0:T(1024)S(1)} %get-tuple-element.235), kind=kLoop, calls=%fused_computation.16.clone.1 | loop fusion | flops 5242880 | bytes 2113536 | tf_op jit(solution)/shard_map/while/body/sub | solution.py:71
  109.4 5.7 %fusion.78 = f32[512,256]{0,1:T(8,128)S(1)} fusion(f32[512,2048]{1,0:T(8,128)} %get-tuple-element.257, f32[128,2048]{1,0:T(8,128)S(1)} %get-tuple-element.236, f32[128,2048]{1,0:T(8,128)S(1)} %get-tuple-element.237), kind=kOutput, calls=%fused_computation.9.clone.1 | convolution fusion | flops 3221749760 | bytes 6815744 | tf_op jit(solution)/shard_map/while/body/dot_general | solution.py:74
  115.2 6.7 %convolution_add_fusion.2 = f32[512,2048]{1,0:T(8,128)} fusion(f32[512,2048]{1,0:T(8,128)} %get-tuple-element.248, f32[128,2048]{1,0:T(8,128)S(1)} %get-tuple-element.236, f32[128,2048]{1,0:T(8,128)S(1)} %get-tuple-element.237, f32[512,128]{0,1:T(8,128)S(1)} %get-tuple-element.238, f32[512,128]{0,1:T(8,128)S(1)} %get-tuple-element.239), kind=kOutput, calls=%fused_computation.3.clone.1 | convolution fusion | flops 3222929408 | bytes 11010048 | tf_op jit(solution)/shard_map/while/body/dot_general | solution.py:85
  122.0 4.3 %multiply_subtract_fusion.2 = (f32[128,2048]{1,0:T(8,128)S(1)}, f32[128,2048]{1,0:T(8,128)S(1)}) fusion(f32[2048]{0:T(1024)S(1)} %get-tuple-element.234, f32[2048]{0:T(1024)S(1)} %get-tuple-element.235), kind=kLoop, calls=%fused_computation.16.clone.1 | loop fusion | flops 5242880 | bytes 2113536 | tf_op jit(solution)/shard_map/while/body/sub | solution.py:71
  126.3 5.7 %fusion.78 = f32[512,256]{0,1:T(8,128)S(1)} fusion(f32[512,2048]{1,0:T(8,128)} %get-tuple-element.257, f32[128,2048]{1,0:T(8,128)S(1)} %get-tuple-element.236, f32[128,2048]{1,0:T(8,128)S(1)} %get-tuple-element.237), kind=kOutput, calls=%fused_computation.9.clone.1 | convolution fusion | flops 3221749760 | bytes 6815744 | tf_op jit(solution)/shard_map/while/body/dot_general | solution.py:74
  132.1 6.7 %convolution_add_fusion.2 = f32[512,2048]{1,0:T(8,128)} fusion(f32[512,2048]{1,0:T(8,128)} %get-tuple-element.248, f32[128,2048]{1,0:T(8,128)S(1)} %get-tuple-element.236, f32[128,2048]{1,0:T(8,128)S(1)} %get-tuple-element.237, f32[512,128]{0,1:T(8,128)S(1)} %get-tuple-element.238, f32[512,128]{0,1:T(8,128)S(1)} %get-tuple-element.239), kind=kOutput, calls=%fused_computation.3.clone.1 | convolution fusion | flops 3222929408 | bytes 11010048 | tf_op jit(solution)/shard_map/while/body/dot_general | solution.py:85
  138.8 4.3 %multiply_subtract_fusion.2 = (f32[128,2048]{1,0:T(8,128)S(1)}, f32[128,2048]{1,0:T(8,128)S(1)}) fusion(f32[2048]{0:T(1024)S(1)} %get-tuple-element.234, f32[2048]{0:T(1024)S(1)} %get-tuple-element.235), kind=kLoop, calls=%fused_computation.16.clone.1 | loop fusion | flops 5242880 | bytes 2113536 | tf_op jit(solution)/shard_map/while/body/sub | solution.py:71
  143.1 5.7 %fusion.78 = f32[512,256]{0,1:T(8,128)S(1)} fusion(f32[512,2048]{1,0:T(8,128)} %get-tuple-element.257, f32[128,2048]{1,0:T(8,128)S(1)} %get-tuple-element.236, f32[128,2048]{1,0:T(8,128)S(1)} %get-tuple-element.237), kind=kOutput, calls=%fused_computation.9.clone.1 | convolution fusion | flops 3221749760 | bytes 6815744 | tf_op jit(solution)/shard_map/while/body/dot_general | solution.py:74
  148.9 6.7 %convolution_add_fusion.2 = f32[512,2048]{1,0:T(8,128)} fusion(f32[512,2048]{1,0:T(8,128)} %get-tuple-element.248, f32[128,2048]{1,0:T(8,128)S(1)} %get-tuple-element.236, f32[128,2048]{1,0:T(8,128)S(1)} %get-tuple-element.237, f32[512,128]{0,1:T(8,128)S(1)} %get-tuple-element.238, f32[512,128]{0,1:T(8,128)S(1)} %get-tuple-element.239), kind=kOutput, calls=%fused_computation.3.clone.1 | convolution fusion | flops 3222929408 | bytes 11010048 | tf_op jit(solution)/shard_map/while/body/dot_general | solution.py:85
  155.7 4.3 %multiply_subtract_fusion.2 = (f32[128,2048]{1,0:T(8,128)S(1)}, f32[128,2048]{1,0:T(8,128)S(1)}) fusion(f32[2048]{0:T(1024)S(1)} %get-tuple-element.234, f32[2048]{0:T(1024)S(1)} %get-tuple-element.235), kind=kLoop, calls=%fused_computation.16.clone.1 | loop fusion | flops 5242880 | bytes 2113536 | tf_op jit(solution)/shard_map/while/body/sub | solution.py:71
  160.0 5.7 %fusion.78 = f32[512,256]{0,1:T(8,128)S(1)} fusion(f32[512,2048]{1,0:T(8,128)} %get-tuple-element.257, f32[128,2048]{1,0:T(8,128)S(1)} %get-tuple-element.236, f32[128,2048]{1,0:T(8,128)S(1)} %get-tuple-element.237), kind=kOutput, calls=%fused_computation.9.clone.1 | convolution fusion | flops 3221749760 | bytes 6815744 | tf_op jit(solution)/shard_map/while/body/dot_general | solution.py:74
  165.8 6.7 %convolution_add_fusion.2 = f32[512,2048]{1,0:T(8,128)} fusion(f32[512,2048]{1,0:T(8,128)} %get-tuple-element.248, f32[128,2048]{1,0:T(8,128)S(1)} %get-tuple-element.236, f32[128,2048]{1,0:T(8,128)S(1)} %get-tuple-element.237, f32[512,128]{0,1:T(8,128)S(1)} %get-tuple-element.238, f32[512,128]{0,1:T(8,128)S(1)} %get-tuple-element.239), kind=kOutput, calls=%fused_computation.3.clone.1 | convolution fusion | flops 3222929408 | bytes 11010048 | tf_op jit(solution)/shard_map/while/body/dot_general | solution.py:85
  172.6 4.3 %multiply_subtract_fusion.2 = (f32[128,2048]{1,0:T(8,128)S(1)}, f32[128,2048]{1,0:T(8,128)S(1)}) fusion(f32[2048]{0:T(1024)S(1)} %get-tuple-element.234, f32[2048]{0:T(1024)S(1)} %get-tuple-element.235), kind=kLoop, calls=%fused_computation.16.clone.1 | loop fusion | flops 5242880 | bytes 2113536 | tf_op jit(solution)/shard_map/while/body/sub | solution.py:71
  176.8 5.7 %fusion.78 = f32[512,256]{0,1:T(8,128)S(1)} fusion(f32[512,2048]{1,0:T(8,128)} %get-tuple-element.257, f32[128,2048]{1,0:T(8,128)S(1)} %get-tuple-element.236, f32[128,2048]{1,0:T(8,128)S(1)} %get-tuple-element.237), kind=kOutput, calls=%fused_computation.9.clone.1 | convolution fusion | flops 3221749760 | bytes 6815744 | tf_op jit(solution)/shard_map/while/body/dot_general | solution.py:74
  182.7 6.7 %convolution_add_fusion.2 = f32[512,2048]{1,0:T(8,128)} fusion(f32[512,2048]{1,0:T(8,128)} %get-tuple-element.248, f32[128,2048]{1,0:T(8,128)S(1)} %get-tuple-element.236, f32[128,2048]{1,0:T(8,128)S(1)} %get-tuple-element.237, f32[512,128]{0,1:T(8,128)S(1)} %get-tuple-element.238, f32[512,128]{0,1:T(8,128)S(1)} %get-tuple-element.239), kind=kOutput, calls=%fused_computation.3.clone.1 | convolution fusion | flops 3222929408 | bytes 11010048 | tf_op jit(solution)/shard_map/while/body/dot_general | solution.py:85
  189.4 4.3 %multiply_subtract_fusion.2 = (f32[128,2048]{1,0:T(8,128)S(1)}, f32[128,2048]{1,0:T(8,128)S(1)}) fusion(f32[2048]{0:T(1024)S(1)} %get-tuple-element.234, f32[2048]{0:T(1024)S(1)} %get-tuple-element.235), kind=kLoop, calls=%fused_computation.16.clone.1 | loop fusion | flops 5242880 | bytes 2113536 | tf_op jit(solution)/shard_map/while/body/sub | solution.py:71
  193.7 5.7 %fusion.78 = f32[512,256]{0,1:T(8,128)S(1)} fusion(f32[512,2048]{1,0:T(8,128)} %get-tuple-element.257, f32[128,2048]{1,0:T(8,128)S(1)} %get-tuple-element.236, f32[128,2048]{1,0:T(8,128)S(1)} %get-tuple-element.237), kind=kOutput, calls=%fused_computation.9.clone.1 | convolution fusion | flops 3221749760 | bytes 6815744 | tf_op jit(solution)/shard_map/while/body/dot_general | solution.py:74
  199.5 6.7 %convolution_add_fusion.2 = f32[512,2048]{1,0:T(8,128)} fusion(f32[512,2048]{1,0:T(8,128)} %get-tuple-element.248, f32[128,2048]{1,0:T(8,128)S(1)} %get-tuple-element.236, f32[128,2048]{1,0:T(8,128)S(1)} %get-tuple-element.237, f32[512,128]{0,1:T(8,128)S(1)} %get-tuple-element.238, f32[512,128]{0,1:T(8,128)S(1)} %get-tuple-element.239), kind=kOutput, calls=%fused_computation.3.clone.1 | convolution fusion | flops 3222929408 | bytes 11010048 | tf_op jit(solution)/shard_map/while/body/dot_general | solution.py:85
  206.2 4.8 %copy.14 = f32[64,4,8,512]{3,2,0,1:T(8,128)} copy(f32[64,4,8,512]{3,2,1,0:T(8,128)} %bitcast.13) | data formatting | bytes 8388608 | tf_op jit(solution)/shard_map/all_to_all | solution.py:119
  211.0 5.0 %all-to-all-start.1 = ((f32[512,4,512]{2,0,1:T(8,128)}), f32[512,4,512]{2,0,1:T(8,128)}, u32[]{:S(2)}, u32[]{:S(2)}) async-start(f32[512,4,512]{2,0,1:T(8,128)} %bitcast.35), calls=%async_computation.1 | async-start | bytes 8388608 | tf_op jit(solution)/shard_map/all_to_all | solution.py:119
  216.0 2.8 %fusion.68 = (f32[1,32,32,512]{3,2,1,0:T(8,128)S(1)}, f32[1,32,32,512]{3,2,1,0:T(8,128)S(1)}) fusion(f32[3,32,32,512]{3,2,1,0:T(8,128)} %param.4), kind=kLoop, calls=%fused_computation.117 | loop fusion | bytes 8388608 | tf_op jit(solution)/shard_map/slice | solution.py:108
  219.1 2.1 collective-permute-start
  221.2 4.8 %collective-permute-start.1 = (f32[2,32,3,512]{3,2,1,0:T(4,128)S(1)}, f32[2,32,3,512]{3,2,1,0:T(4,128)S(1)}, u32[]{:S(2)}, u32[]{:S(2)}) collective-permute-start(f32[2,32,3,512]{3,2,1,0:T(4,128)S(1)} %get-tuple-element.191), channel_id=1, source_target_pairs={{4,0},{8,4},{12,8},{16,12},{20,16},{24,20},{28,24},{5,1},{9,5},{13... | collective-permute-start | bytes 1179656 | tf_op jit(solution)/shard_map/ppermute | solution.py:23
  226.1 2.6 bitcast_multiply_fusion.1
  228.7 15.6 %collective-permute-done = f32[2,32,3,512]{3,2,1,0:T(4,128)S(1)} collective-permute-done((f32[2,32,3,512]{3,2,1,0:T(4,128)S(1)}, f32[2,32,3,512]{3,2,1,0:T(4,128)S(1)}, u32[]{:S(2)}, u32[]{:S(2)}) %collective-permute-start) | collective-permute-done | bytes 393248 | tf_op jit(solution)/shard_map/ppermute | solution.py:22
  244.3 3.1 %collective-permute-done.1 = f32[2,32,3,512]{3,2,1,0:T(4,128)S(1)} collective-permute-done((f32[2,32,3,512]{3,2,1,0:T(4,128)S(1)}, f32[2,32,3,512]{3,2,1,0:T(4,128)S(1)}, u32[]{:S(2)}, u32[]{:S(2)}) %collective-permute-start.1) | collective-permute-done | bytes 393248 | tf_op jit(solution)/shard_map/ppermute | solution.py:23
  247.4 1.8 maximum_maximum_fusion
  249.2 4.2 %fusion.30 = f32[2,32,32,512]{3,2,1,0:T(8,128)} fusion(f32[2,32,35,512]{3,2,1,0:T(8,128)S(1)} %get-tuple-element.189, f32[2,32,35,512]{3,2,1,0:T(8,128)S(1)} %get-tuple-element.188), kind=kLoop, calls=%fused_computation.47 | loop fusion | flops 11534336 | bytes 29360128 | tf_op jit(solution)/shard_map/add | solution.py:32
  253.4 10.8 %all-to-all-done.1 = f32[512,4,512]{2,0,1:T(8,128)} async-done(((f32[512,4,512]{2,0,1:T(8,128)}), f32[512,4,512]{2,0,1:T(8,128)}, u32[]{:S(2)}, u32[]{:S(2)}) %all-to-all-start.1) | async-done | bytes 4194336 | tf_op jit(solution)/shard_map/all_to_all | solution.py:119
  264.2 2.8 %fusion.69 = (f32[2,512,512]{2,1,0:T(8,128)S(1)}, f32[2,512,512]{2,1,0:T(8,128)S(1)}) fusion(f32[4,512,512]{2,1,0:T(8,128)} %bitcast.3), kind=kLoop, calls=%fused_computation.118 | loop fusion | bytes 8388608 | tf_op jit(solution)/shard_map/slice | solution.py:124
  267.0 0.6 copy-done
  267.7 2.6 fusion.62
  270.5 4.2 %fusion.64 = (f32[1,32,32,512]{3,2,1,0:T(8,128)S(1)}, f32[1,32,32,512]{3,2,1,0:T(8,128)S(1)}) fusion(f32[32,32,512]{2,1,0:T(8,128)S(1)} %copy-done.1, f32[32,32,512]{2,1,0:T(8,128)S(1)} %bitcast.37, f32[32]{0:T(128)S(1)} %multiply_add_fusion.1, f32[32]{0:T(128)S(1)} %get-tuple-element.194, f32[2,32,32,512]{3,2,1,0:T(8,128)S(1)} %copy-done, ...), kind=kLoop, calls=%fused_computation.102 | loop fusion | flops 14155776 | bytes 12583168 | tf_op jit(solution)/shard_map/stack | solution.py:128
  274.7 3.4 %pad_maximum_fusion.5 = f32[3,32,32,512]{3,2,1,0:T(8,128)} fusion(f32[1,32,32,512]{3,2,1,0:T(8,128)S(1)} %get-tuple-element.193, f32[1,32,32,512]{3,2,1,0:T(8,128)S(1)} %get-tuple-element.192, f32[1,32,32,512]{3,2,1,0:T(8,128)S(1)} %fusion.62), kind=kLoop, calls=%fused_computation.42 | loop fusion | flops 3145728 | bytes 12582912 | tf_op jit(solution)/shard_map/stack | solution.py:128
  (42 shorter events, 2.2 us)
Async XLA Ops:
  5.0 5.0 %copy-start.3 = (s32[256]{0:T(256)S(1)}, s32[256]{0:T(256)}, u32[]{:S(2)}) copy-start(s32[256]{0:T(256)} %param.5) | copy-start | bytes 3076
  5.0 53.2 %all-to-all-start = ((f32[4,512,512]{2,1,0:T(8,128)}), f32[4,512,512]{2,1,0:T(8,128)}, u32[]{:S(2)}, u32[]{:S(2)}) async-start(f32[4,512,512]{2,1,0:T(8,128)} %bitcast.34), calls=%async_computation | async-start | bytes 8388608 | tf_op jit(solution)/shard_map/all_to_all | solution.py:112
  211.0 15.1 %slice-start = ((s8[6291456]{0:T(1024)(128)(4,1)}), s8[2097152]{0:T(1024)(128)(4,1)S(1)}, s32[]{:S(2)}) async-start(s8[6291456]{0:T(1024)(128)(4,1)} %bitcast.32), calls=%async_computation.2 | async-start | bytes 4194304
  211.0 53.2 %all-to-all-start.1 = ((f32[512,4,512]{2,0,1:T(8,128)}), f32[512,4,512]{2,0,1:T(8,128)}, u32[]{:S(2)}, u32[]{:S(2)}) async-start(f32[512,4,512]{2,0,1:T(8,128)} %bitcast.35), calls=%async_computation.1 | async-start | bytes 8388608 | tf_op jit(solution)/shard_map/all_to_all | solution.py:119
  216.0 10.1 %slice-start.1 = ((s8[6291456]{0:T(1024)(128)(4,1)}), s8[4194304]{0:T(1024)(128)(4,1)S(1)}, s32[]{:S(2)}) async-start(s8[6291456]{0:T(1024)(128)(4,1)} %bitcast.32), calls=%async_computation.3 | async-start | bytes 8388608
  219.1 25.2 %collective-permute-start = (f32[2,32,3,512]{3,2,1,0:T(4,128)S(1)}, f32[2,32,3,512]{3,2,1,0:T(4,128)S(1)}, u32[]{:S(2)}, u32[]{:S(2)}) collective-permute-start(f32[2,32,3,512]{3,2,1,0:T(4,128)S(1)} %get-tuple-element.190), channel_id=1, source_target_pairs={{0,4},{4,8},{8,12},{12,16},{16,20},{20,24},{24,28},{1,5},{5,9},{9,... | collective-permute-start | bytes 1179656 | tf_op jit(solution)/shard_map/ppermute | solution.py:22
  221.2 26.2 %collective-permute-start.1 = (f32[2,32,3,512]{3,2,1,0:T(4,128)S(1)}, f32[2,32,3,512]{3,2,1,0:T(4,128)S(1)}, u32[]{:S(2)}, u32[]{:S(2)}) collective-permute-start(f32[2,32,3,512]{3,2,1,0:T(4,128)S(1)} %get-tuple-element.191), channel_id=1, source_target_pairs={{4,0},{8,4},{12,8},{16,12},{20,16},{24,20},{28,24},{5,1},{9,5},{13... | collective-permute-start | bytes 1179656 | tf_op jit(solution)/shard_map/ppermute | solution.py:23
  264.2 3.4 %copy-start = (f32[2,32,32,512]{3,2,1,0:T(8,128)S(1)}, f32[2,32,32,512]{3,2,1,0:T(8,128)}, u32[]{:S(2)}) copy-start(f32[2,32,32,512]{3,2,1,0:T(8,128)} %fusion.30) | copy-start | bytes 12582916
  267.6 2.6 copy-start.1
  267.7 2.9 %copy-start.2 = (f32[32,32,512]{2,1,0:T(8,128)S(1)}, f32[32,32,512]{2,1,0:T(8,128)}, u32[]{:S(2)}) copy-start(f32[32,32,512]{2,1,0:T(8,128)} %get-tuple-element.183) | copy-start | bytes 6291460
where the time goes:
time: 279 us; the launch traced here: 278 us
  matrix products  99 us (35%)
  waiting for transfers between devices  76.1 us (27%)
  other arithmetic  55.7 us (20%)
  local copies, waits for them, and re-layouts  29.5 us (11%)
  starting transfers between devices  16.9 us (6%)
    dot_general x8, matrix products, block_step(): jnp.dot(scaled, table, precision=lax.Precision.HIGHEST, preferred_element...  53.6 us
    all_to_all x1, waiting for transfers between devices, on_device(): lax.all_to_all(row_data, 'azim', split_axis=0, concat_axis=1, tiled=True)  46.7 us
    dot_general x8, matrix products, block_step(): lax.dot_general(row_data, table, (((1,), (1,)), ((), ())), precision=lax....  45.4 us
    sub x8, other arithmetic, block_step(): cos_rows = base_cos * offset_cos - base_sin * offset_sin  34.2 us
    ppermute x1, waiting for transfers between devices, extended(): before = lax.ppermute(last, axis, up)  15.6 us
    all_to_all x1, waiting for transfers between devices, on_device(): lax.all_to_all(azimuthal, 'azim', split_axis=1, concat_axis=0, tiled=True)  10.8 us
    another operation x2, other arithmetic, on_device(): return jnp.stack([j_radial, j_polar, j_azim])  7.64 us
    unnamed x13, local copies, waits for them, and re-layouts  6.19 us
  transfers between devices with their start and end apart: 4, of which 4 were waited for; matrix products, arithmetic and copies ran while one was open for 5% of the time, Pallas kernels for 0%

commit v1 on v0

--- a/solution.py
+++ b/solution.py
@@ -1,8 +1,12 @@
+import functools
 import math
 
 import jax
 import jax.numpy as jnp
+import numpy as np
 from jax import lax
+from jax.experimental import pallas as pl
+from jax.experimental.pallas import tpu as pltpu
 from jax.sharding import PartitionSpec as P
 
 MB = 128
@@ -89,16 +93,19 @@
     return lax.fori_loop(0, block_count, block_step, jnp.zeros_like(row_data))
 
 
-def on_device(magnetic, kept_modes):
-    radii_count, th_dev, ph_dev = (magnetic.shape[1], magnetic.shape[2], magnetic.shape[3])
-    lat_size = lax.axis_size("lat")
-    lat_id = lax.axis_index("lat")
-    lat_total = th_dev * lat_size
+def band_geometry(th_dev):
+    lat_total = th_dev * lax.axis_size("lat")
     spacing = math.pi / lat_total
-    band_start = lat_id * th_dev
+    band_start = lax.axis_index("lat") * th_dev
     colatitude = (
         (band_start + jnp.arange(th_dev, dtype=jnp.int32)).astype(jnp.float32) + 0.5
     ) * spacing
+    return spacing, band_start, colatitude
+
+
+def on_device(magnetic, kept_modes):
+    radii_count, th_dev, ph_dev = (magnetic.shape[1], magnetic.shape[2], magnetic.shape[3])
+    spacing, band_start, colatitude = band_geometry(th_dev)
     radius = (inner_radius + (jnp.arange(radii_count, dtype=jnp.float32) + 0.5) * spacing)[
         :, None, None
     ]
@@ -128,10 +135,246 @@
     return jnp.stack([j_radial, j_polar, j_azim])
 
 
+CHUNKS = 2
+TO_Y = [(0, 2), (2, 0), (1, 3), (3, 1)]
+TO_C = [(0, 1), (1, 0), (2, 3), (3, 2)]
+TO_YC = [(0, 3), (3, 0), (1, 2), (2, 1)]
+VMEM = 60 * 1024 * 1024
+
+
+def halves(table):
+    high = table.astype(jnp.bfloat16)
+    low = (table - high.astype(np.float64)).astype(jnp.bfloat16)
+    return np.stack([high, low])
+
+
+def mode_tables(lon_total):
+    quarter = lon_total // 4
+
+    def pair(modes, length):
+        phase = (np.arange(length)[:, None] * modes[None, :] % lon_total) * (2.0 * np.pi / lon_total)
+        forward = np.concatenate([np.cos(phase), np.sin(phase)], axis=1)
+        inverse = np.concatenate([-np.sin(phase), np.cos(phase)], axis=1).T
+        return halves(forward), halves(inverse)
+
+    zero = 4 * np.arange(quarter // 2)
+    two = zero + 2
+    odd = 2 * np.arange(quarter) + 1
+    mode_ids = np.concatenate([zero, zero, two, two, odd, odd]).astype(np.float32)[None, :]
+    return pair(zero, quarter), pair(two, quarter), pair(odd, 2 * quarter), mode_ids
+
+
+def triple_dot(value, table):
+    high = value.astype(jnp.bfloat16)
+    low = (value - high.astype(jnp.float32)).astype(jnp.bfloat16)
+    dot = functools.partial(jnp.dot, preferred_element_type=jnp.float32)
+    return dot(high, table[0]) + dot(high, table[1]) + dot(low, table[0])
+
+
+def transform_kernel(
+    place, own, across, beside, diagonal, kept, modes, f0, f2, f1, i0, i2, i1, out_own, out_across, out_beside, out_diagonal
+):
+    quarter = own.shape[-1]
+    rows = own.shape[-2] * own.shape[-3]
+    sign_y = (1 - 2 * place[0]).astype(jnp.float32)
+    sign_c = (1 - 2 * place[1]).astype(jnp.float32)
+    first = place[1] == 0
+    a, b, c, d = (ref[...].reshape(rows, quarter) for ref in (own, across, beside, diagonal))
+    near, far = a + b, c + d
+    near_odd, far_odd = sign_y * (a - b), sign_y * (c - d)
+    odd = jnp.concatenate([jnp.where(first, near_odd, far_odd), jnp.where(first, far_odd, near_odd)], axis=1)
+    limit = kept[...]
+    ids = modes[...]
+    weight = jnp.where(ids < limit, ids, 0.0) * (0.5 / quarter)
+
+    def filtered(value, forward, inverse, start):
+        spectrum = triple_dot(value, forward)
+        return triple_dot(spectrum * weight[:, start : start + spectrum.shape[1]], inverse)
+
+    even0 = filtered(near + far, f0, i0, 0)
+    even2 = sign_c * filtered(sign_c * (near - far), f2, i2, quarter)
+    odd_out = sign_y * filtered(odd, f1, i1, 2 * quarter)
+    left, right = odd_out[:, :quarter], odd_out[:, quarter:]
+    odd_near, odd_far = jnp.where(first, left, right), jnp.where(first, right, left)
+    even_near, even_far = even0 + even2, even0 - even2
+    shape = out_own.shape
+    out_own[...] = (even_near + odd_near).reshape(shape)
+    out_across[...] = (even_near - odd_near).reshape(shape)
+    out_beside[...] = (even_far + odd_far).reshape(shape)
+    out_diagonal[...] = (even_far - odd_far).reshape(shape)
+
+
+def transform(place, magnetic, start, across, beside, beside_start, diagonal, kept_rows, tables):
+    depth, th_dev, quarter = across.shape
+    zero, two, odd, mode_ids = tables
+    whole = pl.BlockSpec(memory_space=pltpu.VMEM)
+    rows = depth * th_dev
+    half = magnetic.shape[1] // 2
+    grid_spec = pltpu.PrefetchScalarGridSpec(
+        num_scalar_prefetch=1,
+        grid=(1,),
+        in_specs=[
+            pl.BlockSpec((None, depth, th_dev, quarter), lambda i, p: (p[1], p[0] * (half // depth) + start // depth, 0, 0)),
+            whole,
+            pl.BlockSpec((depth, th_dev, quarter), lambda i, p: (beside_start // depth, 0, 0)),
+            whole,
+        ]
+        + [whole] * 8,
+        out_specs=[whole] * 4,
+    )
+    flops = 2 * 3 * 2 * rows * 6 * quarter * quarter
+    return pl.pallas_call(
+        transform_kernel,
+        grid_spec=grid_spec,
+        out_shape=[jax.ShapeDtypeStruct((depth, th_dev, quarter), jnp.float32)] * 4,
+        compiler_params=pltpu.CompilerParams(vmem_limit_bytes=VMEM),
+        cost_estimate=pl.CostEstimate(flops=flops, bytes_accessed=48 * quarter * quarter, transcendentals=0),
+    )(place, magnetic, across, beside, diagonal, kept_rows, mode_ids, zero[0], two[0], odd[0], zero[1], two[1], odd[1])
+
+
+def diff_along(padded, axis, length):
+    total = None
+    for offset in range(-3, 4):
+        if offset != 0:
+            term = stencil_coeffs[offset + 3] * lax.slice_in_dim(padded, 3 + offset, 3 + offset + length, axis=axis)
+            total = term if total is None else total + term
+    return total
+
+
+def local_kernel(field, before, after, radius, inv_radius, cot, out):
+    radii, th_dev, width = field.shape[1:]
+    rad, inv = radius[...], inv_radius[...]
+    edge = jnp.zeros((3, th_dev, width), jnp.float32)
+
+    def theta(value, which):
+        return diff_along(jnp.concatenate([before[which], value, after[which]], axis=1), 1, th_dev)
+
+    def radial(value):
+        return diff_along(jnp.concatenate([edge, rad * value, edge], axis=0), 0, radii)
+
+    b_azim = field[2]
+    out[0] = (theta(b_azim, 1) + cot[...] * b_azim) * inv
+    out[1] = -radial(b_azim) * inv
+    out[2] = (radial(field[1]) - theta(field[0], 0)) * inv
+
+
+def local_part(magnetic, before, after, radius, inv_radius, cot):
+    width = 128
+    radii, th_dev, ph_dev = magnetic.shape[1:]
+    fixed = lambda *shape: pl.BlockSpec(shape, lambda i: (0, 0, 0))
+    wide = lambda *lead: pl.BlockSpec(lead + (width,), lambda i: (0, 0, 0, i))
+    return pl.pallas_call(
+        local_kernel,
+        grid=(ph_dev // width,),
+        in_specs=[
+            wide(3, radii, th_dev),
+            wide(2, radii, 3),
+            wide(2, radii, 3),
+            fixed(radii, 1, 1),
+            fixed(radii, 1, 1),
+            fixed(1, th_dev, 1),
+        ],
+        out_specs=wide(3, radii, th_dev),
+        out_shape=jax.ShapeDtypeStruct(magnetic.shape, jnp.float32),
+        compiler_params=pltpu.CompilerParams(vmem_limit_bytes=VMEM),
+        cost_estimate=pl.CostEstimate(flops=60 * magnetic.size, bytes_accessed=8 * magnetic.size, transcendentals=0),
+    )(magnetic, before, after, radius, inv_radius, cot)
+
+
+def add_kernel(place, base, azim, scale, out):
+    out[...] = base[...] + azim[...] * scale[...]
+
+
+def add_azim(place, current, azim, part, start, field_of, half_of, scale):
+    depth, th_dev, ph_dev = azim.shape
+    half = current.shape[1] // 2
+    at = lambda i, p: (1 - field_of(p), half_of(p) * (half // depth) + start // depth, 0, 0)
+    block = pl.BlockSpec((None, depth, th_dev, ph_dev), at)
+    return pl.pallas_call(
+        add_kernel,
+        grid_spec=pltpu.PrefetchScalarGridSpec(
+            num_scalar_prefetch=1,
+            grid=(1,),
+            in_specs=[
+                block,
+                pl.BlockSpec((depth, th_dev, ph_dev), lambda i, p: (0, 0, 0)),
+                pl.BlockSpec((None, depth, th_dev, 1), lambda i, p: (field_of(p), half_of(p) * (half // depth) + start // depth, 0, 0)),
+            ],
+            out_specs=block,
+        ),
+        out_shape=jax.ShapeDtypeStruct(current.shape, jnp.float32),
+        input_output_aliases={1: 0},
+        compiler_params=pltpu.CompilerParams(vmem_limit_bytes=VMEM),
+        cost_estimate=pl.CostEstimate(flops=2 * azim.size, bytes_accessed=12 * azim.size, transcendentals=0),
+    )(place, current, azim, scale)
+
+
+def on_four(magnetic, kept_modes):
+    radii, th_dev, ph_dev = (magnetic.shape[1], magnetic.shape[2], magnetic.shape[3])
+    half = radii // 2
+    depth = half // CHUNKS
+    index = lax.axis_index("azim")
+    y, c = index // 2, index % 2
+    place = jnp.stack([y, c]).astype(jnp.int32)
+    send = lambda value, pairs: lax.ppermute(value, "azim", pairs)
+
+    def cut(field, start, length):
+        return lax.dynamic_slice(magnetic, (field, start, 0, 0), (1, length, th_dev, ph_dev))[0]
+
+    across, diagonal = [], []
+    for k in range(CHUNKS):
+        across.append(send(cut(c, (1 - y) * half + k * depth, depth), TO_Y))
+        diagonal.append(send(cut(1 - c, (1 - y) * half + k * depth, depth), TO_YC))
+        if k == 0:
+            beside = send(cut(1 - c, y * half, half), TO_C)
+
+    spacing, band_start, colatitude = band_geometry(th_dev)
+    radius = (inner_radius + (jnp.arange(radii, dtype=jnp.float32) + 0.5) * spacing)[:, None, None]
+    inv_radius = 1.0 / radius
+    inv_sin = (1.0 / jnp.sin(colatitude))[None, :, None]
+    cot = spacing * (jnp.cos(colatitude) / jnp.sin(colatitude))[None, :, None]
+    scale = spacing * inv_sin * inv_radius
+    scale = jnp.stack([scale, -scale])
+    band_counts = lax.dynamic_slice_in_dim(kept_modes, band_start, th_dev).astype(jnp.float32)
+    kept_rows = jnp.broadcast_to(band_counts[None, :, None], (depth, th_dev, 1)).reshape(depth * th_dev, 1)
+
+    lat_size = lax.axis_size("lat")
+    up = [(i, i + 1) for i in range(lat_size - 1)]
+    down = [(i + 1, i) for i in range(lat_size - 1)]
+    before = lax.ppermute(magnetic[0::2, :, th_dev - 3 :], "lat", up)
+    after = lax.ppermute(magnetic[0::2, :, :3], "lat", down)
+    current = local_part(magnetic, before, after, radius, inv_radius, cot)
+
+    tables = mode_tables(4 * ph_dev)
+    back = []
+    for k in range(CHUNKS):
+        mine, to_y, to_c, to_yc = transform(
+            place, magnetic, k * depth, across[k], beside, k * depth, diagonal[k], kept_rows, tables
+        )
+        back.append((mine, send(to_y, TO_Y), send(to_yc, TO_YC), send(to_c, TO_C)))
+    for k, (mine, from_y, from_yc, from_c) in enumerate(back):
+        own_field, other_field = lambda p: p[1], lambda p: 1 - p[1]
+        own_half, other_half = lambda p: p[0], lambda p: 1 - p[0]
+        for azim, field_of, half_of in (
+            (mine, own_field, own_half),
+            (from_c, other_field, own_half),
+            (from_y, own_field, other_half),
+            (from_yc, other_field, other_half),
+        ):
+            current = add_azim(place, current, azim, k, k * depth, field_of, half_of, scale)
+    return current
+
+
 def solution(mesh):
     placed = (P(None, None, "lat", "azim"), P())
+
+    def run(magnetic, kept_modes):
+        radii, ph_dev = magnetic.shape[1], magnetic.shape[3]
+        four = lax.axis_size("azim") == 4 and radii % (2 * CHUNKS) == 0 and ph_dev % 256 == 0
+        return (on_four if four else on_device)(magnetic, kept_modes)
+
     return jax.shard_map(
-        on_device,
+        run,
         mesh=mesh,
         in_specs=placed,
         out_specs=P(None, None, "lat", "azim"),

time: 279 us -> 112 us (0.40)
  the two profiles are of different devices: /device:TPU:16 before, /device:TPU:1 now
where the time goes in v1:
time: 112 us
  Pallas kernels  59.6 us (53%)
  starting transfers between devices  17.8 us (16%)
  waiting for transfers between devices  17.8 us (16%)
  local copies, waits for them, and re-layouts  14.2 us (13%)
  other arithmetic  2.2 us (2%)
    pallas_call x2, Pallas kernels, transform(): pl.pallas_call(transform_kernel, grid_spec=grid_spec, out_shape=[jax.Shap...  25.5 us
    pallas_call x8, Pallas kernels, add_azim(): pl.pallas_call(add_kernel, grid_spec=pltpu.PrefetchScalarGridSpec(num_sca...  22.3 us
    ppermute x11, waiting for transfers between devices, on_four(): send = lambda value, pairs: lax.ppermute(value, 'azim', pairs)  17.8 us
    pallas_call x1, Pallas kernels, local_part(): pl.pallas_call(local_kernel, grid=(ph_dev // width,), in_specs=[wide(3, r...  11.8 us
    ppermute x11, starting transfers between devices, on_four(): send = lambda value, pairs: lax.ppermute(value, 'azim', pairs)  11.7 us
    unnamed x22, local copies, waits for them, and re-layouts  4.98 us
    ppermute x1, starting transfers between devices, on_four(): before = lax.ppermute(magnetic[0::2, :, th_dev - 3:], 'lat', up)  4.8 us
    squeeze x2, local copies, waits for them, and re-layouts, cut(): lax.dynamic_slice(magnetic, (field, start, 0, 0), (1, length, th_dev, ph_...  4.21 us
  transfers between devices with their start and end apart: 13, of which 3 were waited for; matrix products, arithmetic and copies ran while one was open for 9% of the time, Pallas kernels for 51%

profile of v1, /device:TPU:1, one launch (start us, length us, event | category | flops | bytes accessed | tf_op | source)
XLA Modules:
  0.0 111.7 jit_solution(16775817954047441727)
XLA Ops:
  0.0 1.3 %dynamic-slice_bitcast_fusion = f32[16,32,512]{2,1,0:T(8,128)S(1)} fusion(f32[3,32,32,512]{3,2,1,0:T(8,128)} %own.3, s32[]{:T(128)S(6)} %select_n.38, s32[]{:T(128)S(6)} %select_n.39), kind=kLoop, calls=%fused_computation | loop fusion | bytes 2097160 | tf_op jit(solution)/shard_map/squeeze | solution.py:322
  1.3 0.1 collective-permute-start.3
  1.5 2.9 %dynamic-slice_bitcast_fusion.1 = (f32[8,32,512]{2,1,0:T(8,128)}, f32[8,32,512]{2,1,0:T(8,128)}, f32[8,32,512]{2,1,0:T(8,128)}, f32[8,32,512]{2,1,0:T(8,128)}) fusion(f32[3,32,32,512]{3,2,1,0:T(8,128)} %own.3, s32[]{:T(128)S(6)} %select_n.38, s32[]{:T(128)S(6)} %select_n.41, s32[]{:T(128)S(6)} %select_n.36, s32[]{:T(128)S(6)} %select_n.37), kind=kLoop, calls=%fused_computation.1 | loop fusion | bytes 4194320 | tf_op jit(solution)/shard_map/squeeze | solution.py:322
  4.3 2.6 %collective-permute-start.4 = (f32[8,32,512]{2,1,0:T(8,128)}, f32[8,32,512]{2,1,0:T(8,128)S(1)}, u32[]{:S(2)}, u32[]{:S(2)}) collective-permute-start(f32[8,32,512]{2,1,0:T(8,128)} %get-tuple-element.23), channel_id=1, source_target_pairs={{0,3},{3,0},{1,2},{2,1},{4,7},{7,4},{5,6},{6,5},{8,11},{11,8},{9,1... | collective-permute-start | bytes 1572872 | tf_op jit(solution)/shard_map/ppermute | solution.py:319
  7.0 0.1 collective-permute-start.2
  7.1 2.8 %fusion.1 = (f32[2,32,3,512]{3,2,1,0:T(4,128)}, f32[2,32,3,512]{3,2,1,0:T(4,128)}) fusion(f32[3,32,32,512]{3,2,1,0:T(8,128)} %own.3), kind=kLoop, calls=%fused_computation.15 | loop fusion | bytes 1572864 | tf_op jit(solution)/shard_map/slice | solution.py:345
  9.8 1.3 %collective-permute-start.1 = (f32[2,32,3,512]{3,2,1,0:T(4,128)}, f32[2,32,3,512]{3,2,1,0:T(4,128)}, u32[]{:S(2)}, u32[]{:S(2)}) collective-permute-start(f32[2,32,3,512]{3,2,1,0:T(4,128)} %get-tuple-element.25), channel_id=1, source_target_pairs={{4,0},{8,4},{12,8},{16,12},{20,16},{24,20},{28,24},{5,1},{9,5},{13... | collective-permute-start | bytes 1179656 | tf_op jit(solution)/shard_map/ppermute | solution.py:345
  11.1 4.8 %collective-permute-start = (f32[2,32,3,512]{3,2,1,0:T(4,128)}, f32[2,32,3,512]{3,2,1,0:T(4,128)}, u32[]{:S(2)}, u32[]{:S(2)}) collective-permute-start(f32[2,32,3,512]{3,2,1,0:T(4,128)} %get-tuple-element.26), channel_id=1, source_target_pairs={{0,4},{4,8},{8,12},{12,16},{16,20},{20,24},{24,28},{1,5},{5,9},{9,... | collective-permute-start | bytes 1179656 | tf_op jit(solution)/shard_map/ppermute | solution.py:344
  15.9 0.1 dynamic-slice_convert_fusion
  16.0 0.8 broadcast_in_dim.6.kept
  16.9 0.7 pad_add_fusion.place
  17.5 2.5 %collective-permute-done.4.diagonal = f32[8,32,512]{2,1,0:T(8,128)S(1)} collective-permute-done((f32[8,32,512]{2,1,0:T(8,128)}, f32[8,32,512]{2,1,0:T(8,128)S(1)}, u32[]{:S(2)}, u32[]{:S(2)}) %collective-permute-start.4) | collective-permute-done | bytes 524320 | tf_op jit(solution)/shard_map/ppermute | solution.py:319
  20.1 0.8 collective-permute-start.9
  20.8 9.9 %collective-permute-done.2.across = f32[8,32,512]{2,1,0:T(8,128)S(1)} collective-permute-done((f32[8,32,512]{2,1,0:T(8,128)}, f32[8,32,512]{2,1,0:T(8,128)S(1)}, u32[]{:S(2)}, u32[]{:S(2)}) %collective-permute-start.2) | collective-permute-done | bytes 524320 | tf_op jit(solution)/shard_map/ppermute | solution.py:319
  30.7 1.0 collective-permute-start.8
  31.8 0.0 collective-permute-done.3.beside
  31.8 0.0 copy-start
  31.8 1.0 copy-done
  32.7 12.8 %shard_map.92 = (f32[8,32,512]{2,1,0:T(8,128)}, f32[8,32,512]{2,1,0:T(8,128)}, f32[8,32,512]{2,1,0:T(8,128)}, f32[8,32,512]{2,1,0:T(8,128)}) custom-call(s32[2]{0:T(128)} %pad_add_fusion.place, f32[3,32,32,512]{3,2,1,0:T(8,128)} %own.3, f32[8,32,512]{2,1,0:T(8,128)} %copy-done.8, f32[16,32,512]{2,1,0:T(8,128)} %copy-done, f32[8,32,512]{2,1,0:T(8,128)} %copy-done.4, ...), custom_call_target="tpu_custom_call" | custom-call | flops 4831838208 | bytes 12582912 | tf_op jit(solution)/shard_map/pallas_call | solution.py:226
  45.5 1.9 %collective-permute-start.5 = (f32[8,32,512]{2,1,0:T(8,128)}, f32[8,32,512]{2,1,0:T(8,128)S(1)}, u32[]{:S(2)}, u32[]{:S(2)}) collective-permute-start(f32[8,32,512]{2,1,0:T(8,128)} %get-tuple-element.14), channel_id=1, source_target_pairs={{0,1},{1,0},{2,3},{3,2},{4,5},{5,4},{6,7},{7,6},{8,9},{9,8},{10,11... | collective-permute-start | bytes 1572872 | tf_op jit(solution)/shard_map/ppermute | solution.py:319
  47.4 0.0 collective-permute-done.9.diagonal
  47.4 0.6 collective-permute-start.6
  48.0 5.3 %collective-permute-done.8.across = f32[8,32,512]{2,1,0:T(8,128)} collective-permute-done((f32[8,32,512]{2,1,0:T(8,128)}, f32[8,32,512]{2,1,0:T(8,128)}, u32[]{:S(2)}, u32[]{:S(2)}) %collective-permute-start.8) | collective-permute-done | bytes 524320 | tf_op jit(solution)/shard_map/ppermute | solution.py:319
  53.3 2.5 %collective-permute-start.7 = (f32[8,32,512]{2,1,0:T(8,128)}, f32[8,32,512]{2,1,0:T(8,128)S(1)}, u32[]{:S(2)}, u32[]{:S(2)}) collective-permute-start(f32[8,32,512]{2,1,0:T(8,128)} %get-tuple-element.16), channel_id=1, source_target_pairs={{0,3},{3,0},{1,2},{2,1},{4,7},{7,4},{5,6},{6,5},{8,11},{11,8},{9,1... | collective-permute-start | bytes 1572872 | tf_op jit(solution)/shard_map/ppermute | solution.py:319
  55.8 12.8 %shard_map.97 = (f32[8,32,512]{2,1,0:T(8,128)}, f32[8,32,512]{2,1,0:T(8,128)}, f32[8,32,512]{2,1,0:T(8,128)}, f32[8,32,512]{2,1,0:T(8,128)}) custom-call(s32[2]{0:T(128)} %pad_add_fusion.place, f32[3,32,32,512]{3,2,1,0:T(8,128)} %own.3, f32[8,32,512]{2,1,0:T(8,128)} %collective-permute-done.8.across, f32[16,32,512]{2,1,0:T(8,128)} %copy-done, ...), custom_call_target="tpu_custom_call" | custom-call | flops 4831838208 | bytes 12582912 | tf_op jit(solution)/shard_map/pallas_call | solution.py:226
  68.6 0.0 collective-permute-done.1.after
  68.6 0.1 collective-permute-start.10
  68.7 0.0 collective-permute-done.before
  68.7 0.1 collective-permute-start.11
  68.8 2.0 %collective-permute-start.12 = (f32[8,32,512]{2,1,0:T(8,128)}, f32[8,32,512]{2,1,0:T(8,128)S(1)}, u32[]{:S(2)}, u32[]{:S(2)}) collective-permute-start(f32[8,32,512]{2,1,0:T(8,128)} %get-tuple-element.20), channel_id=1, source_target_pairs={{0,3},{3,0},{1,2},{2,1},{4,7},{7,4},{5,6},{6,5},{8,11},{11,8},{9,1... | collective-permute-start | bytes 1572872 | tf_op jit(solution)/shard_map/ppermute | solution.py:319
  70.8 0.1 broadcast_multiply_fusion
  70.9 1.4 %copy.33.scale = f32[2,32,32,1]{3,2,1,0:T(8,128)} copy(f32[2,32,32,1]{2,1,3,0:T(8,128)S(1)} %pad_maximum_fusion) | data formatting | bytes 16384 | tf_op jit(solution)/shard_map/stack | solution.py:337
  72.3 0.7 divide_multiply_fusion.cot
  73.0 0.6 multiply_add_fusion
  73.6 11.8 %shard_map.91.base = f32[3,32,32,512]{3,2,1,0:T(8,128)} custom-call(f32[3,32,32,512]{3,2,1,0:T(8,128)} %own.3, f32[2,32,3,512]{3,2,1,0:T(4,128)} %collective-permute-done.before, f32[2,32,3,512]{3,2,1,0:T(4,128)} %collective-permute-done.1.after, f32[32,1,1]{2,1,0:T(1,128)} %get-tuple-element.29.radius, f32[32,1,1]{2,1,0:T(1,128)} %get-tuple-element.30.inv_radius, ...), custom_call_target="tpu_custom_call" | custom-call | flops 94371840 | bytes 12582912 | tf_op jit(solution)/shard_map/pallas_call | solution.py:266
  85.4 2.8 %shard_map.93.base = f32[3,32,32,512]{3,2,1,0:T(8,128)} custom-call(s32[2]{0:T(128)} %pad_add_fusion.place, f32[3,32,32,512]{3,2,1,0:T(8,128)} %shard_map.91.base, f32[8,32,512]{2,1,0:T(8,128)} %get-tuple-element.13.azim, f32[2,32,32,1]{3,2,1,0:T(8,128)} %copy.33.scale), custom_call_target="tpu_custom_call", output_to_operand_aliasing={{}: (1, {})} | custom-call | flops 262144 | bytes 1572864 | tf_op jit(solution)/shard_map/pallas_call | solution.py:293
  88.2 2.8 %shard_map.94.base = f32[3,32,32,512]{3,2,1,0:T(8,128)} custom-call(s32[2]{0:T(128)} %pad_add_fusion.place, f32[3,32,32,512]{3,2,1,0:T(8,128)} %shard_map.93.base, f32[8,32,512]{2,1,0:T(8,128)} %copy-done.1, f32[2,32,32,1]{3,2,1,0:T(8,128)} %copy.33.scale), custom_call_target="tpu_custom_call", output_to_operand_aliasing={{}: (1, {})} | custom-call | flops 262144 | bytes 1572864 | tf_op jit(solution)/shard_map/pallas_call | solution.py:293
  91.0 0.8 copy-done.2
  91.8 2.8 %shard_map.95.base = f32[3,32,32,512]{3,2,1,0:T(8,128)} custom-call(s32[2]{0:T(128)} %pad_add_fusion.place, f32[3,32,32,512]{3,2,1,0:T(8,128)} %shard_map.94.base, f32[8,32,512]{2,1,0:T(8,128)} %copy-done.2, f32[2,32,32,1]{3,2,1,0:T(8,128)} %copy.33.scale), custom_call_target="tpu_custom_call", output_to_operand_aliasing={{}: (1, {})} | custom-call | flops 262144 | bytes 1572864 | tf_op jit(solution)/shard_map/pallas_call | solution.py:293
  94.6 0.8 copy-done.3
  95.4 2.8 %shard_map.96.base = f32[3,32,32,512]{3,2,1,0:T(8,128)} custom-call(s32[2]{0:T(128)} %pad_add_fusion.place, f32[3,32,32,512]{3,2,1,0:T(8,128)} %shard_map.95.base, f32[8,32,512]{2,1,0:T(8,128)} %copy-done.3, f32[2,32,32,1]{3,2,1,0:T(8,128)} %copy.33.scale), custom_call_target="tpu_custom_call", output_to_operand_aliasing={{}: (1, {})} | custom-call | flops 262144 | bytes 1572864 | tf_op jit(solution)/shard_map/pallas_call | solution.py:293
  98.2 2.8 %shard_map.98.base = f32[3,32,32,512]{3,2,1,0:T(8,128)} custom-call(s32[2]{0:T(128)} %pad_add_fusion.place, f32[3,32,32,512]{3,2,1,0:T(8,128)} %shard_map.96.base, f32[8,32,512]{2,1,0:T(8,128)} %get-tuple-element.17.azim, f32[2,32,32,1]{3,2,1,0:T(8,128)} %copy.33.scale), custom_call_target="tpu_custom_call", output_to_operand_aliasing={{}: (1, {})} | custom-call | flops 262144 | bytes 1572864 | tf_op jit(solution)/shard_map/pallas_call | solution.py:293
  101.0 0.8 copy-done.5
  101.8 2.8 %shard_map.99.base = f32[3,32,32,512]{3,2,1,0:T(8,128)} custom-call(s32[2]{0:T(128)} %pad_add_fusion.place, f32[3,32,32,512]{3,2,1,0:T(8,128)} %shard_map.98.base, f32[8,32,512]{2,1,0:T(8,128)} %copy-done.5, f32[2,32,32,1]{3,2,1,0:T(8,128)} %copy.33.scale), custom_call_target="tpu_custom_call", output_to_operand_aliasing={{}: (1, {})} | custom-call | flops 262144 | bytes 1572864 | tf_op jit(solution)/shard_map/pallas_call | solution.py:293
  104.6 0.8 copy-done.6
  105.4 2.8 %shard_map.100.base = f32[3,32,32,512]{3,2,1,0:T(8,128)} custom-call(s32[2]{0:T(128)} %pad_add_fusion.place, f32[3,32,32,512]{3,2,1,0:T(8,128)} %shard_map.99.base, f32[8,32,512]{2,1,0:T(8,128)} %copy-done.6, f32[2,32,32,1]{3,2,1,0:T(8,128)} %copy.33.scale), custom_call_target="tpu_custom_call", output_to_operand_aliasing={{}: (1, {})} | custom-call | flops 262144 | bytes 1572864 | tf_op jit(solution)/shard_map/pallas_call | solution.py:293
  108.2 0.8 copy-done.7
  109.0 2.8 %shard_map.101 = f32[3,32,32,512]{3,2,1,0:T(8,128)} custom-call(s32[2]{0:T(128)} %pad_add_fusion.place, f32[3,32,32,512]{3,2,1,0:T(8,128)} %shard_map.100.base, f32[8,32,512]{2,1,0:T(8,128)} %copy-done.7, f32[2,32,32,1]{3,2,1,0:T(8,128)} %copy.33.scale), custom_call_target="tpu_custom_call", output_to_operand_aliasing={{}: (1, {})} | custom-call | flops 262144 | bytes 1572864 | tf_op jit(solution)/shard_map/pallas_call | solution.py:293
  (25 shorter events, 0.1 us)
Async XLA Ops:
  0.0 15.9 %copy-start.10 = (s32[256]{0:T(256)S(1)}, s32[256]{0:T(256)}, u32[]{:S(2)}) copy-start(s32[256]{0:T(256)} %param.10) | copy-start | bytes 3076
  1.3 30.4 %collective-permute-start.3 = (f32[16,32,512]{2,1,0:T(8,128)S(1)}, f32[16,32,512]{2,1,0:T(8,128)S(1)}, u32[]{:S(2)}, u32[]{:S(2)}) collective-permute-start(f32[16,32,512]{2,1,0:T(8,128)S(1)} %dynamic-slice_bitcast_fusion), channel_id=1, source_target_pairs={{0,1},{1,0},{2,3},{3,2},{4,5},{5,4},{6,7},{7,6},{8,9},{9,8},{10,11... | collective-permute-start | bytes 3145736 | tf_op jit(solution)/shard_map/ppermute | solution.py:319
  4.3 15.7 %collective-permute-start.4 = (f32[8,32,512]{2,1,0:T(8,128)}, f32[8,32,512]{2,1,0:T(8,128)S(1)}, u32[]{:S(2)}, u32[]{:S(2)}) collective-permute-start(f32[8,32,512]{2,1,0:T(8,128)} %get-tuple-element.23), channel_id=1, source_target_pairs={{0,3},{3,0},{1,2},{2,1},{4,7},{7,4},{5,6},{6,5},{8,11},{11,8},{9,1... | collective-permute-start | bytes 1572872 | tf_op jit(solution)/shard_map/ppermute | solution.py:319
  7.0 23.8 %collective-permute-start.2 = (f32[8,32,512]{2,1,0:T(8,128)}, f32[8,32,512]{2,1,0:T(8,128)S(1)}, u32[]{:S(2)}, u32[]{:S(2)}) collective-permute-start(f32[8,32,512]{2,1,0:T(8,128)} %get-tuple-element.24), channel_id=1, source_target_pairs={{0,2},{2,0},{1,3},{3,1},{4,6},{6,4},{5,7},{7,5},{8,10},{10,8},{9,1... | collective-permute-start | bytes 1572872 | tf_op jit(solution)/shard_map/ppermute | solution.py:319
  9.8 58.7 %collective-permute-start.1 = (f32[2,32,3,512]{3,2,1,0:T(4,128)}, f32[2,32,3,512]{3,2,1,0:T(4,128)}, u32[]{:S(2)}, u32[]{:S(2)}) collective-permute-start(f32[2,32,3,512]{3,2,1,0:T(4,128)} %get-tuple-element.25), channel_id=1, source_target_pairs={{4,0},{8,4},{12,8},{16,12},{20,16},{24,20},{28,24},{5,1},{9,5},{13... | collective-permute-start | bytes 1179656 | tf_op jit(solution)/shard_map/ppermute | solution.py:345
  11.1 57.5 %collective-permute-start = (f32[2,32,3,512]{3,2,1,0:T(4,128)}, f32[2,32,3,512]{3,2,1,0:T(4,128)}, u32[]{:S(2)}, u32[]{:S(2)}) collective-permute-start(f32[2,32,3,512]{3,2,1,0:T(4,128)} %get-tuple-element.26), channel_id=1, source_target_pairs={{0,4},{4,8},{8,12},{12,16},{16,20},{20,24},{24,28},{1,5},{5,9},{9,... | collective-permute-start | bytes 1179656 | tf_op jit(solution)/shard_map/ppermute | solution.py:344
  20.0 11.7 %copy-start.4 = (f32[8,32,512]{2,1,0:T(8,128)}, f32[8,32,512]{2,1,0:T(8,128)S(1)}, u32[]{:S(2)}) copy-start(f32[8,32,512]{2,1,0:T(8,128)S(1)} %collective-permute-done.4.diagonal) | copy-start | bytes 1572868
  20.1 27.3 %collective-permute-start.9 = (f32[8,32,512]{2,1,0:T(8,128)}, f32[8,32,512]{2,1,0:T(8,128)S(1)}, u32[]{:S(2)}, u32[]{:S(2)}) collective-permute-start(f32[8,32,512]{2,1,0:T(8,128)} %get-tuple-element.21), channel_id=1, source_target_pairs={{0,3},{3,0},{1,2},{2,1},{4,7},{7,4},{5,6},{6,5},{8,11},{11,8},{9,1... | collective-permute-start | bytes 1572872 | tf_op jit(solution)/shard_map/ppermute | solution.py:319
  30.7 1.0 copy-start.8
  30.7 22.6 %collective-permute-start.8 = (f32[8,32,512]{2,1,0:T(8,128)}, f32[8,32,512]{2,1,0:T(8,128)}, u32[]{:S(2)}, u32[]{:S(2)}) collective-permute-start(f32[8,32,512]{2,1,0:T(8,128)} %get-tuple-element.22), channel_id=1, source_target_pairs={{0,2},{2,0},{1,3},{3,1},{4,6},{6,4},{5,7},{7,5},{8,10},{10,8},{9,1... | collective-permute-start | bytes 1572872 | tf_op jit(solution)/shard_map/ppermute | solution.py:319
  31.8 1.0 copy-start
  45.5 23.3 %collective-permute-start.5 = (f32[8,32,512]{2,1,0:T(8,128)}, f32[8,32,512]{2,1,0:T(8,128)S(1)}, u32[]{:S(2)}, u32[]{:S(2)}) collective-permute-start(f32[8,32,512]{2,1,0:T(8,128)} %get-tuple-element.14), channel_id=1, source_target_pairs={{0,1},{1,0},{2,3},{3,2},{4,5},{5,4},{6,7},{7,6},{8,9},{9,8},{10,11... | collective-permute-start | bytes 1572872 | tf_op jit(solution)/shard_map/ppermute | solution.py:319
  47.4 8.4 %copy-start.9 = (f32[8,32,512]{2,1,0:T(8,128)}, f32[8,32,512]{2,1,0:T(8,128)S(1)}, u32[]{:S(2)}) copy-start(f32[8,32,512]{2,1,0:T(8,128)S(1)} %collective-permute-done.9.diagonal) | copy-start | bytes 1572868
  47.4 43.6 %collective-permute-start.6 = (f32[8,32,512]{2,1,0:T(8,128)}, f32[8,32,512]{2,1,0:T(8,128)S(1)}, u32[]{:S(2)}, u32[]{:S(2)}) collective-permute-start(f32[8,32,512]{2,1,0:T(8,128)} %get-tuple-element.15), channel_id=1, source_target_pairs={{0,2},{2,0},{1,3},{3,1},{4,6},{6,4},{5,7},{7,5},{8,10},{10,8},{9,1... | collective-permute-start | bytes 1572872 | tf_op jit(solution)/shard_map/ppermute | solution.py:319
  53.3 41.3 %collective-permute-start.7 = (f32[8,32,512]{2,1,0:T(8,128)}, f32[8,32,512]{2,1,0:T(8,128)S(1)}, u32[]{:S(2)}, u32[]{:S(2)}) collective-permute-start(f32[8,32,512]{2,1,0:T(8,128)} %get-tuple-element.16), channel_id=1, source_target_pairs={{0,3},{3,0},{1,2},{2,1},{4,7},{7,4},{5,6},{6,5},{8,11},{11,8},{9,1... | collective-permute-start | bytes 1572872 | tf_op jit(solution)/shard_map/ppermute | solution.py:319
  68.6 32.4 %collective-permute-start.10 = (f32[8,32,512]{2,1,0:T(8,128)}, f32[8,32,512]{2,1,0:T(8,128)S(1)}, u32[]{:S(2)}, u32[]{:S(2)}) collective-permute-start(f32[8,32,512]{2,1,0:T(8,128)} %get-tuple-element.18), channel_id=1, source_target_pairs={{0,1},{1,0},{2,3},{3,2},{4,5},{5,4},{6,7},{7,6},{8,9},{9,8},{10,11... | collective-permute-start | bytes 1572872 | tf_op jit(solution)/shard_map/ppermute | solution.py:319
  68.7 35.9 %collective-permute-start.11 = (f32[8,32,512]{2,1,0:T(8,128)}, f32[8,32,512]{2,1,0:T(8,128)S(1)}, u32[]{:S(2)}, u32[]{:S(2)}) collective-permute-start(f32[8,32,512]{2,1,0:T(8,128)} %get-tuple-element.19), channel_id=1, source_target_pairs={{0,2},{2,0},{1,3},{3,1},{4,6},{6,4},{5,7},{7,5},{8,10},{10,8},{9,1... | collective-permute-start | bytes 1572872 | tf_op jit(solution)/shard_map/ppermute | solution.py:319
  68.8 16.6 %copy-start.1 = (f32[8,32,512]{2,1,0:T(8,128)}, f32[8,32,512]{2,1,0:T(8,128)S(1)}, u32[]{:S(2)}) copy-start(f32[8,32,512]{2,1,0:T(8,128)S(1)} %collective-permute-done.5.azim) | copy-start | bytes 1572868
  68.8 39.4 %collective-permute-start.12 = (f32[8,32,512]{2,1,0:T(8,128)}, f32[8,32,512]{2,1,0:T(8,128)S(1)}, u32[]{:S(2)}, u32[]{:S(2)}) collective-permute-start(f32[8,32,512]{2,1,0:T(8,128)} %get-tuple-element.20), channel_id=1, source_target_pairs={{0,3},{3,0},{1,2},{2,1},{4,7},{7,4},{5,6},{6,5},{8,11},{11,8},{9,1... | collective-permute-start | bytes 1572872 | tf_op jit(solution)/shard_map/ppermute | solution.py:319
  91.0 0.8 copy-start.2
  94.6 0.8 copy-start.3
  101.0 0.8 copy-start.5
  104.6 0.8 copy-start.6
  108.1 0.8 copy-start.7

commit v2 on v1

--- a/solution.py
+++ b/solution.py
@@ -172,7 +172,7 @@
 
 
 def transform_kernel(
-    place, own, across, beside, diagonal, kept, modes, f0, f2, f1, i0, i2, i1, out_own, out_across, out_beside, out_diagonal
+    place, own, across, beside, diagonal, kept, gain, modes, f0, f2, f1, i0, i2, i1, out_own, out_across, out_beside, out_diagonal
 ):
     quarter = own.shape[-1]
     rows = own.shape[-2] * own.shape[-3]
@@ -185,7 +185,7 @@
     odd = jnp.concatenate([jnp.where(first, near_odd, far_odd), jnp.where(first, far_odd, near_odd)], axis=1)
     limit = kept[...]
     ids = modes[...]
-    weight = jnp.where(ids < limit, ids, 0.0) * (0.5 / quarter)
+    weight = jnp.where(ids < limit, ids, 0.0) * gain[...]
 
     def filtered(value, forward, inverse, start):
         spectrum = triple_dot(value, forward)
@@ -204,7 +204,7 @@
     out_diagonal[...] = (even_far - odd_far).reshape(shape)
 
 
-def transform(place, magnetic, start, across, beside, beside_start, diagonal, kept_rows, tables):
+def transform(place, magnetic, start, across, beside, beside_start, diagonal, kept_rows, gain_rows, tables):
     depth, th_dev, quarter = across.shape
     zero, two, odd, mode_ids = tables
     whole = pl.BlockSpec(memory_space=pltpu.VMEM)
@@ -219,7 +219,7 @@
             pl.BlockSpec((depth, th_dev, quarter), lambda i, p: (beside_start // depth, 0, 0)),
             whole,
         ]
-        + [whole] * 8,
+        + [whole] * 9,
         out_specs=[whole] * 4,
     )
     flops = 2 * 3 * 2 * rows * 6 * quarter * quarter
@@ -229,7 +229,7 @@
         out_shape=[jax.ShapeDtypeStruct((depth, th_dev, quarter), jnp.float32)] * 4,
         compiler_params=pltpu.CompilerParams(vmem_limit_bytes=VMEM),
         cost_estimate=pl.CostEstimate(flops=flops, bytes_accessed=48 * quarter * quarter, transcendentals=0),
-    )(place, magnetic, across, beside, diagonal, kept_rows, mode_ids, zero[0], two[0], odd[0], zero[1], two[1], odd[1])
+    )(place, magnetic, across, beside, diagonal, kept_rows, gain_rows, mode_ids, zero[0], two[0], odd[0], zero[1], two[1], odd[1])
 
 
 def diff_along(padded, axis, length):
@@ -281,32 +281,54 @@
     )(magnetic, before, after, radius, inv_radius, cot)
 
 
-def add_kernel(place, base, azim, scale, out):
-    out[...] = base[...] + azim[...] * scale[...]
-
-
-def add_azim(place, current, azim, part, start, field_of, half_of, scale):
-    depth, th_dev, ph_dev = azim.shape
-    half = current.shape[1] // 2
-    at = lambda i, p: (1 - field_of(p), half_of(p) * (half // depth) + start // depth, 0, 0)
-    block = pl.BlockSpec((None, depth, th_dev, ph_dev), at)
+def add_azim(place, current, groups, step_radii):
+    depth, th_dev, ph_dev = groups[0][0].shape
+    steps = depth // step_radii
+    half_steps = current.shape[1] // 2 // step_radii
+
+    def radius_block(i, p):
+        block = 0
+        for g, (_, _, own_half, start) in enumerate(groups):
+            half = p[0] if own_half else 1 - p[0]
+            here = half * half_steps + start // step_radii + i - g * steps
+            block = jnp.where(i // steps == g, here, block)
+        return block
+
+    current_block = pl.BlockSpec((2, step_radii, th_dev, ph_dev), lambda i, p: (0, radius_block(i, p), 0, 0))
+
+    def group_block(g):
+        at = lambda i, p: (jnp.clip(i - g * steps, 0, steps - 1), 0, 0)
+        return pl.BlockSpec((step_radii, th_dev, ph_dev), at)
+
+    def kernel(place, base, *refs):
+        out = refs[-1]
+        own_part = 1 - place[1]
+        for g in range(len(groups)):
+
+            @pl.when(pl.program_id(0) // steps == g)
+            def _():
+                out[own_part] = base[own_part] + refs[2 * g][...]
+                out[1 - own_part] = base[1 - own_part] + refs[2 * g + 1][...]
+
+    azims = [azim for own, other, _, _ in groups for azim in (own, other)]
+    size = sum(azim.size for azim in azims)
     return pl.pallas_call(
-        add_kernel,
+        kernel,
         grid_spec=pltpu.PrefetchScalarGridSpec(
             num_scalar_prefetch=1,
-            grid=(1,),
-            in_specs=[
-                block,
-                pl.BlockSpec((depth, th_dev, ph_dev), lambda i, p: (0, 0, 0)),
-                pl.BlockSpec((None, depth, th_dev, 1), lambda i, p: (field_of(p), half_of(p) * (half // depth) + start // depth, 0, 0)),
-            ],
-            out_specs=block,
+            grid=(len(groups) * steps,),
+            in_specs=[current_block] + [group_block(i // 2) for i in range(len(azims))],
+            out_specs=current_block,
         ),
         out_shape=jax.ShapeDtypeStruct(current.shape, jnp.float32),
         input_output_aliases={1: 0},
         compiler_params=pltpu.CompilerParams(vmem_limit_bytes=VMEM),
-        cost_estimate=pl.CostEstimate(flops=2 * azim.size, bytes_accessed=12 * azim.size, transcendentals=0),
-    )(place, current, azim, scale)
+        cost_estimate=pl.CostEstimate(flops=2 * size, bytes_accessed=12 * size, transcendentals=0),
+    )(place, current, *azims)
+
+
+def after(first, *then):
+    return lax.optimization_barrier((first, then))[1]
 
 
 def on_four(magnetic, kept_modes):
@@ -318,51 +340,55 @@
     place = jnp.stack([y, c]).astype(jnp.int32)
     send = lambda value, pairs: lax.ppermute(value, "azim", pairs)
 
-    def cut(field, start, length):
-        return lax.dynamic_slice(magnetic, (field, start, 0, 0), (1, length, th_dev, ph_dev))[0]
+    def cut(source, field, start, length):
+        return lax.dynamic_slice(source, (field, start, 0, 0), (1, length, th_dev, ph_dev))[0]
 
     across, diagonal = [], []
+    source = magnetic
     for k in range(CHUNKS):
-        across.append(send(cut(c, (1 - y) * half + k * depth, depth), TO_Y))
-        diagonal.append(send(cut(1 - c, (1 - y) * half + k * depth, depth), TO_YC))
+        to_y = cut(source, c, (1 - y) * half + k * depth, depth)
+        (source,) = after(to_y, source)
+        to_yc = cut(source, 1 - c, (1 - y) * half + k * depth, depth)
+        (source,) = after(to_yc, source)
+        across.append(send(to_y, TO_Y))
+        diagonal.append(send(to_yc, TO_YC))
         if k == 0:
-            beside = send(cut(1 - c, y * half, half), TO_C)
+            to_c = cut(source, 1 - c, y * half, half)
+            (source,) = after(to_c, source)
+            beside = send(to_c, TO_C)
 
     spacing, band_start, colatitude = band_geometry(th_dev)
     radius = (inner_radius + (jnp.arange(radii, dtype=jnp.float32) + 0.5) * spacing)[:, None, None]
     inv_radius = 1.0 / radius
-    inv_sin = (1.0 / jnp.sin(colatitude))[None, :, None]
+    inv_sin = 1.0 / jnp.sin(colatitude)
     cot = spacing * (jnp.cos(colatitude) / jnp.sin(colatitude))[None, :, None]
-    scale = spacing * inv_sin * inv_radius
-    scale = jnp.stack([scale, -scale])
+    sign_c = (1 - 2 * c).astype(jnp.float32)
+    row_gain = (sign_c * spacing * 0.5 / ph_dev) * inv_sin[None, :] * inv_radius[:, 0]
     band_counts = lax.dynamic_slice_in_dim(kept_modes, band_start, th_dev).astype(jnp.float32)
-    kept_rows = jnp.broadcast_to(band_counts[None, :, None], (depth, th_dev, 1)).reshape(depth * th_dev, 1)
+    rows = depth * th_dev
+    kept_rows = jnp.broadcast_to(band_counts[None, :], (depth, th_dev)).reshape(rows, 1)
 
     lat_size = lax.axis_size("lat")
     up = [(i, i + 1) for i in range(lat_size - 1)]
     down = [(i + 1, i) for i in range(lat_size - 1)]
-    before = lax.ppermute(magnetic[0::2, :, th_dev - 3 :], "lat", up)
-    after = lax.ppermute(magnetic[0::2, :, :3], "lat", down)
-    current = local_part(magnetic, before, after, radius, inv_radius, cot)
+    north = lax.ppermute(source[0::2, :, th_dev - 3 :], "lat", up)
+    south = lax.ppermute(source[0::2, :, :3], "lat", down)
+    current = local_part(magnetic, north, south, radius, inv_radius, cot)
 
     tables = mode_tables(4 * ph_dev)
-    back = []
+    own_half, other_half = [], []
     for k in range(CHUNKS):
+        gain_rows = lax.dynamic_slice_in_dim(row_gain, y * half + k * depth, depth).reshape(rows, 1)
+        if k == 0:
+            (gain_rows,) = after(current, gain_rows)
         mine, to_y, to_c, to_yc = transform(
-            place, magnetic, k * depth, across[k], beside, k * depth, diagonal[k], kept_rows, tables
+            place, magnetic, k * depth, across[k], beside, k * depth, diagonal[k], kept_rows, gain_rows, tables
         )
-        back.append((mine, send(to_y, TO_Y), send(to_yc, TO_YC), send(to_c, TO_C)))
-    for k, (mine, from_y, from_yc, from_c) in enumerate(back):
-        own_field, other_field = lambda p: p[1], lambda p: 1 - p[1]
-        own_half, other_half = lambda p: p[0], lambda p: 1 - p[0]
-        for azim, field_of, half_of in (
-            (mine, own_field, own_half),
-            (from_c, other_field, own_half),
-            (from_y, own_field, other_half),
-            (from_yc, other_field, other_half),
-        ):
-            current = add_azim(place, current, azim, k, k * depth, field_of, half_of, scale)
-    return current
+        from_y, from_yc, from_c = send(to_y, TO_Y), send(to_yc, TO_YC), send(to_c, TO_C)
+        own_half.append((mine, from_c, True, k * depth))
+        other_half.append((from_y, from_yc, False, k * depth))
+    current = add_azim(place, current, own_half + other_half[:-1], 2)
+    return add_azim(place, current, other_half[-1:], 2)
 
 
 def solution(mesh):

time: 112 us -> 158 us (1.41)
  waiting for transfers between devices: 17.8 us -> 70.9 us
  Pallas kernels: 59.6 us -> 50.7 us
  local copies, waits for them, and re-layouts: 14.2 us -> 18.2 us
  starting transfers between devices: 17.8 us -> 15.5 us
    ppermute x11, waiting for transfers between devices: 17.8 us -> 64.5 us  [on_four(): send = lambda value, pairs: lax.ppermute(value, 'azim', pairs)]
    pallas_call x8 -> x2, Pallas kernels: 22.3 us -> 13.6 us  [add_azim(): pl.pallas_call(kernel, grid_spec=pltpu.PrefetchScalarGridSpec(num_scalar_...]
    ppermute x2, waiting for transfers between devices: 0.01 us -> 6.38 us  [the longest x1 6.38 us: on_four(): north = lax.ppermute(source[0::2, :, th_dev - 3:], 'lat', up)]
    squeeze x2 -> x5, local copies, waits for them, and re-layouts: 4.21 us -> 8.83 us  [cut(): lax.dynamic_slice(source, (field, start, 0, 0), (1, length, th_dev, ph_dev))]
    ppermute x11, starting transfers between devices: 11.7 us -> 9.4 us  [on_four(): send = lambda value, pairs: lax.ppermute(value, 'azim', pairs)]
    reshape x0 -> x3, local copies, waits for them, and re-layouts: none -> 1.66 us  [the longest x2 0.86 us: on_four(): lax.dynamic_slice_in_dim(row_gain, y * half + k * depth, depth)]
  transfers between devices with their start and end apart: 13 -> 13, of which waited for: 3 -> 6; matrix products, arithmetic and copies ran while one was open for 9% -> 9% of each run, Pallas kernels for 51% -> 29%
where the time goes in v2:
time: 158 us
  waiting for transfers between devices  70.9 us (45%)
  Pallas kernels  50.7 us (32%)
  local copies, waits for them, and re-layouts  18.2 us (12%)
  starting transfers between devices  15.5 us (10%)
  other arithmetic  2.19 us (1%)
    ppermute x11, waiting for transfers between devices, on_four(): send = lambda value, pairs: lax.ppermute(value, 'azim', pairs)  64.5 us
    pallas_call x2, Pallas kernels, transform(): pl.pallas_call(transform_kernel, grid_spec=grid_spec, out_shape=[jax.Shap...  25.3 us
    pallas_call x2, Pallas kernels, add_azim(): pl.pallas_call(kernel, grid_spec=pltpu.PrefetchScalarGridSpec(num_scalar_...  13.6 us
    pallas_call x1, Pallas kernels, local_part(): pl.pallas_call(local_kernel, grid=(ph_dev // width,), in_specs=[wide(3, r...  11.8 us
    ppermute x11, starting transfers between devices, on_four(): send = lambda value, pairs: lax.ppermute(value, 'azim', pairs)  9.4 us
    squeeze x5, local copies, waits for them, and re-layouts, cut(): lax.dynamic_slice(source, (field, start, 0, 0), (1, length, th_dev, ph_dev))  8.83 us
    ppermute x1, waiting for transfers between devices, on_four(): north = lax.ppermute(source[0::2, :, th_dev - 3:], 'lat', up)  6.38 us
    ppermute x1, starting transfers between devices, on_four(): north = lax.ppermute(source[0::2, :, th_dev - 3:], 'lat', up)  4.81 us
  transfers between devices with their start and end apart: 13, of which 6 were waited for; matrix products, arithmetic and copies ran while one was open for 9% of the time, Pallas kernels for 29%

profile of v2, /device:TPU:1, one launch (start us, length us, event | category | flops | bytes accessed | tf_op | source)
XLA Modules:
  0.0 157.5 jit_solution(12633675208010762963)
XLA Ops:
  0.0 1.9 %dynamic-slice_bitcast_fusion.4 = f32[8,32,512]{2,1,0:T(8,128)} fusion(f32[3,32,32,512]{3,2,1,0:T(8,128)} %own.3, s32[]{:T(128)S(6)} %select_n.40, s32[]{:T(128)S(6)} %select_n.41), kind=kLoop, calls=%fused_computation.4 | loop fusion | bytes 1048584 | tf_op jit(solution)/shard_map/squeeze | solution.py:344
  1.9 2.1 %collective-permute-start.2 = (f32[8,32,512]{2,1,0:T(8,128)}, f32[8,32,512]{2,1,0:T(8,128)S(1)}, u32[]{:S(2)}, u32[]{:S(2)}) collective-permute-start(f32[8,32,512]{2,1,0:T(8,128)} %dynamic-slice_bitcast_fusion.4), channel_id=1, source_target_pairs={{0,2},{2,0},{1,3},{3,1},{4,6},{6,4},{5,7},{7,5},{8,10},{10,8},{9,1... | collective-permute-start | bytes 1572872 | tf_op jit(solution)/shard_map/ppermute | solution.py:341
  4.0 1.9 %dynamic-slice_bitcast_fusion.3 = f32[8,32,512]{2,1,0:T(8,128)} fusion(f32[3,32,32,512]{3,2,1,0:T(8,128)} %own.3, s32[]{:T(128)S(6)} %select_n.42, s32[]{:T(128)S(6)} %select_n.41), kind=kLoop, calls=%fused_computation.3 | loop fusion | bytes 1048584 | tf_op jit(solution)/shard_map/squeeze | solution.py:344
  5.9 0.6 collective-permute-start.4
  6.4 1.3 dynamic-slice_bitcast_fusion
  7.7 0.5 collective-permute-start.3
  8.2 1.9 %dynamic-slice_bitcast_fusion.2 = f32[8,32,512]{2,1,0:T(8,128)} fusion(f32[3,32,32,512]{3,2,1,0:T(8,128)} %own.3, s32[]{:T(128)S(6)} %select_n.40, s32[]{:T(128)S(6)} %select_n.44), kind=kLoop, calls=%fused_computation.2 | loop fusion | bytes 1048584 | tf_op jit(solution)/shard_map/squeeze | solution.py:344
  10.1 1.4 collective-permute-start.6
  11.5 1.9 %dynamic-slice_bitcast_fusion.1 = f32[8,32,512]{2,1,0:T(8,128)} fusion(f32[3,32,32,512]{3,2,1,0:T(8,128)} %own.3, s32[]{:T(128)S(6)} %select_n.42, s32[]{:T(128)S(6)} %select_n.44), kind=kLoop, calls=%fused_computation.1 | loop fusion | bytes 1048584 | tf_op jit(solution)/shard_map/squeeze | solution.py:344
  13.3 0.4 collective-permute-start.7
  13.8 0.1 broadcast_multiply_fusion
  13.9 0.1 dynamic-slice_convert_fusion
  13.9 0.1 reshape.76
  14.0 0.8 reshape.78.kept
  14.8 0.8 reshape.79.gain
  15.6 0.7 pad_add_fusion.place
  16.3 0.6 multiply_add_fusion
  16.9 2.6 %fusion = (f32[2,32,3,512]{3,2,1,0:T(4,128)}, f32[2,32,3,512]{3,2,1,0:T(4,128)S(1)}) fusion(f32[3,32,32,512]{3,2,1,0:T(8,128)} %own.3), kind=kLoop, calls=%fused_computation.15 | loop fusion | bytes 1572864 | tf_op jit(solution)/shard_map/slice | solution.py:375
  19.5 30.7 %collective-permute-done.7.diagonal = f32[8,32,512]{2,1,0:T(8,128)} collective-permute-done((f32[8,32,512]{2,1,0:T(8,128)}, f32[8,32,512]{2,1,0:T(8,128)}, u32[]{:S(2)}, u32[]{:S(2)}) %collective-permute-start.7) | collective-permute-done | bytes 524320 | tf_op jit(solution)/shard_map/ppermute | solution.py:341
  50.2 1.3 collective-permute-start.1
  51.5 0.0 collective-permute-done.6.across
  51.5 4.8 %collective-permute-start = (f32[2,32,3,512]{3,2,1,0:T(4,128)S(1)}, f32[2,32,3,512]{3,2,1,0:T(4,128)}, u32[]{:S(2)}, u32[]{:S(2)}) collective-permute-start(f32[2,32,3,512]{3,2,1,0:T(4,128)S(1)} %get-tuple-element.34), channel_id=1, source_target_pairs={{0,4},{4,8},{8,12},{12,16},{16,20},{20,24},{24,28},{1,5},{5,9},{9,... | collective-permute-start | bytes 1179656 | tf_op jit(solution)/shard_map/ppermute | solution.py:374
  56.3 0.0 collective-permute-done.3.beside
  56.3 1.0 copy-done
  57.3 12.6 %shard_map.93 = (f32[8,32,512]{2,1,0:T(8,128)}, f32[8,32,512]{2,1,0:T(8,128)}, f32[8,32,512]{2,1,0:T(8,128)}, f32[8,32,512]{2,1,0:T(8,128)}) custom-call(s32[2]{0:T(128)} %pad_add_fusion.place, f32[3,32,32,512]{3,2,1,0:T(8,128)} %own.3, f32[8,32,512]{2,1,0:T(8,128)} %collective-permute-done.6.across, f32[16,32,512]{2,1,0:T(8,128)} %copy-done, ...), custom_call_target="tpu_custom_call" | custom-call | flops 4831838208 | bytes 12582912 | tf_op jit(solution)/shard_map/pallas_call | solution.py:226
  69.9 0.5 collective-permute-start.8
  70.4 0.7 divide_multiply_fusion.cot
  71.1 0.0 collective-permute-done.1.after
  71.1 6.4 %collective-permute-done.before = f32[2,32,3,512]{3,2,1,0:T(4,128)} collective-permute-done((f32[2,32,3,512]{3,2,1,0:T(4,128)S(1)}, f32[2,32,3,512]{3,2,1,0:T(4,128)}, u32[]{:S(2)}, u32[]{:S(2)}) %collective-permute-start) | collective-permute-done | bytes 393248 | tf_op jit(solution)/shard_map/ppermute | solution.py:374
  77.5 11.8 %shard_map.91.base = f32[3,32,32,512]{3,2,1,0:T(8,128)} custom-call(f32[3,32,32,512]{3,2,1,0:T(8,128)} %own.3, f32[2,32,3,512]{3,2,1,0:T(4,128)} %collective-permute-done.before, f32[2,32,3,512]{3,2,1,0:T(4,128)} %collective-permute-done.1.after, f32[32,1,1]{2,1,0:T(1,128)} %get-tuple-element.37.radius, f32[32,1,1]{2,1,0:T(1,128)} %get-tuple-element.38.inv_radius, ...), custom_call_target="tpu_custom_call" | custom-call | flops 94371840 | bytes 12582912 | tf_op jit(solution)/shard_map/pallas_call | solution.py:266
  89.3 0.8 copy.19.gain
  90.1 0.0 collective-permute-done.4.diagonal
  90.1 0.8 copy-done.2
  90.9 0.8 copy-done.1
  91.7 12.7 %shard_map.92 = (f32[8,32,512]{2,1,0:T(8,128)}, f32[8,32,512]{2,1,0:T(8,128)}, f32[8,32,512]{2,1,0:T(8,128)}, f32[8,32,512]{2,1,0:T(8,128)}) custom-call(s32[2]{0:T(128)} %pad_add_fusion.place, f32[3,32,32,512]{3,2,1,0:T(8,128)} %own.3, f32[8,32,512]{2,1,0:T(8,128)} %copy-done.1, f32[16,32,512]{2,1,0:T(8,128)} %copy-done, f32[8,32,512]{2,1,0:T(8,128)} %copy-done.2, ...), custom_call_target="tpu_custom_call" | custom-call | flops 4831838208 | bytes 12582912 | tf_op jit(solution)/shard_map/pallas_call | solution.py:226
  104.4 0.5 collective-permute-start.5
  104.9 1.2 collective-permute-start.9
  106.1 0.4 collective-permute-start.10
  106.6 1.3 collective-permute-start.11
  107.8 0.6 collective-permute-start.12
  108.4 10.1 %collective-permute-done.9.refs_4_ = f32[8,32,512]{2,1,0:T(8,128)S(1)} collective-permute-done((f32[8,32,512]{2,1,0:T(8,128)}, f32[8,32,512]{2,1,0:T(8,128)S(1)}, u32[]{:S(2)}, u32[]{:S(2)}) %collective-permute-start.9) | collective-permute-done | bytes 524320 | tf_op jit(solution)/shard_map/ppermute | solution.py:341
  118.6 11.8 %collective-permute-done.10.refs_5_ = f32[8,32,512]{2,1,0:T(8,128)S(1)} collective-permute-done((f32[8,32,512]{2,1,0:T(8,128)}, f32[8,32,512]{2,1,0:T(8,128)S(1)}, u32[]{:S(2)}, u32[]{:S(2)}) %collective-permute-start.10) | collective-permute-done | bytes 524320 | tf_op jit(solution)/shard_map/ppermute | solution.py:341
  130.4 0.8 copy-done.6
  131.2 9.4 %shard_map.94.base = f32[3,32,32,512]{3,2,1,0:T(8,128)} custom-call(s32[2]{0:T(128)} %pad_add_fusion.place, f32[3,32,32,512]{3,2,1,0:T(8,128)} %shard_map.91.base, f32[8,32,512]{2,1,0:T(8,128)} %get-tuple-element.25.refs_0_, f32[8,32,512]{2,1,0:T(8,128)} %copy-done.4, f32[8,32,512]{2,1,0:T(8,128)} %get-tuple-element.27.refs_2_, ...), custom_call_target="tpu_custom_call", output_to_operand_aliasing={{}: (1, {})} | custom-call | flops 1572864 | bytes 9437184 | tf_op jit(solution)/shard_map/pallas_call | solution.py:315
  140.6 0.4 collective-permute-done.11.refs_0_
  141.0 11.4 %collective-permute-done.12.refs_1_ = f32[8,32,512]{2,1,0:T(8,128)S(1)} collective-permute-done((f32[8,32,512]{2,1,0:T(8,128)S(1)}, f32[8,32,512]{2,1,0:T(8,128)S(1)}, u32[]{:S(2)}, u32[]{:S(2)}) %collective-permute-start.12) | collective-permute-done | bytes 524320 | tf_op jit(solution)/shard_map/ppermute | solution.py:341
  152.4 0.8 copy-done.8
  153.3 4.3 %shard_map.95 = f32[3,32,32,512]{3,2,1,0:T(8,128)} custom-call(s32[2]{0:T(128)} %pad_add_fusion.place, f32[3,32,32,512]{3,2,1,0:T(8,128)} %shard_map.94.base, f32[8,32,512]{2,1,0:T(8,128)} %copy-done.7, f32[8,32,512]{2,1,0:T(8,128)} %copy-done.8), custom_call_target="tpu_custom_call", output_to_operand_aliasing={{}: (1, {})} | custom-call | flops 524288 | bytes 3145728 | tf_op jit(solution)/shard_map/pallas_call | solution.py:315
  (24 shorter events, 0.1 us)
Async XLA Ops:
  0.0 13.9 %copy-start.10 = (s32[256]{0:T(256)S(1)}, s32[256]{0:T(256)}, u32[]{:S(2)}) copy-start(s32[256]{0:T(256)} %param.10) | copy-start | bytes 3076
  1.9 88.2 %collective-permute-start.2 = (f32[8,32,512]{2,1,0:T(8,128)}, f32[8,32,512]{2,1,0:T(8,128)S(1)}, u32[]{:S(2)}, u32[]{:S(2)}) collective-permute-start(f32[8,32,512]{2,1,0:T(8,128)} %dynamic-slice_bitcast_fusion.4), channel_id=1, source_target_pairs={{0,2},{2,0},{1,3},{3,1},{4,6},{6,4},{5,7},{7,5},{8,10},{10,8},{9,1... | collective-permute-start | bytes 1572872 | tf_op jit(solution)/shard_map/ppermute | solution.py:341
  5.9 84.2 %collective-permute-start.4 = (f32[8,32,512]{2,1,0:T(8,128)}, f32[8,32,512]{2,1,0:T(8,128)S(1)}, u32[]{:S(2)}, u32[]{:S(2)}) collective-permute-start(f32[8,32,512]{2,1,0:T(8,128)} %dynamic-slice_bitcast_fusion.3), channel_id=1, source_target_pairs={{0,3},{3,0},{1,2},{2,1},{4,7},{7,4},{5,6},{6,5},{8,11},{11,8},{9,1... | collective-permute-start | bytes 1572872 | tf_op jit(solution)/shard_map/ppermute | solution.py:341
  7.7 48.6 %collective-permute-start.3 = (f32[16,32,512]{2,1,0:T(8,128)S(1)}, f32[16,32,512]{2,1,0:T(8,128)S(1)}, u32[]{:S(2)}, u32[]{:S(2)}) collective-permute-start(f32[16,32,512]{2,1,0:T(8,128)S(1)} %dynamic-slice_bitcast_fusion), channel_id=1, source_target_pairs={{0,1},{1,0},{2,3},{3,2},{4,5},{5,4},{6,7},{7,6},{8,9},{9,8},{10,11... | collective-permute-start | bytes 3145736 | tf_op jit(solution)/shard_map/ppermute | solution.py:341
  10.1 41.4 %collective-permute-start.6 = (f32[8,32,512]{2,1,0:T(8,128)}, f32[8,32,512]{2,1,0:T(8,128)}, u32[]{:S(2)}, u32[]{:S(2)}) collective-permute-start(f32[8,32,512]{2,1,0:T(8,128)} %dynamic-slice_bitcast_fusion.2), channel_id=1, source_target_pairs={{0,2},{2,0},{1,3},{3,1},{4,6},{6,4},{5,7},{7,5},{8,10},{10,8},{9,1... | collective-permute-start | bytes 1572872 | tf_op jit(solution)/shard_map/ppermute | solution.py:341
  13.3 36.9 %collective-permute-start.7 = (f32[8,32,512]{2,1,0:T(8,128)}, f32[8,32,512]{2,1,0:T(8,128)}, u32[]{:S(2)}, u32[]{:S(2)}) collective-permute-start(f32[8,32,512]{2,1,0:T(8,128)} %dynamic-slice_bitcast_fusion.1), channel_id=1, source_target_pairs={{0,3},{3,0},{1,2},{2,1},{4,7},{7,4},{5,6},{6,5},{8,11},{11,8},{9,1... | collective-permute-start | bytes 1572872 | tf_op jit(solution)/shard_map/ppermute | solution.py:341
  50.2 21.0 %collective-permute-start.1 = (f32[2,32,3,512]{3,2,1,0:T(4,128)}, f32[2,32,3,512]{3,2,1,0:T(4,128)}, u32[]{:S(2)}, u32[]{:S(2)}) collective-permute-start(f32[2,32,3,512]{3,2,1,0:T(4,128)} %get-tuple-element.33), channel_id=1, source_target_pairs={{4,0},{8,4},{12,8},{16,12},{20,16},{24,20},{28,24},{5,1},{9,5},{13... | collective-permute-start | bytes 1179656 | tf_op jit(solution)/shard_map/ppermute | solution.py:375
  51.5 26.0 %collective-permute-start = (f32[2,32,3,512]{3,2,1,0:T(4,128)S(1)}, f32[2,32,3,512]{3,2,1,0:T(4,128)}, u32[]{:S(2)}, u32[]{:S(2)}) collective-permute-start(f32[2,32,3,512]{3,2,1,0:T(4,128)S(1)} %get-tuple-element.34), channel_id=1, source_target_pairs={{0,4},{4,8},{8,12},{12,16},{16,20},{20,24},{24,28},{1,5},{5,9},{9,... | collective-permute-start | bytes 1179656 | tf_op jit(solution)/shard_map/ppermute | solution.py:374
  56.3 1.0 copy-start
  69.9 37.9 %collective-permute-start.8 = (f32[8,32,512]{2,1,0:T(8,128)}, f32[8,32,512]{2,1,0:T(8,128)S(1)}, u32[]{:S(2)}, u32[]{:S(2)}) collective-permute-start(f32[8,32,512]{2,1,0:T(8,128)} %get-tuple-element.28), channel_id=1, source_target_pairs={{0,1},{1,0},{2,3},{3,2},{4,5},{5,4},{6,7},{7,6},{8,9},{9,8},{10,11... | collective-permute-start | bytes 1572872 | tf_op jit(solution)/shard_map/ppermute | solution.py:341
  90.1 17.8 %copy-start.9 = (f32[8,32,512]{2,1,0:T(8,128)S(1)}, f32[8,32,512]{2,1,0:T(8,128)}, u32[]{:S(2)}) copy-start(f32[8,32,512]{2,1,0:T(8,128)} %get-tuple-element.32) | copy-start | bytes 1572868
  90.1 0.8 copy-start.2
  90.9 0.8 copy-start.1
  104.4 4.0 %collective-permute-start.5 = (f32[8,32,512]{2,1,0:T(8,128)}, f32[8,32,512]{2,1,0:T(8,128)S(1)}, u32[]{:S(2)}, u32[]{:S(2)}) collective-permute-start(f32[8,32,512]{2,1,0:T(8,128)} %get-tuple-element.26), channel_id=1, source_target_pairs={{0,1},{1,0},{2,3},{3,2},{4,5},{5,4},{6,7},{7,6},{8,9},{9,8},{10,11... | collective-permute-start | bytes 1572872 | tf_op jit(solution)/shard_map/ppermute | solution.py:341
  104.9 13.7 %collective-permute-start.9 = (f32[8,32,512]{2,1,0:T(8,128)}, f32[8,32,512]{2,1,0:T(8,128)S(1)}, u32[]{:S(2)}, u32[]{:S(2)}) collective-permute-start(f32[8,32,512]{2,1,0:T(8,128)} %get-tuple-element.29), channel_id=1, source_target_pairs={{0,2},{2,0},{1,3},{3,1},{4,6},{6,4},{5,7},{7,5},{8,10},{10,8},{9,1... | collective-permute-start | bytes 1572872 | tf_op jit(solution)/shard_map/ppermute | solution.py:341
  106.1 24.3 %collective-permute-start.10 = (f32[8,32,512]{2,1,0:T(8,128)}, f32[8,32,512]{2,1,0:T(8,128)S(1)}, u32[]{:S(2)}, u32[]{:S(2)}) collective-permute-start(f32[8,32,512]{2,1,0:T(8,128)} %get-tuple-element.30), channel_id=1, source_target_pairs={{0,3},{3,0},{1,2},{2,1},{4,7},{7,4},{5,6},{6,5},{8,11},{11,8},{9,1... | collective-permute-start | bytes 1572872 | tf_op jit(solution)/shard_map/ppermute | solution.py:341
  106.6 34.5 %collective-permute-start.11 = (f32[8,32,512]{2,1,0:T(8,128)}, f32[8,32,512]{2,1,0:T(8,128)S(1)}, u32[]{:S(2)}, u32[]{:S(2)}) collective-permute-start(f32[8,32,512]{2,1,0:T(8,128)} %get-tuple-element.31), channel_id=1, source_target_pairs={{0,2},{2,0},{1,3},{3,1},{4,6},{6,4},{5,7},{7,5},{8,10},{10,8},{9,1... | collective-permute-start | bytes 1572872 | tf_op jit(solution)/shard_map/ppermute | solution.py:341
  107.8 22.6 %copy-start.3 = (f32[8,32,512]{2,1,0:T(8,128)}, f32[8,32,512]{2,1,0:T(8,128)S(1)}, u32[]{:S(2)}) copy-start(f32[8,32,512]{2,1,0:T(8,128)S(1)} %collective-permute-done.8.refs_3_) | copy-start | bytes 1572868
  107.8 44.6 %collective-permute-start.12 = (f32[8,32,512]{2,1,0:T(8,128)S(1)}, f32[8,32,512]{2,1,0:T(8,128)S(1)}, u32[]{:S(2)}, u32[]{:S(2)}) collective-permute-start(f32[8,32,512]{2,1,0:T(8,128)S(1)} %copy-done.9), channel_id=1, source_target_pairs={{0,3},{3,0},{1,2},{2,1},{4,7},{7,4},{5,6},{6,5},{8,11},{11,8},{9,1... | collective-permute-start | bytes 1572872 | tf_op jit(solution)/shard_map/ppermute | solution.py:341
  108.4 22.0 %copy-start.4 = (f32[8,32,512]{2,1,0:T(8,128)}, f32[8,32,512]{2,1,0:T(8,128)S(1)}, u32[]{:S(2)}) copy-start(f32[8,32,512]{2,1,0:T(8,128)S(1)} %collective-permute-done.5.refs_1_) | copy-start | bytes 1572868
  118.6 11.9 %copy-start.5 = (f32[8,32,512]{2,1,0:T(8,128)}, f32[8,32,512]{2,1,0:T(8,128)S(1)}, u32[]{:S(2)}) copy-start(f32[8,32,512]{2,1,0:T(8,128)S(1)} %collective-permute-done.9.refs_4_) | copy-start | bytes 1572868
  130.4 0.8 copy-start.6
  141.0 11.4 %copy-start.7 = (f32[8,32,512]{2,1,0:T(8,128)}, f32[8,32,512]{2,1,0:T(8,128)S(1)}, u32[]{:S(2)}) copy-start(f32[8,32,512]{2,1,0:T(8,128)S(1)} %collective-permute-done.11.refs_0_) | copy-start | bytes 1572868
  152.4 0.8 copy-start.8

commit v3 on v2

--- a/solution.py
+++ b/solution.py
@@ -135,11 +135,12 @@
     return jnp.stack([j_radial, j_polar, j_azim])
 
 
-CHUNKS = 2
+CHUNKS = (8, 8)
 TO_Y = [(0, 2), (2, 0), (1, 3), (3, 1)]
 TO_C = [(0, 1), (1, 0), (2, 3), (3, 2)]
 TO_YC = [(0, 3), (3, 0), (1, 2), (2, 1)]
 VMEM = 60 * 1024 * 1024
+SHORT = pl.CostEstimate(flops=1, bytes_accessed=1, transcendentals=0)
 
 
 def halves(table):
@@ -171,11 +172,13 @@
     return dot(high, table[0]) + dot(high, table[1]) + dot(low, table[0])
 
 
-def transform_kernel(
-    place, own, across, beside, diagonal, kept, gain, modes, f0, f2, f1, i0, i2, i1, out_own, out_across, out_beside, out_diagonal
-):
+def transform_kernel(place, own, across, beside, diagonal, kept, gain, modes, *refs):
+    tables, out_own, out_beside, outs, held, sems = refs[:6], refs[6], refs[7], refs[8:-7], refs[-7:-1], refs[-1]
+    copies = [pltpu.make_async_copy(table, ref, sems.at[i]) for i, (table, ref) in enumerate(zip(tables, held))]
+    for copy in copies:
+        copy.start()
     quarter = own.shape[-1]
-    rows = own.shape[-2] * own.shape[-3]
+    rows = diagonal.shape[0] * diagonal.shape[1]
     sign_y = (1 - 2 * place[0]).astype(jnp.float32)
     sign_c = (1 - 2 * place[1]).astype(jnp.float32)
     first = place[1] == 0
@@ -187,49 +190,62 @@
     ids = modes[...]
     weight = jnp.where(ids < limit, ids, 0.0) * gain[...]
 
-    def filtered(value, forward, inverse, start):
-        spectrum = triple_dot(value, forward)
-        return triple_dot(spectrum * weight[:, start : start + spectrum.shape[1]], inverse)
-
-    even0 = filtered(near + far, f0, i0, 0)
-    even2 = sign_c * filtered(sign_c * (near - far), f2, i2, quarter)
-    odd_out = sign_y * filtered(odd, f1, i1, 2 * quarter)
+    def filtered(value, which, start):
+        copies[2 * which].wait()
+        spectrum = triple_dot(value, held[2 * which])
+        copies[2 * which + 1].wait()
+        return triple_dot(spectrum * weight[:, start : start + spectrum.shape[1]], held[2 * which + 1])
+
+    even0 = filtered(near + far, 0, 0)
+    even2 = sign_c * filtered(sign_c * (near - far), 1, quarter)
+    odd_out = sign_y * filtered(odd, 2, 2 * quarter)
     left, right = odd_out[:, :quarter], odd_out[:, quarter:]
     odd_near, odd_far = jnp.where(first, left, right), jnp.where(first, right, left)
     even_near, even_far = even0 + even2, even0 - even2
     shape = out_own.shape
     out_own[...] = (even_near + odd_near).reshape(shape)
-    out_across[...] = (even_near - odd_near).reshape(shape)
     out_beside[...] = (even_far + odd_far).reshape(shape)
-    out_diagonal[...] = (even_far - odd_far).reshape(shape)
-
-
-def transform(place, magnetic, start, across, beside, beside_start, diagonal, kept_rows, gain_rows, tables):
-    depth, th_dev, quarter = across.shape
+    across, diagonal = (even_near - odd_near).reshape(shape), (even_far - odd_far).reshape(shape)
+    if len(outs) == 1:
+        outs[0][0], outs[0][1] = across, diagonal
+    else:
+        outs[0][...], outs[1][...] = across, diagonal
+
+
+def transform(place, magnetic, start, both, beside, diagonal, row_kept, row_gain, tables, paired):
+    depth, th_dev, quarter = diagonal.shape
     zero, two, odd, mode_ids = tables
     whole = pl.BlockSpec(memory_space=pltpu.VMEM)
     rows = depth * th_dev
     half = magnetic.shape[1] // 2
+    part = (pl.Element(1), pl.Element(depth), pl.Element(th_dev), pl.Element(quarter))
+    row_block = pl.BlockSpec((pl.Element(rows), pl.Element(1)), lambda i, p: (start * th_dev, 0))
     grid_spec = pltpu.PrefetchScalarGridSpec(
         num_scalar_prefetch=1,
         grid=(1,),
         in_specs=[
-            pl.BlockSpec((None, depth, th_dev, quarter), lambda i, p: (p[1], p[0] * (half // depth) + start // depth, 0, 0)),
+            pl.BlockSpec(part, lambda i, p: (p[1], p[0] * half + start, 0, 0)),
+            pl.BlockSpec((None, depth, th_dev, quarter), lambda i, p: (p[1], 0, 0, 0)),
+            pl.BlockSpec(part[1:], lambda i, p: (start, 0, 0)),
             whole,
-            pl.BlockSpec((depth, th_dev, quarter), lambda i, p: (beside_start // depth, 0, 0)),
+            row_block,
+            row_block,
             whole,
         ]
-        + [whole] * 9,
-        out_specs=[whole] * 4,
+        + [pl.BlockSpec(memory_space=pl.ANY)] * 6,
+        out_specs=[whole] * (3 if paired else 4),
+        scratch_shapes=[pltpu.VMEM(t.shape, jnp.bfloat16) for t in (*zero, *two, *odd)] + [pltpu.SemaphoreType.DMA((6,))],
     )
-    flops = 2 * 3 * 2 * rows * 6 * quarter * quarter
-    return pl.pallas_call(
+    shape = (depth, th_dev, quarter)
+    shapes = [shape, shape, (2,) + shape] if paired else [shape] * 4
+    outs = pl.pallas_call(
         transform_kernel,
         grid_spec=grid_spec,
-        out_shape=[jax.ShapeDtypeStruct((depth, th_dev, quarter), jnp.float32)] * 4,
+        out_shape=[jax.ShapeDtypeStruct(shape, jnp.float32) for shape in shapes],
         compiler_params=pltpu.CompilerParams(vmem_limit_bytes=VMEM),
-        cost_estimate=pl.CostEstimate(flops=flops, bytes_accessed=48 * quarter * quarter, transcendentals=0),
-    )(place, magnetic, across, beside, diagonal, kept_rows, gain_rows, mode_ids, zero[0], two[0], odd[0], zero[1], two[1], odd[1])
+        cost_estimate=SHORT,
+    )(place, magnetic, both, beside, diagonal, row_kept, row_gain, mode_ids, *zero, *two, *odd)
+    return (*outs, None) if paired else outs
 
 
 def diff_along(padded, axis, length):
@@ -241,90 +257,80 @@
     return total
 
 
-def local_kernel(field, before, after, radius, inv_radius, cot, out):
-    radii, th_dev, width = field.shape[1:]
-    rad, inv = radius[...], inv_radius[...]
-    edge = jnp.zeros((3, th_dev, width), jnp.float32)
-
-    def theta(value, which):
-        return diff_along(jnp.concatenate([before[which], value, after[which]], axis=1), 1, th_dev)
-
-    def radial(value):
-        return diff_along(jnp.concatenate([edge, rad * value, edge], axis=0), 0, radii)
-
-    b_azim = field[2]
-    out[0] = (theta(b_azim, 1) + cot[...] * b_azim) * inv
-    out[1] = -radial(b_azim) * inv
-    out[2] = (radial(field[1]) - theta(field[0], 0)) * inv
-
-
-def local_part(magnetic, before, after, radius, inv_radius, cot):
+def local_part(place, magnetic, before, after, radius, inv_radius, cot, groups):
     width = 128
     radii, th_dev, ph_dev = magnetic.shape[1:]
-    fixed = lambda *shape: pl.BlockSpec(shape, lambda i: (0, 0, 0))
-    wide = lambda *lead: pl.BlockSpec(lead + (width,), lambda i: (0, 0, 0, i))
-    return pl.pallas_call(
-        local_kernel,
-        grid=(ph_dev // width,),
-        in_specs=[
-            wide(3, radii, th_dev),
-            wide(2, radii, 3),
-            wide(2, radii, 3),
-            fixed(radii, 1, 1),
-            fixed(radii, 1, 1),
-            fixed(1, th_dev, 1),
-        ],
-        out_specs=wide(3, radii, th_dev),
-        out_shape=jax.ShapeDtypeStruct(magnetic.shape, jnp.float32),
-        compiler_params=pltpu.CompilerParams(vmem_limit_bytes=VMEM),
-        cost_estimate=pl.CostEstimate(flops=60 * magnetic.size, bytes_accessed=8 * magnetic.size, transcendentals=0),
-    )(magnetic, before, after, radius, inv_radius, cot)
-
-
-def add_azim(place, current, groups, step_radii):
-    depth, th_dev, ph_dev = groups[0][0].shape
-    steps = depth // step_radii
-    half_steps = current.shape[1] // 2 // step_radii
-
-    def radius_block(i, p):
-        block = 0
-        for g, (_, _, own_half, start) in enumerate(groups):
-            half = p[0] if own_half else 1 - p[0]
-            here = half * half_steps + start // step_radii + i - g * steps
-            block = jnp.where(i // steps == g, here, block)
-        return block
-
-    current_block = pl.BlockSpec((2, step_radii, th_dev, ph_dev), lambda i, p: (0, radius_block(i, p), 0, 0))
-
-    def group_block(g):
-        at = lambda i, p: (jnp.clip(i - g * steps, 0, steps - 1), 0, 0)
-        return pl.BlockSpec((step_radii, th_dev, ph_dev), at)
-
-    def kernel(place, base, *refs):
-        out = refs[-1]
-        own_part = 1 - place[1]
-        for g in range(len(groups)):
-
-            @pl.when(pl.program_id(0) // steps == g)
-            def _():
-                out[own_part] = base[own_part] + refs[2 * g][...]
-                out[1 - own_part] = base[1 - own_part] + refs[2 * g + 1][...]
-
-    azims = [azim for own, other, _, _ in groups for azim in (own, other)]
-    size = sum(azim.size for azim in azims)
+    fixed = lambda *shape: pl.BlockSpec(shape, lambda i, p: (0, 0, 0))
+    wide = lambda *lead: pl.BlockSpec(lead + (width,), lambda i, p: (0,) * len(lead) + (i,))
+
+    def kernel(place, field, before, after, radius, inv_radius, cot, *refs):
+        out, azims = refs[-1], refs[:-1]
+        rad, inv = radius[...], inv_radius[...]
+        edge = jnp.zeros((3, th_dev, width), jnp.float32)
+
+        def theta(value, which):
+            return diff_along(jnp.concatenate([before[which], value, after[which]], axis=1), 1, th_dev)
+
+        def radial(value):
+            return diff_along(jnp.concatenate([edge, rad * value, edge], axis=0), 0, radii)
+
+        b_azim = field[2]
+        out[0] = (theta(b_azim, 1) + cot[...] * b_azim) * inv
+        out[1] = -radial(b_azim) * inv
+        out[2] = (radial(field[1]) - theta(field[0], 0)) * inv
+        for k, (_, _, own_half, start) in enumerate(groups):
+            half = place[0] if own_half else 1 - place[0]
+            here = pl.ds(half * (radii // 2) + start, azims[2 * k].shape[0])
+            out[1 - place[1], here] += azims[2 * k][...]
+            out[place[1], here] += azims[2 * k + 1][...]
+
+    azims = [azim for own, crossed, _, _ in groups for azim in (own, crossed)]
     return pl.pallas_call(
         kernel,
         grid_spec=pltpu.PrefetchScalarGridSpec(
             num_scalar_prefetch=1,
-            grid=(len(groups) * steps,),
-            in_specs=[current_block] + [group_block(i // 2) for i in range(len(azims))],
-            out_specs=current_block,
+            grid=(ph_dev // width,),
+            in_specs=[
+                wide(3, radii, th_dev),
+                wide(2, radii, 3),
+                wide(2, radii, 3),
+                fixed(radii, 1, 1),
+                fixed(radii, 1, 1),
+                fixed(1, th_dev, 1),
+            ]
+            + [wide(*azim.shape[:-1]) for azim in azims],
+            out_specs=wide(3, radii, th_dev),
+        ),
+        out_shape=jax.ShapeDtypeStruct(magnetic.shape, jnp.float32),
+        compiler_params=pltpu.CompilerParams(vmem_limit_bytes=VMEM),
+        cost_estimate=SHORT,
+    )(place, magnetic, before, after, radius, inv_radius, cot, *azims)
+
+
+def add_pair(place, current, from_y, from_yc, start):
+    depth, th_dev, ph_dev = from_y.shape
+    half = current.shape[1] // 2
+    whole = pl.BlockSpec(memory_space=pltpu.VMEM)
+    block = pl.BlockSpec(
+        (pl.Element(2), pl.Element(depth), pl.Element(th_dev), pl.Element(ph_dev)),
+        lambda i, p: (0, (1 - p[0]) * half + start, 0, 0),
+    )
+
+    def kernel(place, base, own, other, out):
+        part = 1 - place[1]
+        out[part] = base[part] + own[...]
+        out[1 - part] = base[1 - part] + other[...]
+
+    return pl.pallas_call(
+        kernel,
+        grid_spec=pltpu.PrefetchScalarGridSpec(
+            num_scalar_prefetch=1, grid=(1,), in_specs=[block, whole, whole], out_specs=block
         ),
         out_shape=jax.ShapeDtypeStruct(current.shape, jnp.float32),
         input_output_aliases={1: 0},
-        compiler_params=pltpu.CompilerParams(vmem_limit_bytes=VMEM),
-        cost_estimate=pl.CostEstimate(flops=2 * size, bytes_accessed=12 * size, transcendentals=0),
-    )(place, current, *azims)
+        compiler_params=pltpu.CompilerParams(vmem_limit_bytes=VMEM // 6),
+        cost_estimate=SHORT,
+    )(place, current, from_y, from_yc)
 
 
 def after(first, *then):
@@ -334,7 +340,9 @@
 def on_four(magnetic, kept_modes):
     radii, th_dev, ph_dev = (magnetic.shape[1], magnetic.shape[2], magnetic.shape[3])
     half = radii // 2
-    depth = half // CHUNKS
+    total = sum(CHUNKS)
+    depths = [half * part // total for part in CHUNKS]
+    starts = [sum(depths[:k]) for k in range(len(depths))]
     index = lax.axis_index("azim")
     y, c = index // 2, index % 2
     place = jnp.stack([y, c]).astype(jnp.int32)
@@ -343,16 +351,19 @@
     def cut(source, field, start, length):
         return lax.dynamic_slice(source, (field, start, 0, 0), (1, length, th_dev, ph_dev))[0]
 
-    across, diagonal = [], []
+    arrived = []
     source = magnetic
-    for k in range(CHUNKS):
-        to_y = cut(source, c, (1 - y) * half + k * depth, depth)
-        (source,) = after(to_y, source)
-        to_yc = cut(source, 1 - c, (1 - y) * half + k * depth, depth)
-        (source,) = after(to_yc, source)
-        across.append(send(to_y, TO_Y))
-        diagonal.append(send(to_yc, TO_YC))
+    for k, depth in enumerate(depths):
+        both = lax.dynamic_slice(source, (0, (1 - y) * half + starts[k], 0, 0), (2, depth, th_dev, ph_dev))
+        (source,) = after(both, source)
+        arrived.append(send(both, TO_Y))
         if k == 0:
+            lat_size = lax.axis_size("lat")
+            up = [(i, i + 1) for i in range(lat_size - 1)]
+            down = [(i + 1, i) for i in range(lat_size - 1)]
+            last, first = source[0::2, :, th_dev - 3 :], source[0::2, :, :3]
+            (source,) = after((last, first), source)
+            north, south = lax.ppermute(last, "lat", up), lax.ppermute(first, "lat", down)
             to_c = cut(source, 1 - c, y * half, half)
             (source,) = after(to_c, source)
             beside = send(to_c, TO_C)
@@ -364,31 +375,32 @@
     cot = spacing * (jnp.cos(colatitude) / jnp.sin(colatitude))[None, :, None]
     sign_c = (1 - 2 * c).astype(jnp.float32)
     row_gain = (sign_c * spacing * 0.5 / ph_dev) * inv_sin[None, :] * inv_radius[:, 0]
+    row_gain = lax.dynamic_slice_in_dim(row_gain, y * half, half).reshape(half * th_dev, 1)
     band_counts = lax.dynamic_slice_in_dim(kept_modes, band_start, th_dev).astype(jnp.float32)
-    rows = depth * th_dev
-    kept_rows = jnp.broadcast_to(band_counts[None, :], (depth, th_dev)).reshape(rows, 1)
-
-    lat_size = lax.axis_size("lat")
-    up = [(i, i + 1) for i in range(lat_size - 1)]
-    down = [(i + 1, i) for i in range(lat_size - 1)]
-    north = lax.ppermute(source[0::2, :, th_dev - 3 :], "lat", up)
-    south = lax.ppermute(source[0::2, :, :3], "lat", down)
-    current = local_part(magnetic, north, south, radius, inv_radius, cot)
+    row_kept = jnp.broadcast_to(band_counts[None, :], (half, th_dev)).reshape(half * th_dev, 1)
 
     tables = mode_tables(4 * ph_dev)
-    own_half, other_half = [], []
-    for k in range(CHUNKS):
-        gain_rows = lax.dynamic_slice_in_dim(row_gain, y * half + k * depth, depth).reshape(rows, 1)
-        if k == 0:
-            (gain_rows,) = after(current, gain_rows)
-        mine, to_y, to_c, to_yc = transform(
-            place, magnetic, k * depth, across[k], beside, k * depth, diagonal[k], kept_rows, gain_rows, tables
+    mine, from_c, returned = [], [], []
+    for k, (start, depth) in enumerate(zip(starts, depths)):
+        both = arrived[k]
+        if k > 0:
+            (both,) = after((mine[-1], north, south), both)
+            (row_gain,) = after(from_c[-1], row_gain)
+        diagonal = send(cut(both, 1 - c, 0, depth), TO_C)
+        out, to_c, to_y, to_yc = transform(
+            place, magnetic, start, both, beside, diagonal, row_kept, row_gain, tables, k + 1 < len(depths)
         )
-        from_y, from_yc, from_c = send(to_y, TO_Y), send(to_yc, TO_YC), send(to_c, TO_C)
-        own_half.append((mine, from_c, True, k * depth))
-        other_half.append((from_y, from_yc, False, k * depth))
-    current = add_azim(place, current, own_half + other_half[:-1], 2)
-    return add_azim(place, current, other_half[-1:], 2)
+        mine.append(out)
+        from_c.append(send(to_c, TO_C))
+        returned.append(send(to_y, TO_Y))
+    final = returned.pop(), send(to_yc, TO_YC)
+
+    groups = [(own, crossed, True, start) for own, crossed, start in zip(mine, from_c, starts)]
+    for value, start in zip(returned, starts):
+        groups.append((value[0], send(value[1], TO_C), False, start))
+    north, south = after(mine[-1], north, south)
+    current = local_part(place, magnetic, north, south, radius, inv_radius, cot, groups)
+    return add_pair(place, current, *final, starts[-1])
 
 
 def solution(mesh):
@@ -396,7 +408,7 @@
 
     def run(magnetic, kept_modes):
         radii, ph_dev = magnetic.shape[1], magnetic.shape[3]
-        four = lax.axis_size("azim") == 4 and radii % (2 * CHUNKS) == 0 and ph_dev % 256 == 0
+        four = lax.axis_size("azim") == 4 and radii % (2 * sum(CHUNKS)) == 0 and ph_dev % 256 == 0
         return (on_four if four else on_device)(magnetic, kept_modes)
 
     return jax.shard_map(

time: 158 us -> 119 us (0.75)
  waiting for transfers between devices: 70.9 us -> 45.2 us
  Pallas kernels: 50.7 us -> 38 us
    ppermute x11, waiting for transfers between devices: 64.5 us -> 23.6 us  [on_four(): send = lambda value, pairs: lax.ppermute(value, 'azim', pairs)]
    ppermute x2, waiting for transfers between devices: 6.38 us -> 21.6 us  [the longest x1 11.8 us: on_four(): lax.ppermute(last, 'lat', up)]
    pallas_call x3 -> x2, Pallas kernels: 25.4 us -> 16.1 us  [the longest x1 13.3 us: local_part(): pl.pallas_call(kernel, grid_spec=pltpu.PrefetchScalarGridSpec(num_scalar_...]
    squeeze x5 -> x3, local copies, waits for them, and re-layouts: 8.83 us -> 4.1 us  [cut(): lax.dynamic_slice(source, (field, start, 0, 0), (1, length, th_dev, ph_dev))]
    dynamic_slice x1 -> x3, local copies, waits for them, and re-layouts: 0.01 us -> 4.69 us  [the longest x2 4.61 us: on_four(): lax.dynamic_slice(source, (0, (1 - y) * half + starts[k], 0, 0), (2, dept...]
    pallas_call x2, Pallas kernels: 25.3 us -> 21.9 us  [transform(): pl.pallas_call(transform_kernel, grid_spec=grid_spec, out_shape=[jax.Shap...]
    unnamed x22 -> x20, local copies, waits for them, and re-layouts: 4.28 us -> 2.01 us
  transfers between devices with their start and end apart: 13 -> 13, of which waited for: 6 -> 6; matrix products, arithmetic and copies ran while one was open for 9% -> 13% of each run, Pallas kernels for 29% -> 30%
where the time goes in v3:
time: 119 us; the launch traced here: 118 us
  waiting for transfers between devices  45.2 us (38%)
  Pallas kernels  38 us (32%)
  local copies, waits for them, and re-layouts  17.2 us (14%)
  starting transfers between devices  15.4 us (13%)
  other arithmetic  2.19 us (2%)
    ppermute x11, waiting for transfers between devices, on_four(): send = lambda value, pairs: lax.ppermute(value, 'azim', pairs)  23.6 us
    pallas_call x2, Pallas kernels, transform(): pl.pallas_call(transform_kernel, grid_spec=grid_spec, out_shape=[jax.Shap...  21.9 us
    pallas_call x1, Pallas kernels, local_part(): pl.pallas_call(kernel, grid_spec=pltpu.PrefetchScalarGridSpec(num_scalar_...  13.3 us
    ppermute x1, waiting for transfers between devices, on_four(): lax.ppermute(last, 'lat', up)  11.8 us
    ppermute x11, starting transfers between devices, on_four(): send = lambda value, pairs: lax.ppermute(value, 'azim', pairs)  9.9 us
    ppermute x1, waiting for transfers between devices, on_four(): lax.ppermute(first, 'lat', down)  9.82 us
    dynamic_slice x2, local copies, waits for them, and re-layouts, on_four(): lax.dynamic_slice(source, (0, (1 - y) * half + starts[k], 0, 0), (2, dept...  4.61 us
    ppermute x1, starting transfers between devices, on_four(): lax.ppermute(last, 'lat', up)  4.2 us
  transfers between devices with their start and end apart: 13, of which 6 were waited for; matrix products, arithmetic and copies ran while one was open for 13% of the time, Pallas kernels for 30%

profile of v3, /device:TPU:1, one launch (start us, length us, event | category | flops | bytes accessed | tf_op | source)
XLA Modules:
  0.0 118.1 jit_solution(5624826923958921149)
XLA Ops:
  0.0 2.3 %constant_dynamic-slice_fusion.1 = f32[2,8,32,512]{3,2,1,0:T(8,128)} fusion(f32[3,32,32,512]{3,2,1,0:T(8,128)} %field.1, s32[]{:T(128)S(6)} %select_n.33), kind=kLoop, calls=%fused_computation.10 | loop fusion | bytes 2097156 | tf_op jit(solution)/shard_map/dynamic_slice | solution.py:357
  2.3 2.1 %collective-permute-start = (f32[2,8,32,512]{3,2,1,0:T(8,128)}, f32[2,8,32,512]{3,2,1,0:T(8,128)S(1)}, u32[]{:S(2)}, u32[]{:S(2)}) collective-permute-start(f32[2,8,32,512]{3,2,1,0:T(8,128)} %constant_dynamic-slice_fusion.1), channel_id=1, source_target_pairs={{0,2},{2,0},{1,3},{3,1},{4,6},{6,4},{5,7},{7,5},{8,10},{10,8},{9,1... | collective-permute-start | bytes 3145736 | tf_op jit(solution)/shard_map/ppermute | solution.py:349
  4.4 2.8 %fusion = (f32[2,32,3,512]{3,2,1,0:T(4,128)}, f32[2,32,3,512]{3,2,1,0:T(4,128)}) fusion(f32[3,32,32,512]{3,2,1,0:T(8,128)} %field.1), kind=kLoop, calls=%fused_computation.15 | loop fusion | bytes 1572864 | tf_op jit(solution)/shard_map/slice | solution.py:364
  7.1 2.3 %dynamic-slice_bitcast_fusion = f32[16,32,512]{2,1,0:T(8,128)} fusion(f32[3,32,32,512]{3,2,1,0:T(8,128)} %field.1, s32[]{:T(128)S(6)} %select_n.34, s32[]{:T(128)S(6)} %select_n.35), kind=kLoop, calls=%fused_computation | loop fusion | bytes 2097160 | tf_op jit(solution)/shard_map/squeeze | solution.py:352
  9.5 1.0 collective-permute-start.1
  10.4 2.3 %constant_dynamic-slice_fusion = f32[2,8,32,512]{3,2,1,0:T(8,128)} fusion(f32[3,32,32,512]{3,2,1,0:T(8,128)} %field.1, s32[]{:T(128)S(6)} %select_n.38), kind=kLoop, calls=%fused_computation.9 | loop fusion | bytes 2097156 | tf_op jit(solution)/shard_map/dynamic_slice | solution.py:357
  12.7 0.0 collective-permute-start.5
  12.7 0.1 dynamic-slice
  12.8 14.6 %collective-permute-done.across = f32[2,8,32,512]{3,2,1,0:T(8,128)S(1)} collective-permute-done((f32[2,8,32,512]{3,2,1,0:T(8,128)}, f32[2,8,32,512]{3,2,1,0:T(8,128)S(1)}, u32[]{:S(2)}, u32[]{:S(2)}) %collective-permute-start) | collective-permute-done | bytes 1048608 | tf_op jit(solution)/shard_map/ppermute | solution.py:349
  27.5 0.9 dynamic-slice_bitcast_fusion.2
  28.4 2.1 %collective-permute-start.2 = (f32[8,32,512]{2,1,0:T(8,128)}, f32[8,32,512]{2,1,0:T(8,128)}, u32[]{:S(2)}, u32[]{:S(2)}) collective-permute-start(f32[8,32,512]{2,1,0:T(8,128)} %dynamic-slice_bitcast_fusion.2), channel_id=1, source_target_pairs={{0,1},{1,0},{2,3},{3,2},{4,5},{5,4},{6,7},{7,6},{8,9},{9,8},{10,11... | collective-permute-start | bytes 1572872 | tf_op jit(solution)/shard_map/ppermute | solution.py:349
  30.5 0.1 broadcast_multiply_fusion
  30.6 0.1 reshape.73
  30.7 0.1 dynamic-slice_convert_fusion
  30.7 1.0 reshape.74.kept
  31.7 0.8 copy.16.gain
  32.6 0.7 pad_add_fusion.place
  33.2 0.0 collective-permute-done.2.diagonal
  33.3 1.0 copy-done.1
  34.2 10.9 %shard_map.91 = (f32[8,32,512]{2,1,0:T(8,128)}, f32[8,32,512]{2,1,0:T(8,128)}, f32[2,8,32,512]{3,2,1,0:T(8,128)}) custom-call(s32[2]{0:T(128)} %pad_add_fusion.place, f32[3,32,32,512]{3,2,1,0:T(8,128)} %field.1, f32[2,8,32,512]{3,2,1,0:T(8,128)} %copy-done.3, f32[16,32,512]{2,1,0:T(8,128)} %copy-done.1, f32[8,32,512]{2,1,0:T(8,128)} %collective-permute-done.2.diagonal, ...), custom_call_target="tpu_custom_call" | custom-call | flops 1 | bytes 1 | tf_op jit(solution)/shard_map/pallas_call | solution.py:241
  45.2 1.8 %collective-permute-start.9 = (f32[2,8,32,512]{3,2,1,0:T(8,128)}, f32[2,8,32,512]{3,2,1,0:T(8,128)S(1)}, u32[]{:S(2)}, u32[]{:S(2)}) collective-permute-start(f32[2,8,32,512]{3,2,1,0:T(8,128)} %get-tuple-element.30), channel_id=1, source_target_pairs={{0,2},{2,0},{1,3},{3,1},{4,6},{6,4},{5,7},{7,5},{8,10},{10,8},{9,1... | collective-permute-start | bytes 3145736 | tf_op jit(solution)/shard_map/ppermute | solution.py:349
  47.0 1.3 %collective-permute-start.4 = (f32[2,32,3,512]{3,2,1,0:T(4,128)}, f32[2,32,3,512]{3,2,1,0:T(4,128)S(1)}, u32[]{:S(2)}, u32[]{:S(2)}) collective-permute-start(f32[2,32,3,512]{3,2,1,0:T(4,128)} %get-tuple-element.33), channel_id=1, source_target_pairs={{4,0},{8,4},{12,8},{16,12},{20,16},{24,20},{28,24},{5,1},{9,5},{13... | collective-permute-start | bytes 1179656 | tf_op jit(solution)/shard_map/ppermute | solution.py:366
  48.3 4.2 %collective-permute-start.3 = (f32[2,32,3,512]{3,2,1,0:T(4,128)S(1)}, f32[2,32,3,512]{3,2,1,0:T(4,128)S(1)}, u32[]{:S(2)}, u32[]{:S(2)}) collective-permute-start(f32[2,32,3,512]{3,2,1,0:T(4,128)S(1)} %copy-done.8), channel_id=1, source_target_pairs={{0,4},{4,8},{8,12},{12,16},{16,20},{20,24},{24,28},{1,5},{5,9},{9,... | collective-permute-start | bytes 1179656 | tf_op jit(solution)/shard_map/ppermute | solution.py:366
  52.5 9.8 %collective-permute-done.4.after = f32[2,32,3,512]{3,2,1,0:T(4,128)S(1)} collective-permute-done((f32[2,32,3,512]{3,2,1,0:T(4,128)}, f32[2,32,3,512]{3,2,1,0:T(4,128)S(1)}, u32[]{:S(2)}, u32[]{:S(2)}) %collective-permute-start.4) | collective-permute-done | bytes 393248 | tf_op jit(solution)/shard_map/ppermute | solution.py:366
  62.4 11.8 %collective-permute-done.3.before = f32[2,32,3,512]{3,2,1,0:T(4,128)S(1)} collective-permute-done((f32[2,32,3,512]{3,2,1,0:T(4,128)S(1)}, f32[2,32,3,512]{3,2,1,0:T(4,128)S(1)}, u32[]{:S(2)}, u32[]{:S(2)}) %collective-permute-start.3) | collective-permute-done | bytes 393248 | tf_op jit(solution)/shard_map/ppermute | solution.py:366
  74.1 0.5 collective-permute-start.7
  74.6 0.8 dynamic-slice_bitcast_fusion.1
  75.4 0.1 collective-permute-start.6
  75.6 0.9 collective-permute-done.7.refs_1_
  76.5 0.8 copy.18.gain
  77.3 0.4 collective-permute-done.6.diagonal
  77.7 11.0 %shard_map.92 = (f32[8,32,512]{2,1,0:T(8,128)}, f32[8,32,512]{2,1,0:T(8,128)}, f32[8,32,512]{2,1,0:T(8,128)}, f32[8,32,512]{2,1,0:T(8,128)}) custom-call(s32[2]{0:T(128)} %pad_add_fusion.place, f32[3,32,32,512]{3,2,1,0:T(8,128)} %field.1, f32[2,8,32,512]{3,2,1,0:T(8,128)} %copy-done.2, f32[16,32,512]{2,1,0:T(8,128)} %copy-done.1, ...), custom_call_target="tpu_custom_call" | custom-call | flops 1 | bytes 1 | tf_op jit(solution)/shard_map/pallas_call | solution.py:241
  88.7 0.2 collective-permute-start.8
  88.9 0.0 collective-permute-done.9
  88.9 0.9 slice_bitcast_fusion
  89.8 0.4 collective-permute-start.10
  90.2 0.2 collective-permute-start.11
  90.4 1.5 %collective-permute-start.12 = (f32[8,32,512]{2,1,0:T(8,128)}, f32[8,32,512]{2,1,0:T(8,128)S(1)}, u32[]{:S(2)}, u32[]{:S(2)}) collective-permute-start(f32[8,32,512]{2,1,0:T(8,128)} %get-tuple-element.32), channel_id=1, source_target_pairs={{0,3},{3,0},{1,2},{2,1},{4,7},{7,4},{5,6},{6,5},{8,11},{11,8},{9,1... | collective-permute-start | bytes 1572872 | tf_op jit(solution)/shard_map/ppermute | solution.py:349
  91.9 0.7 divide_multiply_fusion.cot
  92.6 0.6 multiply_add_fusion
  93.3 0.0 collective-permute-done.8.refs_3_
  93.3 0.0 collective-permute-done.10.refs_5_
  93.3 0.8 copy-done.6
  94.1 0.2 copy-done.7
  94.3 13.3 %shard_map.93.base = f32[3,32,32,512]{3,2,1,0:T(8,128)} custom-call(s32[2]{0:T(128)} %pad_add_fusion.place, f32[3,32,32,512]{3,2,1,0:T(8,128)} %field.1, f32[2,32,3,512]{3,2,1,0:T(4,128)} %copy-done.5, f32[2,32,3,512]{3,2,1,0:T(4,128)} %copy-done.4, f32[32,1,1]{2,1,0:T(1,128)} %get-tuple-element.37.radius, f32[32,1,1]{2,1,0:T(1,128)} %get-tuple-element.38.inv_radius, ...), custom_call_target="tpu_custom_call" | custom-call | flops 1 | bytes 1 | tf_op jit(solution)/shard_map/pallas_call | solution.py:288
  107.6 0.0 collective-permute-done.11.own
  107.6 7.7 %collective-permute-done.12.other = f32[8,32,512]{2,1,0:T(8,128)S(1)} collective-permute-done((f32[8,32,512]{2,1,0:T(8,128)}, f32[8,32,512]{2,1,0:T(8,128)S(1)}, u32[]{:S(2)}, u32[]{:S(2)}) %collective-permute-start.12) | collective-permute-done | bytes 524320 | tf_op jit(solution)/shard_map/ppermute | solution.py:349
  115.3 2.8 %shard_map.94 = f32[3,32,32,512]{3,2,1,0:T(8,128)} custom-call(s32[2]{0:T(128)S(1)} %copy-done, f32[3,32,32,512]{3,2,1,0:T(8,128)} %shard_map.93.base, f32[8,32,512]{2,1,0:T(8,128)S(1)} %collective-permute-done.11.own, f32[8,32,512]{2,1,0:T(8,128)S(1)} %collective-permute-done.12.other), custom_call_target="tpu_custom_call", output_to_operand_aliasing={{}: (1, {})} | custom-call | flops 1 | bytes 1 | tf_op jit(solution)/shard_map/pallas_call | solution.py:324
  (22 shorter events, 0.1 us)
Async XLA Ops:
  0.0 30.7 %copy-start.9 = (s32[256]{0:T(256)S(1)}, s32[256]{0:T(256)}, u32[]{:S(2)}) copy-start(s32[256]{0:T(256)} %param.10) | copy-start | bytes 3076
  2.3 25.2 %collective-permute-start = (f32[2,8,32,512]{3,2,1,0:T(8,128)}, f32[2,8,32,512]{3,2,1,0:T(8,128)S(1)}, u32[]{:S(2)}, u32[]{:S(2)}) collective-permute-start(f32[2,8,32,512]{3,2,1,0:T(8,128)} %constant_dynamic-slice_fusion.1), channel_id=1, source_target_pairs={{0,2},{2,0},{1,3},{3,1},{4,6},{6,4},{5,7},{7,5},{8,10},{10,8},{9,1... | collective-permute-start | bytes 3145736 | tf_op jit(solution)/shard_map/ppermute | solution.py:349
  9.5 23.8 %collective-permute-start.1 = (f32[16,32,512]{2,1,0:T(8,128)}, f32[16,32,512]{2,1,0:T(8,128)S(1)}, u32[]{:S(2)}, u32[]{:S(2)}) collective-permute-start(f32[16,32,512]{2,1,0:T(8,128)} %dynamic-slice_bitcast_fusion), channel_id=1, source_target_pairs={{0,1},{1,0},{2,3},{3,2},{4,5},{5,4},{6,7},{7,6},{8,9},{9,8},{10,11... | collective-permute-start | bytes 3145736 | tf_op jit(solution)/shard_map/ppermute | solution.py:349
  12.7 61.4 %collective-permute-start.5 = (f32[2,8,32,512]{3,2,1,0:T(8,128)}, f32[2,8,32,512]{3,2,1,0:T(8,128)S(1)}, u32[]{:S(2)}, u32[]{:S(2)}) collective-permute-start(f32[2,8,32,512]{3,2,1,0:T(8,128)} %constant_dynamic-slice_fusion), channel_id=1, source_target_pairs={{0,2},{2,0},{1,3},{3,1},{4,6},{6,4},{5,7},{7,5},{8,10},{10,8},{9,1... | collective-permute-start | bytes 3145736 | tf_op jit(solution)/shard_map/ppermute | solution.py:349
  27.5 5.8 %copy-start.3 = (f32[2,8,32,512]{3,2,1,0:T(8,128)}, f32[2,8,32,512]{3,2,1,0:T(8,128)S(1)}, u32[]{:S(2)}) copy-start(f32[2,8,32,512]{3,2,1,0:T(8,128)S(1)} %collective-permute-done.across) | copy-start | bytes 3145732
  28.4 4.9 %collective-permute-start.2 = (f32[8,32,512]{2,1,0:T(8,128)}, f32[8,32,512]{2,1,0:T(8,128)}, u32[]{:S(2)}, u32[]{:S(2)}) collective-permute-start(f32[8,32,512]{2,1,0:T(8,128)} %dynamic-slice_bitcast_fusion.2), channel_id=1, source_target_pairs={{0,1},{1,0},{2,3},{3,2},{4,5},{5,4},{6,7},{7,6},{8,9},{9,8},{10,11... | collective-permute-start | bytes 1572872 | tf_op jit(solution)/shard_map/ppermute | solution.py:349
  33.2 15.1 %copy-start.8 = (f32[2,32,3,512]{3,2,1,0:T(4,128)S(1)}, f32[2,32,3,512]{3,2,1,0:T(4,128)}, u32[]{:S(2)}) copy-start(f32[2,32,3,512]{3,2,1,0:T(4,128)} %get-tuple-element.34) | copy-start | bytes 1179652
  33.2 1.0 copy-start.1
  45.2 43.7 %collective-permute-start.9 = (f32[2,8,32,512]{3,2,1,0:T(8,128)}, f32[2,8,32,512]{3,2,1,0:T(8,128)S(1)}, u32[]{:S(2)}, u32[]{:S(2)}) collective-permute-start(f32[2,8,32,512]{3,2,1,0:T(8,128)} %get-tuple-element.30), channel_id=1, source_target_pairs={{0,2},{2,0},{1,3},{3,1},{4,6},{6,4},{5,7},{7,5},{8,10},{10,8},{9,1... | collective-permute-start | bytes 3145736 | tf_op jit(solution)/shard_map/ppermute | solution.py:349
  47.0 15.3 %collective-permute-start.4 = (f32[2,32,3,512]{3,2,1,0:T(4,128)}, f32[2,32,3,512]{3,2,1,0:T(4,128)S(1)}, u32[]{:S(2)}, u32[]{:S(2)}) collective-permute-start(f32[2,32,3,512]{3,2,1,0:T(4,128)} %get-tuple-element.33), channel_id=1, source_target_pairs={{4,0},{8,4},{12,8},{16,12},{20,16},{24,20},{28,24},{5,1},{9,5},{13... | collective-permute-start | bytes 1179656 | tf_op jit(solution)/shard_map/ppermute | solution.py:366
  48.3 25.8 %collective-permute-start.3 = (f32[2,32,3,512]{3,2,1,0:T(4,128)S(1)}, f32[2,32,3,512]{3,2,1,0:T(4,128)S(1)}, u32[]{:S(2)}, u32[]{:S(2)}) collective-permute-start(f32[2,32,3,512]{3,2,1,0:T(4,128)S(1)} %copy-done.8), channel_id=1, source_target_pairs={{0,4},{4,8},{8,12},{12,16},{16,20},{20,24},{24,28},{1,5},{5,9},{9,... | collective-permute-start | bytes 1179656 | tf_op jit(solution)/shard_map/ppermute | solution.py:366
  62.3 30.9 %copy-start.4 = (f32[2,32,3,512]{3,2,1,0:T(4,128)}, f32[2,32,3,512]{3,2,1,0:T(4,128)S(1)}, u32[]{:S(2)}) copy-start(f32[2,32,3,512]{3,2,1,0:T(4,128)S(1)} %collective-permute-done.4.after) | copy-start | bytes 1179652
  74.1 19.2 %copy-start.5 = (f32[2,32,3,512]{3,2,1,0:T(4,128)}, f32[2,32,3,512]{3,2,1,0:T(4,128)S(1)}, u32[]{:S(2)}) copy-start(f32[2,32,3,512]{3,2,1,0:T(4,128)S(1)} %collective-permute-done.3.before) | copy-start | bytes 1179652
  74.1 3.6 %copy-start.2 = (f32[2,8,32,512]{3,2,1,0:T(8,128)}, f32[2,8,32,512]{3,2,1,0:T(8,128)S(1)}, u32[]{:S(2)}) copy-start(f32[2,8,32,512]{3,2,1,0:T(8,128)S(1)} %collective-permute-done.5.across) | copy-start | bytes 3145732
  74.1 2.4 %collective-permute-start.7 = (f32[8,32,512]{2,1,0:T(8,128)}, f32[8,32,512]{2,1,0:T(8,128)}, u32[]{:S(2)}, u32[]{:S(2)}) collective-permute-start(f32[8,32,512]{2,1,0:T(8,128)} %get-tuple-element.24), channel_id=1, source_target_pairs={{0,1},{1,0},{2,3},{3,2},{4,5},{5,4},{6,7},{7,6},{8,9},{9,8},{10,11... | collective-permute-start | bytes 1572872 | tf_op jit(solution)/shard_map/ppermute | solution.py:349
  75.4 2.3 %collective-permute-start.6 = (f32[8,32,512]{2,1,0:T(8,128)}, f32[8,32,512]{2,1,0:T(8,128)}, u32[]{:S(2)}, u32[]{:S(2)}) collective-permute-start(f32[8,32,512]{2,1,0:T(8,128)} %dynamic-slice_bitcast_fusion.1), channel_id=1, source_target_pairs={{0,1},{1,0},{2,3},{3,2},{4,5},{5,4},{6,7},{7,6},{8,9},{9,8},{10,11... | collective-permute-start | bytes 1572872 | tf_op jit(solution)/shard_map/ppermute | solution.py:349
  88.7 4.6 %collective-permute-start.8 = (f32[8,32,512]{2,1,0:T(8,128)}, f32[8,32,512]{2,1,0:T(8,128)S(1)}, u32[]{:S(2)}, u32[]{:S(2)}) collective-permute-start(f32[8,32,512]{2,1,0:T(8,128)} %get-tuple-element.29), channel_id=1, source_target_pairs={{0,1},{1,0},{2,3},{3,2},{4,5},{5,4},{6,7},{7,6},{8,9},{9,8},{10,11... | collective-permute-start | bytes 1572872 | tf_op jit(solution)/shard_map/ppermute | solution.py:349
  89.8 3.5 %collective-permute-start.10 = (f32[8,32,512]{2,1,0:T(8,128)S(1)}, f32[8,32,512]{2,1,0:T(8,128)S(1)}, u32[]{:S(2)}, u32[]{:S(2)}) collective-permute-start(f32[8,32,512]{2,1,0:T(8,128)S(1)} %get-tuple-element.35), channel_id=1, source_target_pairs={{0,1},{1,0},{2,3},{3,2},{4,5},{5,4},{6,7},{7,6},{8,9},{9,8},{10,11... | collective-permute-start | bytes 1572872 | tf_op jit(solution)/shard_map/ppermute | solution.py:349
  90.2 17.4 %collective-permute-start.11 = (f32[8,32,512]{2,1,0:T(8,128)}, f32[8,32,512]{2,1,0:T(8,128)S(1)}, u32[]{:S(2)}, u32[]{:S(2)}) collective-permute-start(f32[8,32,512]{2,1,0:T(8,128)} %get-tuple-element.31), channel_id=1, source_target_pairs={{0,2},{2,0},{1,3},{3,1},{4,6},{6,4},{5,7},{7,5},{8,10},{10,8},{9,1... | collective-permute-start | bytes 1572872 | tf_op jit(solution)/shard_map/ppermute | solution.py:349
  90.4 24.9 %collective-permute-start.12 = (f32[8,32,512]{2,1,0:T(8,128)}, f32[8,32,512]{2,1,0:T(8,128)S(1)}, u32[]{:S(2)}, u32[]{:S(2)}) collective-permute-start(f32[8,32,512]{2,1,0:T(8,128)} %get-tuple-element.32), channel_id=1, source_target_pairs={{0,3},{3,0},{1,2},{2,1},{4,7},{7,4},{5,6},{6,5},{8,11},{11,8},{9,1... | collective-permute-start | bytes 1572872 | tf_op jit(solution)/shard_map/ppermute | solution.py:349
  93.3 0.8 copy-start.6
  93.3 1.0 copy-start.7
  94.3 21.0 %copy-start = (s32[2]{0:T(128)S(1)}, s32[2]{0:T(128)}, u32[]{:S(2)}) copy-start(s32[2]{0:T(128)} %pad_add_fusion.place) | copy-start | bytes 28

commit v4 on v3

--- a/solution.py
+++ b/solution.py
@@ -135,7 +135,7 @@
     return jnp.stack([j_radial, j_polar, j_azim])
 
 
-CHUNKS = (8, 8)
+CHUNKS = (7, 9)
 TO_Y = [(0, 2), (2, 0), (1, 3), (3, 1)]
 TO_C = [(0, 1), (1, 0), (2, 3), (3, 2)]
 TO_YC = [(0, 3), (3, 0), (1, 2), (2, 1)]
@@ -248,13 +248,25 @@
     return (*outs, None) if paired else outs
 
 
-def diff_along(padded, axis, length):
-    total = None
-    for offset in range(-3, 4):
-        if offset != 0:
-            term = stencil_coeffs[offset + 3] * lax.slice_in_dim(padded, 3 + offset, 3 + offset + length, axis=axis)
-            total = term if total is None else total + term
-    return total
+def edge_rows(magnetic):
+    radii, th_dev, ph_dev = magnetic.shape[1:]
+    edge = lambda at: pl.BlockSpec((None, radii, 8, ph_dev), lambda i: (2 * i, 0, at, 0))
+    rows = pl.BlockSpec((None, 3, radii, ph_dev), lambda i: (i, 0, 0, 0))
+
+    def kernel(top, bottom, last, first):
+        for i in range(3):
+            last[i] = bottom[:, 5 + i, :]
+            first[i] = top[:, i, :]
+
+    return pl.pallas_call(
+        kernel,
+        grid=(2,),
+        in_specs=[edge(0), edge(th_dev // 8 - 1)],
+        out_specs=[rows, rows],
+        out_shape=[jax.ShapeDtypeStruct((2, 3, radii, ph_dev), jnp.float32)] * 2,
+        compiler_params=pltpu.CompilerParams(vmem_limit_bytes=VMEM),
+        cost_estimate=SHORT,
+    )(magnetic, magnetic)
 
 
 def local_part(place, magnetic, before, after, radius, inv_radius, cot, groups):
@@ -262,21 +274,29 @@
     radii, th_dev, ph_dev = magnetic.shape[1:]
     fixed = lambda *shape: pl.BlockSpec(shape, lambda i, p: (0, 0, 0))
     wide = lambda *lead: pl.BlockSpec(lead + (width,), lambda i, p: (0,) * len(lead) + (i,))
+    weights = [stencil_coeffs[3 + offset] for offset in (1, 2, 3)]
 
     def kernel(place, field, before, after, radius, inv_radius, cot, *refs):
-        out, azims = refs[-1], refs[:-1]
-        rad, inv = radius[...], inv_radius[...]
-        edge = jnp.zeros((3, th_dev, width), jnp.float32)
+        azims, out, rows, layers = refs[:-3], *refs[-3:]
+        inv = inv_radius[...]
 
         def theta(value, which):
-            return diff_along(jnp.concatenate([before[which], value, after[which]], axis=1), 1, th_dev)
+            rows[:, 8 : 8 + th_dev, :] = value
+            for i in range(3):
+                rows[:, 5 + i, :] = before[which, i]
+                rows[:, 8 + th_dev + i, :] = after[which, i]
+            shifted = lambda offset: rows[:, 8 + offset : 8 + offset + th_dev, :]
+            return sum(w * (shifted(o) - shifted(-o)) for o, w in enumerate(weights, 1))
 
         def radial(value):
-            return diff_along(jnp.concatenate([edge, rad * value, edge], axis=0), 0, radii)
-
-        b_azim = field[2]
-        out[0] = (theta(b_azim, 1) + cot[...] * b_azim) * inv
-        out[1] = -radial(b_azim) * inv
+            layers[3 : 3 + radii] = radius[...] * value
+            shifted = lambda offset: layers[3 + offset : 3 + offset + radii]
+            return sum(w * (shifted(o) - shifted(-o)) for o, w in enumerate(weights, 1))
+
+        layers[:3] = jnp.zeros((3, th_dev, width), jnp.float32)
+        layers[3 + radii :] = jnp.zeros((3, th_dev, width), jnp.float32)
+        out[0] = (theta(field[2], 1) + cot[...] * field[2]) * inv
+        out[1] = -radial(field[2]) * inv
         out[2] = (radial(field[1]) - theta(field[0], 0)) * inv
         for k, (_, _, own_half, start) in enumerate(groups):
             half = place[0] if own_half else 1 - place[0]
@@ -292,14 +312,18 @@
             grid=(ph_dev // width,),
             in_specs=[
                 wide(3, radii, th_dev),
-                wide(2, radii, 3),
-                wide(2, radii, 3),
+                wide(2, 3, radii),
+                wide(2, 3, radii),
                 fixed(radii, 1, 1),
                 fixed(radii, 1, 1),
                 fixed(1, th_dev, 1),
             ]
             + [wide(*azim.shape[:-1]) for azim in azims],
             out_specs=wide(3, radii, th_dev),
+            scratch_shapes=[
+                pltpu.VMEM((radii, th_dev + 16, width), jnp.float32),
+                pltpu.VMEM((radii + 6, th_dev, width), jnp.float32),
+            ],
         ),
         out_shape=jax.ShapeDtypeStruct(magnetic.shape, jnp.float32),
         compiler_params=pltpu.CompilerParams(vmem_limit_bytes=VMEM),
@@ -361,7 +385,7 @@
             lat_size = lax.axis_size("lat")
             up = [(i, i + 1) for i in range(lat_size - 1)]
             down = [(i + 1, i) for i in range(lat_size - 1)]
-            last, first = source[0::2, :, th_dev - 3 :], source[0::2, :, :3]
+            last, first = edge_rows(source)
             (source,) = after((last, first), source)
             north, south = lax.ppermute(last, "lat", up), lax.ppermute(first, "lat", down)
             to_c = cut(source, 1 - c, y * half, half)
@@ -384,8 +408,8 @@
     for k, (start, depth) in enumerate(zip(starts, depths)):
         both = arrived[k]
         if k > 0:
-            (both,) = after((mine[-1], north, south), both)
-            (row_gain,) = after(from_c[-1], row_gain)
+            (both,) = after(mine[-1], both)
+        (row_gain,) = after(from_c[-1] if k > 0 else (north, south), row_gain)
         diagonal = send(cut(both, 1 - c, 0, depth), TO_C)
         out, to_c, to_y, to_yc = transform(
             place, magnetic, start, both, beside, diagonal, row_kept, row_gain, tables, k + 1 < len(depths)

time: 119 us -> 101 us (0.85)
  waiting for transfers between devices: 45.2 us -> 30.2 us
  local copies, waits for them, and re-layouts: 17.2 us -> 15.2 us
    ppermute x1, waiting for transfers between devices: 9.82 us -> 0.01 us  [on_four(): lax.ppermute(first, 'lat', down)]
    ppermute x1, waiting for transfers between devices: 11.8 us -> 3.16 us  [on_four(): lax.ppermute(last, 'lat', up)]
    pallas_call x1, Pallas kernels: 13.3 us -> 9.74 us  [local_part(): pl.pallas_call(kernel, grid_spec=pltpu.PrefetchScalarGridSpec(num_scalar_...]
    ppermute x11, waiting for transfers between devices: 23.6 us -> 27.1 us  [on_four(): send = lambda value, pairs: lax.ppermute(value, 'azim', pairs)]
    slice x1 -> x0, local copies, waits for them, and re-layouts: 2.76 us -> none  [on_four(): last, first = (source[0::2, :, th_dev - 3:], source[0::2, :, :3])]
    pallas_call x0 -> x1, Pallas kernels: none -> 2.38 us  [edge_rows(): pl.pallas_call(kernel, grid=(2,), in_specs=[edge(0), edge(th_dev // 8 - 1...]
  transfers between devices with their start and end apart: 13 -> 13, of which waited for: 6 -> 7; matrix products, arithmetic and copies ran while one was open for 13% -> 12% of each run, Pallas kernels for 30% -> 34%
where the time goes in v4:
time: 101 us; the launch traced here: 100 us
  Pallas kernels  37 us (37%)
  waiting for transfers between devices  30.2 us (30%)
  starting transfers between devices  15.7 us (16%)
  local copies, waits for them, and re-layouts  15.2 us (15%)
  other arithmetic  2.18 us (2%)
    ppermute x11, waiting for transfers between devices, on_four(): send = lambda value, pairs: lax.ppermute(value, 'azim', pairs)  27.1 us
    pallas_call x2, Pallas kernels, transform(): pl.pallas_call(transform_kernel, grid_spec=grid_spec, out_shape=[jax.Shap...  22 us
    ppermute x11, starting transfers between devices, on_four(): send = lambda value, pairs: lax.ppermute(value, 'azim', pairs)  11 us
    pallas_call x1, Pallas kernels, local_part(): pl.pallas_call(kernel, grid_spec=pltpu.PrefetchScalarGridSpec(num_scalar_...  9.74 us
    dynamic_slice x2, local copies, waits for them, and re-layouts, on_four(): lax.dynamic_slice(source, (0, (1 - y) * half + starts[k], 0, 0), (2, dept...  4.6 us
    squeeze x3, local copies, waits for them, and re-layouts, cut(): lax.dynamic_slice(source, (field, start, 0, 0), (1, length, th_dev, ph_dev))  4.13 us
    ppermute x1, starting transfers between devices, on_four(): lax.ppermute(last, 'lat', up)  3.35 us
    ppermute x1, waiting for transfers between devices, on_four(): lax.ppermute(last, 'lat', up)  3.16 us
  transfers between devices with their start and end apart: 13, of which 7 were waited for; matrix products, arithmetic and copies ran while one was open for 12% of the time, Pallas kernels for 34%

profile of v4, /device:TPU:1, one launch (start us, length us, event | category | flops | bytes accessed | tf_op | source)
XLA Modules:
  0.0 100.5 jit_solution(7792158552567777622)
XLA Ops:
  0.0 2.2 %constant_dynamic-slice_fusion.1 = f32[2,7,32,512]{3,2,1,0:T(8,128)} fusion(f32[3,32,32,512]{3,2,1,0:T(8,128)} %field.1, s32[]{:T(128)S(6)} %select_n.33), kind=kLoop, calls=%fused_computation.10 | loop fusion | bytes 1835012 | tf_op jit(solution)/shard_map/dynamic_slice | solution.py:381
  2.2 2.1 %collective-permute-start = (f32[2,7,32,512]{3,2,1,0:T(8,128)}, f32[2,7,32,512]{3,2,1,0:T(8,128)S(1)}, u32[]{:S(2)}, u32[]{:S(2)}) collective-permute-start(f32[2,7,32,512]{3,2,1,0:T(8,128)} %constant_dynamic-slice_fusion.1), channel_id=1, source_target_pairs={{0,2},{2,0},{1,3},{3,1},{4,6},{6,4},{5,7},{7,5},{8,10},{10,8},{9,1... | collective-permute-start | bytes 2752520 | tf_op jit(solution)/shard_map/ppermute | solution.py:373
  4.3 2.4 %shard_map.91 = (f32[2,3,32,512]{3,2,1,0:T(8,128)}, f32[2,3,32,512]{3,2,1,0:T(8,128)}) custom-call(f32[3,32,32,512]{3,2,1,0:T(8,128)} %field.1, f32[3,32,32,512]{3,2,1,0:T(8,128)} %field.1), custom_call_target="tpu_custom_call" | custom-call | flops 1 | bytes 1 | tf_op jit(solution)/shard_map/pallas_call | solution.py:261
  6.6 2.3 %dynamic-slice_bitcast_fusion = f32[16,32,512]{2,1,0:T(8,128)} fusion(f32[3,32,32,512]{3,2,1,0:T(8,128)} %field.1, s32[]{:T(128)S(6)} %select_n.34, s32[]{:T(128)S(6)} %select_n.35), kind=kLoop, calls=%fused_computation | loop fusion | bytes 2097160 | tf_op jit(solution)/shard_map/squeeze | solution.py:376
  9.0 1.0 collective-permute-start.1
  9.9 2.4 %constant_dynamic-slice_fusion = f32[2,9,32,512]{3,2,1,0:T(8,128)} fusion(f32[3,32,32,512]{3,2,1,0:T(8,128)} %field.1, s32[]{:T(128)S(6)} %select_n.38), kind=kLoop, calls=%fused_computation.9 | loop fusion | bytes 2359300 | tf_op jit(solution)/shard_map/dynamic_slice | solution.py:381
  12.3 0.0 collective-permute-start.5
  12.3 3.4 %collective-permute-start.3 = (f32[2,3,32,512]{3,2,1,0:T(8,128)}, f32[2,3,32,512]{3,2,1,0:T(8,128)S(1)}, u32[]{:S(2)}, u32[]{:S(2)}) collective-permute-start(f32[2,3,32,512]{3,2,1,0:T(8,128)} %get-tuple-element.23), channel_id=1, source_target_pairs={{0,4},{4,8},{8,12},{12,16},{16,20},{20,24},{24,28},{1,5},{5,9},{9,... | collective-permute-start | bytes 1179656 | tf_op jit(solution)/shard_map/ppermute | solution.py:390
  15.7 1.3 %collective-permute-start.4 = (f32[2,3,32,512]{3,2,1,0:T(8,128)}, f32[2,3,32,512]{3,2,1,0:T(8,128)}, u32[]{:S(2)}, u32[]{:S(2)}) collective-permute-start(f32[2,3,32,512]{3,2,1,0:T(8,128)} %get-tuple-element.24), channel_id=1, source_target_pairs={{4,0},{8,4},{12,8},{16,12},{20,16},{24,20},{28,24},{5,1},{9,5},{13... | collective-permute-start | bytes 1179656 | tf_op jit(solution)/shard_map/ppermute | solution.py:390
  17.0 7.6 %collective-permute-done.across = f32[2,7,32,512]{3,2,1,0:T(8,128)S(1)} collective-permute-done((f32[2,7,32,512]{3,2,1,0:T(8,128)}, f32[2,7,32,512]{3,2,1,0:T(8,128)S(1)}, u32[]{:S(2)}, u32[]{:S(2)}) %collective-permute-start) | collective-permute-done | bytes 917536 | tf_op jit(solution)/shard_map/ppermute | solution.py:373
  24.7 0.9 dynamic-slice_bitcast_fusion.2
  25.5 2.0 %collective-permute-start.2 = (f32[7,32,512]{2,1,0:T(8,128)}, f32[7,32,512]{2,1,0:T(8,128)}, u32[]{:S(2)}, u32[]{:S(2)}) collective-permute-start(f32[7,32,512]{2,1,0:T(8,128)} %dynamic-slice_bitcast_fusion.2), channel_id=1, source_target_pairs={{0,1},{1,0},{2,3},{3,2},{4,5},{5,4},{6,7},{7,6},{8,9},{9,8},{10,11... | collective-permute-start | bytes 1376264 | tf_op jit(solution)/shard_map/ppermute | solution.py:373
  27.5 0.1 dynamic-slice
  27.6 0.1 broadcast_multiply_fusion
  27.7 0.1 reshape.73
  27.8 0.1 dynamic-slice_convert_fusion
  27.8 1.0 reshape.74.kept
  28.8 0.7 pad_add_fusion.place
  29.5 3.2 %collective-permute-done.3.before = f32[2,3,32,512]{3,2,1,0:T(8,128)S(1)} collective-permute-done((f32[2,3,32,512]{3,2,1,0:T(8,128)}, f32[2,3,32,512]{3,2,1,0:T(8,128)S(1)}, u32[]{:S(2)}, u32[]{:S(2)}) %collective-permute-start.3) | collective-permute-done | bytes 393248 | tf_op jit(solution)/shard_map/ppermute | solution.py:390
  32.6 0.0 collective-permute-done.4.after
  32.6 0.9 copy.16.gain
  33.5 0.0 collective-permute-done.2.diagonal
  33.5 1.0 copy-done.1
  34.5 10.2 %shard_map.92 = (f32[7,32,512]{2,1,0:T(8,128)}, f32[7,32,512]{2,1,0:T(8,128)}, f32[2,7,32,512]{3,2,1,0:T(8,128)}) custom-call(s32[2]{0:T(128)} %pad_add_fusion.place, f32[3,32,32,512]{3,2,1,0:T(8,128)} %field.1, f32[2,7,32,512]{3,2,1,0:T(8,128)} %copy-done.3, f32[16,32,512]{2,1,0:T(8,128)} %copy-done.1, f32[7,32,512]{2,1,0:T(8,128)} %collective-permute-done.2.diagonal, ...), custom_call_target="tpu_custom_call" | custom-call | flops 1 | bytes 1 | tf_op jit(solution)/shard_map/pallas_call | solution.py:241
  44.7 1.3 %collective-permute-start.9 = (f32[2,7,32,512]{3,2,1,0:T(8,128)}, f32[2,7,32,512]{3,2,1,0:T(8,128)S(1)}, u32[]{:S(2)}, u32[]{:S(2)}) collective-permute-start(f32[2,7,32,512]{3,2,1,0:T(8,128)} %get-tuple-element.36), channel_id=1, source_target_pairs={{0,2},{2,0},{1,3},{3,1},{4,6},{6,4},{5,7},{7,5},{8,10},{10,8},{9,1... | collective-permute-start | bytes 2752520 | tf_op jit(solution)/shard_map/ppermute | solution.py:373
  46.0 3.8 %collective-permute-done.5.across = f32[2,9,32,512]{3,2,1,0:T(8,128)S(1)} collective-permute-done((f32[2,9,32,512]{3,2,1,0:T(8,128)}, f32[2,9,32,512]{3,2,1,0:T(8,128)S(1)}, u32[]{:S(2)}, u32[]{:S(2)}) %collective-permute-start.5) | collective-permute-done | bytes 1179680 | tf_op jit(solution)/shard_map/ppermute | solution.py:373
  49.8 0.9 dynamic-slice_bitcast_fusion.1
  50.8 2.1 %collective-permute-start.6 = (f32[9,32,512]{2,1,0:T(8,128)}, f32[9,32,512]{2,1,0:T(8,128)S(1)}, u32[]{:S(2)}, u32[]{:S(2)}) collective-permute-start(f32[9,32,512]{2,1,0:T(8,128)} %dynamic-slice_bitcast_fusion.1), channel_id=1, source_target_pairs={{0,1},{1,0},{2,3},{3,2},{4,5},{5,4},{6,7},{7,6},{8,9},{9,8},{10,11... | collective-permute-start | bytes 1769480 | tf_op jit(solution)/shard_map/ppermute | solution.py:373
  52.8 0.0 collective-permute-start.7
  52.8 2.5 %collective-permute-done.7.refs_1_ = f32[7,32,512]{2,1,0:T(8,128)S(1)} collective-permute-done((f32[7,32,512]{2,1,0:T(8,128)}, f32[7,32,512]{2,1,0:T(8,128)S(1)}, u32[]{:S(2)}, u32[]{:S(2)}) %collective-permute-start.7) | collective-permute-done | bytes 458784 | tf_op jit(solution)/shard_map/ppermute | solution.py:373
  55.3 0.9 copy.18.gain
  56.2 0.0 collective-permute-done.6.diagonal
  56.2 0.8 copy-done.5
  57.1 11.8 %shard_map.93 = (f32[9,32,512]{2,1,0:T(8,128)}, f32[9,32,512]{2,1,0:T(8,128)}, f32[9,32,512]{2,1,0:T(8,128)}, f32[9,32,512]{2,1,0:T(8,128)}) custom-call(s32[2]{0:T(128)} %pad_add_fusion.place, f32[3,32,32,512]{3,2,1,0:T(8,128)} %field.1, f32[2,9,32,512]{3,2,1,0:T(8,128)} %copy-done.2, f32[16,32,512]{2,1,0:T(8,128)} %copy-done.1, f32[9,32,512]{2,1,0:T(8,128)} %copy-done.5, ...), custom_call_target="tpu_custom_call" | custom-call | flops 1 | bytes 1 | tf_op jit(solution)/shard_map/pallas_call | solution.py:241
  68.8 0.4 collective-permute-start.8
  69.3 1.8 %collective-permute-start.11 = (f32[9,32,512]{2,1,0:T(8,128)}, f32[9,32,512]{2,1,0:T(8,128)S(1)}, u32[]{:S(2)}, u32[]{:S(2)}) collective-permute-start(f32[9,32,512]{2,1,0:T(8,128)} %get-tuple-element.37), channel_id=1, source_target_pairs={{0,2},{2,0},{1,3},{3,1},{4,6},{6,4},{5,7},{7,5},{8,10},{10,8},{9,1... | collective-permute-start | bytes 1769480 | tf_op jit(solution)/shard_map/ppermute | solution.py:373
  71.1 0.1 collective-permute-start.12
  71.1 0.9 slice_bitcast_fusion
  72.0 0.4 collective-permute-start.10
  72.4 0.7 divide_multiply_fusion.cot
  73.1 0.6 multiply_add_fusion
  73.7 0.1 collective-permute-done.10.refs_5_
  73.9 0.7 copy-done.4
  74.6 0.1 copy-done.7
  74.7 9.7 %shard_map.94.base = f32[3,32,32,512]{3,2,1,0:T(8,128)} custom-call(s32[2]{0:T(128)} %pad_add_fusion.place, f32[3,32,32,512]{3,2,1,0:T(8,128)} %field.1, f32[2,3,32,512]{3,2,1,0:T(8,128)} %copy-done.8, f32[2,3,32,512]{3,2,1,0:T(8,128)} %collective-permute-done.4.after, f32[32,1,1]{2,1,0:T(1,128)} %get-tuple-element.41.radius, ...), custom_call_target="tpu_custom_call" | custom-call | flops 1 | bytes 1 | tf_op jit(solution)/shard_map/pallas_call | solution.py:308
  84.4 0.4 collective-permute-done.11.own
  84.8 12.7 %collective-permute-done.12.other = f32[9,32,512]{2,1,0:T(8,128)S(1)} collective-permute-done((f32[9,32,512]{2,1,0:T(8,128)}, f32[9,32,512]{2,1,0:T(8,128)S(1)}, u32[]{:S(2)}, u32[]{:S(2)}) %collective-permute-start.12) | collective-permute-done | bytes 589856 | tf_op jit(solution)/shard_map/ppermute | solution.py:373
  97.5 3.0 %shard_map.95 = f32[3,32,32,512]{3,2,1,0:T(8,128)} custom-call(s32[2]{0:T(128)S(1)} %copy-done, f32[3,32,32,512]{3,2,1,0:T(8,128)} %shard_map.94.base, f32[9,32,512]{2,1,0:T(8,128)S(1)} %collective-permute-done.11.own, f32[9,32,512]{2,1,0:T(8,128)S(1)} %collective-permute-done.12.other), custom_call_target="tpu_custom_call", output_to_operand_aliasing={{}: (1, {})} | custom-call | flops 1 | bytes 1 | tf_op jit(solution)/shard_map/pallas_call | solution.py:348
  (22 shorter events, 0.1 us)
Async XLA Ops:
  2.2 25.6 %copy-start.9 = (s32[256]{0:T(256)S(1)}, s32[256]{0:T(256)}, u32[]{:S(2)}) copy-start(s32[256]{0:T(256)} %param.10) | copy-start | bytes 3076
  2.2 22.5 %collective-permute-start = (f32[2,7,32,512]{3,2,1,0:T(8,128)}, f32[2,7,32,512]{3,2,1,0:T(8,128)S(1)}, u32[]{:S(2)}, u32[]{:S(2)}) collective-permute-start(f32[2,7,32,512]{3,2,1,0:T(8,128)} %constant_dynamic-slice_fusion.1), channel_id=1, source_target_pairs={{0,2},{2,0},{1,3},{3,1},{4,6},{6,4},{5,7},{7,5},{8,10},{10,8},{9,1... | collective-permute-start | bytes 2752520 | tf_op jit(solution)/shard_map/ppermute | solution.py:373
  9.0 24.5 %collective-permute-start.1 = (f32[16,32,512]{2,1,0:T(8,128)}, f32[16,32,512]{2,1,0:T(8,128)S(1)}, u32[]{:S(2)}, u32[]{:S(2)}) collective-permute-start(f32[16,32,512]{2,1,0:T(8,128)} %dynamic-slice_bitcast_fusion), channel_id=1, source_target_pairs={{0,1},{1,0},{2,3},{3,2},{4,5},{5,4},{6,7},{7,6},{8,9},{9,8},{10,11... | collective-permute-start | bytes 3145736 | tf_op jit(solution)/shard_map/ppermute | solution.py:373
  12.3 37.5 %collective-permute-start.5 = (f32[2,9,32,512]{3,2,1,0:T(8,128)}, f32[2,9,32,512]{3,2,1,0:T(8,128)S(1)}, u32[]{:S(2)}, u32[]{:S(2)}) collective-permute-start(f32[2,9,32,512]{3,2,1,0:T(8,128)} %constant_dynamic-slice_fusion), channel_id=1, source_target_pairs={{0,2},{2,0},{1,3},{3,1},{4,6},{6,4},{5,7},{7,5},{8,10},{10,8},{9,1... | collective-permute-start | bytes 3538952 | tf_op jit(solution)/shard_map/ppermute | solution.py:373
  12.3 20.3 %collective-permute-start.3 = (f32[2,3,32,512]{3,2,1,0:T(8,128)}, f32[2,3,32,512]{3,2,1,0:T(8,128)S(1)}, u32[]{:S(2)}, u32[]{:S(2)}) collective-permute-start(f32[2,3,32,512]{3,2,1,0:T(8,128)} %get-tuple-element.23), channel_id=1, source_target_pairs={{0,4},{4,8},{8,12},{12,16},{16,20},{20,24},{24,28},{1,5},{5,9},{9,... | collective-permute-start | bytes 1179656 | tf_op jit(solution)/shard_map/ppermute | solution.py:390
  15.7 16.9 %collective-permute-start.4 = (f32[2,3,32,512]{3,2,1,0:T(8,128)}, f32[2,3,32,512]{3,2,1,0:T(8,128)}, u32[]{:S(2)}, u32[]{:S(2)}) collective-permute-start(f32[2,3,32,512]{3,2,1,0:T(8,128)} %get-tuple-element.24), channel_id=1, source_target_pairs={{4,0},{8,4},{12,8},{16,12},{20,16},{24,20},{28,24},{5,1},{9,5},{13... | collective-permute-start | bytes 1179656 | tf_op jit(solution)/shard_map/ppermute | solution.py:390
  24.7 8.9 %copy-start.3 = (f32[2,7,32,512]{3,2,1,0:T(8,128)}, f32[2,7,32,512]{3,2,1,0:T(8,128)S(1)}, u32[]{:S(2)}) copy-start(f32[2,7,32,512]{3,2,1,0:T(8,128)S(1)} %collective-permute-done.across) | copy-start | bytes 2752516
  25.5 8.0 %collective-permute-start.2 = (f32[7,32,512]{2,1,0:T(8,128)}, f32[7,32,512]{2,1,0:T(8,128)}, u32[]{:S(2)}, u32[]{:S(2)}) collective-permute-start(f32[7,32,512]{2,1,0:T(8,128)} %dynamic-slice_bitcast_fusion.2), channel_id=1, source_target_pairs={{0,1},{1,0},{2,3},{3,2},{4,5},{5,4},{6,7},{7,6},{8,9},{9,8},{10,11... | collective-permute-start | bytes 1376264 | tf_op jit(solution)/shard_map/ppermute | solution.py:373
  32.6 36.2 %copy-start.8 = (f32[2,3,32,512]{3,2,1,0:T(8,128)}, f32[2,3,32,512]{3,2,1,0:T(8,128)S(1)}, u32[]{:S(2)}) copy-start(f32[2,3,32,512]{3,2,1,0:T(8,128)S(1)} %collective-permute-done.3.before) | copy-start | bytes 1179652
  33.5 1.0 %copy-start.1 = (f32[16,32,512]{2,1,0:T(8,128)}, f32[16,32,512]{2,1,0:T(8,128)S(1)}, u32[]{:S(2)}) copy-start(f32[16,32,512]{2,1,0:T(8,128)S(1)} %collective-permute-done.1.beside) | copy-start | bytes 3145732
  44.7 26.4 %collective-permute-start.9 = (f32[2,7,32,512]{3,2,1,0:T(8,128)}, f32[2,7,32,512]{3,2,1,0:T(8,128)S(1)}, u32[]{:S(2)}, u32[]{:S(2)}) collective-permute-start(f32[2,7,32,512]{3,2,1,0:T(8,128)} %get-tuple-element.36), channel_id=1, source_target_pairs={{0,2},{2,0},{1,3},{3,1},{4,6},{6,4},{5,7},{7,5},{8,10},{10,8},{9,1... | collective-permute-start | bytes 2752520 | tf_op jit(solution)/shard_map/ppermute | solution.py:373
  49.8 6.4 %copy-start.2 = (f32[2,9,32,512]{3,2,1,0:T(8,128)}, f32[2,9,32,512]{3,2,1,0:T(8,128)S(1)}, u32[]{:S(2)}) copy-start(f32[2,9,32,512]{3,2,1,0:T(8,128)S(1)} %collective-permute-done.5.across) | copy-start | bytes 3538948
  50.8 5.5 %collective-permute-start.6 = (f32[9,32,512]{2,1,0:T(8,128)}, f32[9,32,512]{2,1,0:T(8,128)S(1)}, u32[]{:S(2)}, u32[]{:S(2)}) collective-permute-start(f32[9,32,512]{2,1,0:T(8,128)} %dynamic-slice_bitcast_fusion.1), channel_id=1, source_target_pairs={{0,1},{1,0},{2,3},{3,2},{4,5},{5,4},{6,7},{7,6},{8,9},{9,8},{10,11... | collective-permute-start | bytes 1769480 | tf_op jit(solution)/shard_map/ppermute | solution.py:373
  52.8 2.5 %collective-permute-start.7 = (f32[7,32,512]{2,1,0:T(8,128)}, f32[7,32,512]{2,1,0:T(8,128)S(1)}, u32[]{:S(2)}, u32[]{:S(2)}) collective-permute-start(f32[7,32,512]{2,1,0:T(8,128)} %get-tuple-element.30), channel_id=1, source_target_pairs={{0,1},{1,0},{2,3},{3,2},{4,5},{5,4},{6,7},{7,6},{8,9},{9,8},{10,11... | collective-permute-start | bytes 1376264 | tf_op jit(solution)/shard_map/ppermute | solution.py:373
  55.3 13.5 %copy-start.6 = (f32[7,32,512]{2,1,0:T(8,128)}, f32[7,32,512]{2,1,0:T(8,128)S(1)}, u32[]{:S(2)}) copy-start(f32[7,32,512]{2,1,0:T(8,128)S(1)} %collective-permute-done.7.refs_1_) | copy-start | bytes 1376260
  56.2 0.8 copy-start.5
  68.8 4.9 %collective-permute-start.8 = (f32[9,32,512]{2,1,0:T(8,128)}, f32[9,32,512]{2,1,0:T(8,128)S(1)}, u32[]{:S(2)}, u32[]{:S(2)}) collective-permute-start(f32[9,32,512]{2,1,0:T(8,128)} %get-tuple-element.35), channel_id=1, source_target_pairs={{0,1},{1,0},{2,3},{3,2},{4,5},{5,4},{6,7},{7,6},{8,9},{9,8},{10,11... | collective-permute-start | bytes 1769480 | tf_op jit(solution)/shard_map/ppermute | solution.py:373
  69.3 15.6 %collective-permute-start.11 = (f32[9,32,512]{2,1,0:T(8,128)}, f32[9,32,512]{2,1,0:T(8,128)S(1)}, u32[]{:S(2)}, u32[]{:S(2)}) collective-permute-start(f32[9,32,512]{2,1,0:T(8,128)} %get-tuple-element.37), channel_id=1, source_target_pairs={{0,2},{2,0},{1,3},{3,1},{4,6},{6,4},{5,7},{7,5},{8,10},{10,8},{9,1... | collective-permute-start | bytes 1769480 | tf_op jit(solution)/shard_map/ppermute | solution.py:373
  71.1 26.4 %collective-permute-start.12 = (f32[9,32,512]{2,1,0:T(8,128)}, f32[9,32,512]{2,1,0:T(8,128)S(1)}, u32[]{:S(2)}, u32[]{:S(2)}) collective-permute-start(f32[9,32,512]{2,1,0:T(8,128)} %get-tuple-element.38), channel_id=1, source_target_pairs={{0,3},{3,0},{1,2},{2,1},{4,7},{7,4},{5,6},{6,5},{8,11},{11,8},{9,1... | collective-permute-start | bytes 1769480 | tf_op jit(solution)/shard_map/ppermute | solution.py:373
  72.0 1.8 %collective-permute-start.10 = (f32[7,32,512]{2,1,0:T(8,128)S(1)}, f32[7,32,512]{2,1,0:T(8,128)S(1)}, u32[]{:S(2)}, u32[]{:S(2)}) collective-permute-start(f32[7,32,512]{2,1,0:T(8,128)S(1)} %get-tuple-element.39), channel_id=1, source_target_pairs={{0,1},{1,0},{2,3},{3,2},{4,5},{5,4},{6,7},{7,6},{8,9},{9,8},{10,11... | collective-permute-start | bytes 1376264 | tf_op jit(solution)/shard_map/ppermute | solution.py:373
  73.7 0.8 copy-start.4
  73.9 0.8 copy-start.7
  74.7 22.8 %copy-start = (s32[2]{0:T(128)S(1)}, s32[2]{0:T(128)}, u32[]{:S(2)}) copy-start(s32[2]{0:T(128)} %pad_add_fusion.place) | copy-start | bytes 28

commit v5 on v4

--- a/solution.py
+++ b/solution.py
@@ -135,11 +135,12 @@
     return jnp.stack([j_radial, j_polar, j_azim])
 
 
-CHUNKS = (7, 9)
+CHUNKS = ((7,), (9,))
+LAST = (7, 2)
 TO_Y = [(0, 2), (2, 0), (1, 3), (3, 1)]
 TO_C = [(0, 1), (1, 0), (2, 3), (3, 2)]
 TO_YC = [(0, 3), (3, 0), (1, 2), (2, 1)]
-VMEM = 60 * 1024 * 1024
+VMEM = 52 * 1024 * 1024
 SHORT = pl.CostEstimate(flops=1, bytes_accessed=1, transcendentals=0)
 
 
@@ -172,8 +173,9 @@
     return dot(high, table[0]) + dot(high, table[1]) + dot(low, table[0])
 
 
-def transform_kernel(place, own, across, beside, diagonal, kept, gain, modes, *refs):
-    tables, out_own, out_beside, outs, held, sems = refs[:6], refs[6], refs[7], refs[8:-7], refs[-7:-1], refs[-1]
+def transform_kernel(count, outputs, place, own, beside, diagonal, kept, gain, modes, *refs):
+    across, tables, refs = refs[:count], refs[count : count + 6], refs[count + 6 :]
+    (out_own, out_beside, *outs), held, sems = refs[:outputs], refs[outputs:-1], refs[-1]
     copies = [pltpu.make_async_copy(table, ref, sems.at[i]) for i, (table, ref) in enumerate(zip(tables, held))]
     for copy in copies:
         copy.start()
@@ -182,7 +184,8 @@
     sign_y = (1 - 2 * place[0]).astype(jnp.float32)
     sign_c = (1 - 2 * place[1]).astype(jnp.float32)
     first = place[1] == 0
-    a, b, c, d = (ref[...].reshape(rows, quarter) for ref in (own, across, beside, diagonal))
+    a, c, d = (ref[...].reshape(rows, quarter) for ref in (own, beside, diagonal))
+    b = jnp.concatenate([ref[...].reshape(-1, quarter) for ref in across], axis=0)
     near, far = a + b, c + d
     near_odd, far_odd = sign_y * (a - b), sign_y * (c - d)
     odd = jnp.concatenate([jnp.where(first, near_odd, far_odd), jnp.where(first, far_odd, near_odd)], axis=1)
@@ -209,10 +212,14 @@
     if len(outs) == 1:
         outs[0][0], outs[0][1] = across, diagonal
     else:
-        outs[0][...], outs[1][...] = across, diagonal
-
-
-def transform(place, magnetic, start, both, beside, diagonal, row_kept, row_gain, tables, paired):
+        outs[0][...] = across
+        at = 0
+        for out in outs[1:]:
+            out[...] = diagonal[at : at + out.shape[0]]
+            at += out.shape[0]
+
+
+def transform(place, magnetic, start, parts, beside, diagonal, row_kept, row_gain, tables, cuts):
     depth, th_dev, quarter = diagonal.shape
     zero, two, odd, mode_ids = tables
     whole = pl.BlockSpec(memory_space=pltpu.VMEM)
@@ -220,32 +227,31 @@
     half = magnetic.shape[1] // 2
     part = (pl.Element(1), pl.Element(depth), pl.Element(th_dev), pl.Element(quarter))
     row_block = pl.BlockSpec((pl.Element(rows), pl.Element(1)), lambda i, p: (start * th_dev, 0))
+    shape = (depth, th_dev, quarter)
+    shapes = [shape, shape, (2,) + shape] if cuts is None else [shape] * 3 + [(cut, th_dev, quarter) for cut in cuts]
     grid_spec = pltpu.PrefetchScalarGridSpec(
         num_scalar_prefetch=1,
         grid=(1,),
         in_specs=[
             pl.BlockSpec(part, lambda i, p: (p[1], p[0] * half + start, 0, 0)),
-            pl.BlockSpec((None, depth, th_dev, quarter), lambda i, p: (p[1], 0, 0, 0)),
             pl.BlockSpec(part[1:], lambda i, p: (start, 0, 0)),
             whole,
             row_block,
             row_block,
             whole,
         ]
+        + [pl.BlockSpec((None,) + value.shape[1:], lambda i, p: (p[1], 0, 0, 0)) for value in parts]
         + [pl.BlockSpec(memory_space=pl.ANY)] * 6,
-        out_specs=[whole] * (3 if paired else 4),
+        out_specs=[whole] * len(shapes),
         scratch_shapes=[pltpu.VMEM(t.shape, jnp.bfloat16) for t in (*zero, *two, *odd)] + [pltpu.SemaphoreType.DMA((6,))],
     )
-    shape = (depth, th_dev, quarter)
-    shapes = [shape, shape, (2,) + shape] if paired else [shape] * 4
-    outs = pl.pallas_call(
-        transform_kernel,
+    return pl.pallas_call(
+        functools.partial(transform_kernel, len(parts), len(shapes)),
         grid_spec=grid_spec,
         out_shape=[jax.ShapeDtypeStruct(shape, jnp.float32) for shape in shapes],
         compiler_params=pltpu.CompilerParams(vmem_limit_bytes=VMEM),
         cost_estimate=SHORT,
-    )(place, magnetic, both, beside, diagonal, row_kept, row_gain, mode_ids, *zero, *two, *odd)
-    return (*outs, None) if paired else outs
+    )(place, magnetic, beside, diagonal, row_kept, row_gain, mode_ids, *parts, *zero, *two, *odd)
 
 
 def edge_rows(magnetic):
@@ -267,6 +273,35 @@
         compiler_params=pltpu.CompilerParams(vmem_limit_bytes=VMEM),
         cost_estimate=SHORT,
     )(magnetic, magnetic)
+
+
+def copy_part(place, magnetic, start, depth):
+    radii, th_dev, ph_dev = magnetic.shape[1:]
+
+    def kernel(place, magnetic, out, sems):
+        first = (1 - place[0]) * (radii // 2) + start
+        copies = [
+            pltpu.make_async_copy(magnetic.at[field, pl.ds(first, depth)], out.at[field], sems.at[field])
+            for field in range(2)
+        ]
+        for copy in copies:
+            copy.start()
+        for copy in copies:
+            copy.wait()
+
+    return pl.pallas_call(
+        kernel,
+        grid_spec=pltpu.PrefetchScalarGridSpec(
+            num_scalar_prefetch=1,
+            grid=(1,),
+            in_specs=[pl.BlockSpec(memory_space=pl.ANY)],
+            out_specs=pl.BlockSpec(memory_space=pltpu.VMEM),
+            scratch_shapes=[pltpu.SemaphoreType.DMA((2,))],
+        ),
+        out_shape=jax.ShapeDtypeStruct((2, depth, th_dev, ph_dev), jnp.float32),
+        compiler_params=pltpu.CompilerParams(vmem_limit_bytes=VMEM),
+        cost_estimate=SHORT,
+    )(place, magnetic)
 
 
 def local_part(place, magnetic, before, after, radius, inv_radius, cot, groups):
@@ -331,30 +366,58 @@
     )(place, magnetic, before, after, radius, inv_radius, cot, *azims)
 
 
-def add_pair(place, current, from_y, from_yc, start):
-    depth, th_dev, ph_dev = from_y.shape
+def add_one(place, current, azim, own_field, start):
+    depth, th_dev, ph_dev = azim.shape
     half = current.shape[1] // 2
-    whole = pl.BlockSpec(memory_space=pltpu.VMEM)
+    part = lambda p: 1 - p[1] if own_field else p[1]
     block = pl.BlockSpec(
-        (pl.Element(2), pl.Element(depth), pl.Element(th_dev), pl.Element(ph_dev)),
-        lambda i, p: (0, (1 - p[0]) * half + start, 0, 0),
+        (pl.Element(1), pl.Element(depth), pl.Element(th_dev), pl.Element(ph_dev)),
+        lambda i, p: (part(p), (1 - p[0]) * half + start, 0, 0),
     )
 
-    def kernel(place, base, own, other, out):
-        part = 1 - place[1]
-        out[part] = base[part] + own[...]
-        out[1 - part] = base[1 - part] + other[...]
+    def kernel(place, base, azim, out):
+        out[0] = base[0] + azim[...]
 
     return pl.pallas_call(
         kernel,
         grid_spec=pltpu.PrefetchScalarGridSpec(
-            num_scalar_prefetch=1, grid=(1,), in_specs=[block, whole, whole], out_specs=block
+            num_scalar_prefetch=1,
+            grid=(1,),
+            in_specs=[block, pl.BlockSpec(memory_space=pltpu.VMEM)],
+            out_specs=block,
         ),
         out_shape=jax.ShapeDtypeStruct(current.shape, jnp.float32),
         input_output_aliases={1: 0},
         compiler_params=pltpu.CompilerParams(vmem_limit_bytes=VMEM // 6),
         cost_estimate=SHORT,
-    )(place, current, from_y, from_yc)
+    )(place, current, azim)
+
+
+def put_sum(place, current, base, azim, start):
+    depth = azim.shape[0]
+    half = current.shape[1] // 2
+    whole = pl.BlockSpec(memory_space=pltpu.VMEM)
+
+    def kernel(place, current, base, azim, out, total, sem):
+        total[...] = base[...] + azim[...]
+        copy = pltpu.make_async_copy(total, out.at[place[1], pl.ds((1 - place[0]) * half + start, depth)], sem)
+        copy.start()
+        copy.wait()
+
+    return pl.pallas_call(
+        kernel,
+        grid_spec=pltpu.PrefetchScalarGridSpec(
+            num_scalar_prefetch=1,
+            grid=(1,),
+            in_specs=[pl.BlockSpec(memory_space=pl.ANY), whole, whole],
+            out_specs=pl.BlockSpec(memory_space=pl.ANY),
+            scratch_shapes=[pltpu.VMEM(azim.shape, jnp.float32), pltpu.SemaphoreType.DMA],
+        ),
+        out_shape=jax.ShapeDtypeStruct(current.shape, jnp.float32),
+        input_output_aliases={1: 0},
+        compiler_params=pltpu.CompilerParams(vmem_limit_bytes=VMEM // 6),
+        cost_estimate=SHORT,
+    )(place, current, base, azim)
 
 
 def after(first, *then):
@@ -364,8 +427,10 @@
 def on_four(magnetic, kept_modes):
     radii, th_dev, ph_dev = (magnetic.shape[1], magnetic.shape[2], magnetic.shape[3])
     half = radii // 2
-    total = sum(CHUNKS)
-    depths = [half * part // total for part in CHUNKS]
+    unit = half // sum(map(sum, CHUNKS))
+    pieces = [[unit * piece for piece in chunk] for chunk in CHUNKS]
+    depths = [sum(chunk) for chunk in pieces]
+    last_cuts = [unit * piece for piece in LAST]
     starts = [sum(depths[:k]) for k in range(len(depths))]
     index = lax.axis_index("azim")
     y, c = index // 2, index % 2
@@ -377,10 +442,16 @@
 
     arrived = []
     source = magnetic
-    for k, depth in enumerate(depths):
-        both = lax.dynamic_slice(source, (0, (1 - y) * half + starts[k], 0, 0), (2, depth, th_dev, ph_dev))
-        (source,) = after(both, source)
-        arrived.append(send(both, TO_Y))
+    for k, chunk in enumerate(pieces):
+        arrived.append([])
+        for i, depth in enumerate(chunk):
+            at = (1 - y) * half + starts[k] + sum(chunk[:i])
+            if k == 0:
+                both = copy_part(place, source, starts[k] + sum(chunk[:i]), depth)
+            else:
+                both = lax.dynamic_slice(source, (0, at, 0, 0), (2, depth, th_dev, ph_dev))
+            (source,) = after(both, source)
+            arrived[k].append(send(both, TO_Y))
         if k == 0:
             lat_size = lax.axis_size("lat")
             up = [(i, i + 1) for i in range(lat_size - 1)]
@@ -405,26 +476,34 @@
 
     tables = mode_tables(4 * ph_dev)
     mine, from_c, returned = [], [], []
-    for k, (start, depth) in enumerate(zip(starts, depths)):
-        both = arrived[k]
+    for k, start in enumerate(starts):
+        parts = arrived[k]
         if k > 0:
-            (both,) = after(mine[-1], both)
+            parts = after(mine[-1], *parts)
         (row_gain,) = after(from_c[-1] if k > 0 else (north, south), row_gain)
-        diagonal = send(cut(both, 1 - c, 0, depth), TO_C)
-        out, to_c, to_y, to_yc = transform(
-            place, magnetic, start, both, beside, diagonal, row_kept, row_gain, tables, k + 1 < len(depths)
+        diagonal = send(jnp.concatenate([cut(part, 1 - c, 0, part.shape[1]) for part in parts]), TO_C)
+        cuts = None if k + 1 < len(starts) else last_cuts
+        out, to_c, to_y, *to_yc = transform(
+            place, magnetic, start, parts, beside, diagonal, row_kept, row_gain, tables, cuts
         )
         mine.append(out)
         from_c.append(send(to_c, TO_C))
         returned.append(send(to_y, TO_Y))
-    final = returned.pop(), send(to_yc, TO_YC)
+    final = [(returned.pop(), True, starts[-1])]
+    for i, value in enumerate(to_yc):
+        final.append((send(value, TO_YC), False, starts[-1] + sum(last_cuts[:i])))
 
     groups = [(own, crossed, True, start) for own, crossed, start in zip(mine, from_c, starts)]
     for value, start in zip(returned, starts):
         groups.append((value[0], send(value[1], TO_C), False, start))
     north, south = after(mine[-1], north, south)
     current = local_part(place, magnetic, north, south, radius, inv_radius, cot, groups)
-    return add_pair(place, current, *final, starts[-1])
+    azim, _, start = final[-1]
+    base = cut(current, c, (1 - y) * half + start, azim.shape[0])
+    (current,) = after(base, current)
+    for value, own_field, at in final[:-1]:
+        current = add_one(place, current, value, own_field, at)
+    return put_sum(place, current, base, azim, start)
 
 
 def solution(mesh):
@@ -432,7 +511,7 @@
 
     def run(magnetic, kept_modes):
         radii, ph_dev = magnetic.shape[1], magnetic.shape[3]
-        four = lax.axis_size("azim") == 4 and radii % (2 * sum(CHUNKS)) == 0 and ph_dev % 256 == 0
+        four = lax.axis_size("azim") == 4 and radii % (2 * sum(map(sum, CHUNKS))) == 0 and ph_dev % 256 == 0
         return (on_four if four else on_device)(magnetic, kept_modes)
 
     return jax.shard_map(

time: 101 us -> 99.6 us (0.986)
  local copies, waits for them, and re-layouts: 15.2 us -> 12.9 us
  Pallas kernels: 37 us -> 39.3 us
  starting transfers between devices: 15.7 us -> 17.6 us
  other arithmetic: 2.18 us -> 0.39 us
  waiting for transfers between devices: 30.2 us -> 28.6 us
    pallas_call x3 -> x6, Pallas kernels: 24.9 us -> 28.9 us  [the longest x2 21.1 us: transform(): pl.pallas_call(functools.partial(transform_kernel, len(parts), len(shapes...]
    ppermute x11 -> x12, waiting for transfers between devices: 27.1 us -> 24.9 us  [on_four(): send = lambda value, pairs: lax.ppermute(value, 'azim', pairs)]
    dynamic_slice x2 -> x1, local copies, waits for them, and re-layouts: 4.6 us -> 2.41 us  [on_four(): both = lax.dynamic_slice(source, (0, at, 0, 0), (2, depth, th_dev, ph_dev))]
    ppermute x11 -> x12, starting transfers between devices: 11 us -> 12.9 us  [on_four(): send = lambda value, pairs: lax.ppermute(value, 'azim', pairs)]
    squeeze x3 -> x4, local copies, waits for them, and re-layouts: 4.13 us -> 6 us  [cut(): lax.dynamic_slice(source, (field, start, 0, 0), (1, length, th_dev, ph_dev))]
    optimization_barrier x2, local copies, waits for them, and re-layouts: 1.77 us -> 0.29 us  [after(): return lax.optimization_barrier((first, then))[1]]
    squeeze x1, local copies, waits for them, and re-layouts: 0.89 us -> 2.15 us  [on_four(): groups.append((value[0], send(value[1], TO_C), False, start))]
    unnamed x20 -> x10, local copies, waits for them, and re-layouts: 2.68 us -> 1.65 us
  transfers between devices with their start and end apart: 13 -> 14, of which waited for: 7 -> 6; matrix products, arithmetic and copies ran while one was open for 12% -> 12% of each run, Pallas kernels for 34% -> 37%
where the time goes in v5:
time: 99.6 us; the launch traced here: 98.9 us
  Pallas kernels  39.3 us (39%)
  waiting for transfers between devices  28.6 us (29%)
  starting transfers between devices  17.6 us (18%)
  local copies, waits for them, and re-layouts  12.9 us (13%)
    ppermute x12, waiting for transfers between devices, on_four(): send = lambda value, pairs: lax.ppermute(value, 'azim', pairs)  24.9 us
    pallas_call x2, Pallas kernels, transform(): pl.pallas_call(functools.partial(transform_kernel, len(parts), len(shapes...  21.1 us
    ppermute x12, starting transfers between devices, on_four(): send = lambda value, pairs: lax.ppermute(value, 'azim', pairs)  12.9 us
    pallas_call x1, Pallas kernels, local_part(): pl.pallas_call(kernel, grid_spec=pltpu.PrefetchScalarGridSpec(num_scalar_...  8.78 us
    squeeze x4, local copies, waits for them, and re-layouts, cut(): lax.dynamic_slice(source, (field, start, 0, 0), (1, length, th_dev, ph_dev))  6 us
    pallas_call x2, Pallas kernels, add_one(): pl.pallas_call(kernel, grid_spec=pltpu.PrefetchScalarGridSpec(num_scalar_...  4.86 us
    ppermute x1, waiting for transfers between devices, on_four(): lax.ppermute(last, 'lat', up)  3.66 us
    ppermute x1, starting transfers between devices, on_four(): lax.ppermute(last, 'lat', up)  3.35 us
  transfers between devices with their start and end apart: 14, of which 6 were waited for; matrix products, arithmetic and copies ran while one was open for 12% of the time, Pallas kernels for 37%

profile of v5, /device:TPU:1, one launch (start us, length us, event | category | flops | bytes accessed | tf_op | source)
XLA Modules:
  0.0 98.9 jit_solution(7617203758305185062)
XLA Ops:
  0.0 0.1 pad_add_fusion.place
  0.1 1.7 %shard_map.91 = f32[2,7,32,512]{3,2,1,0:T(8,128)S(1)} custom-call(s32[2]{0:T(128)S(1)} %pad_add_fusion.place, f32[3,32,32,512]{3,2,1,0:T(8,128)} %field.1), custom_call_target="tpu_custom_call" | custom-call | flops 1 | bytes 1 | tf_op jit(solution)/shard_map/pallas_call | solution.py:292
  1.8 0.0 copy-start.4
  1.8 0.0 copy-start.1
  1.8 2.1 %collective-permute-start.1 = (f32[2,7,32,512]{3,2,1,0:T(8,128)S(1)}, f32[2,7,32,512]{3,2,1,0:T(8,128)S(1)}, u32[]{:S(2)}, u32[]{:S(2)}) collective-permute-start(f32[2,7,32,512]{3,2,1,0:T(8,128)S(1)} %shard_map.91), channel_id=1, source_target_pairs={{0,2},{2,0},{1,3},{3,1},{4,6},{6,4},{5,7},{7,5},{8,10},{10,8},{9,1... | collective-permute-start | bytes 2752520 | tf_op jit(solution)/shard_map/ppermute | solution.py:438
  4.0 1.6 %shard_map.92 = (f32[2,3,32,512]{3,2,1,0:T(8,128)S(1)}, f32[2,3,32,512]{3,2,1,0:T(8,128)S(1)}) custom-call(f32[3,32,32,512]{3,2,1,0:T(8,128)} %field.1, f32[3,32,32,512]{3,2,1,0:T(8,128)} %field.1), custom_call_target="tpu_custom_call" | custom-call | flops 1 | bytes 1 | tf_op jit(solution)/shard_map/pallas_call | solution.py:267
  5.6 2.3 %dynamic-slice_bitcast_fusion = f32[16,32,512]{2,1,0:T(8,128)} fusion(f32[3,32,32,512]{3,2,1,0:T(8,128)} %field.1, s32[]{:T(128)S(6)} %select_n.36, s32[]{:T(128)S(6)} %select_n.37), kind=kLoop, calls=%fused_computation | loop fusion | bytes 2097160 | tf_op jit(solution)/shard_map/squeeze | solution.py:441
  7.9 1.0 collective-permute-start
  8.9 2.4 %constant_dynamic-slice_fusion = f32[2,9,32,512]{3,2,1,0:T(8,128)} fusion(f32[3,32,32,512]{3,2,1,0:T(8,128)} %field.1, s32[]{:T(128)S(6)} %select_n.40), kind=kLoop, calls=%fused_computation.10 | loop fusion | bytes 2359300 | tf_op jit(solution)/shard_map/dynamic_slice | solution.py:452
  11.3 0.0 collective-permute-start.5
  11.3 3.4 %collective-permute-start.3 = (f32[2,3,32,512]{3,2,1,0:T(8,128)S(1)}, f32[2,3,32,512]{3,2,1,0:T(8,128)S(1)}, u32[]{:S(2)}, u32[]{:S(2)}) collective-permute-start(f32[2,3,32,512]{3,2,1,0:T(8,128)S(1)} %get-tuple-element.25), channel_id=1, source_target_pairs={{0,4},{4,8},{8,12},{12,16},{16,20},{20,24},{24,28},{1,5},{5,9},{9,... | collective-permute-start | bytes 1179656 | tf_op jit(solution)/shard_map/ppermute | solution.py:461
  14.7 1.3 %collective-permute-start.4 = (f32[2,3,32,512]{3,2,1,0:T(8,128)S(1)}, f32[2,3,32,512]{3,2,1,0:T(8,128)S(1)}, u32[]{:S(2)}, u32[]{:S(2)}) collective-permute-start(f32[2,3,32,512]{3,2,1,0:T(8,128)S(1)} %get-tuple-element.26), channel_id=1, source_target_pairs={{4,0},{8,4},{12,8},{16,12},{20,16},{24,20},{28,24},{5,1},{9,5},{13... | collective-permute-start | bytes 1179656 | tf_op jit(solution)/shard_map/ppermute | solution.py:461
  16.0 8.1 %collective-permute-done.1.refs_0_ = f32[2,7,32,512]{3,2,1,0:T(8,128)S(1)} collective-permute-done((f32[2,7,32,512]{3,2,1,0:T(8,128)S(1)}, f32[2,7,32,512]{3,2,1,0:T(8,128)S(1)}, u32[]{:S(2)}, u32[]{:S(2)}) %collective-permute-start.1) | collective-permute-done | bytes 917536 | tf_op jit(solution)/shard_map/ppermute | solution.py:438
  24.0 0.8 dynamic-slice_bitcast_fusion.2
  24.9 2.1 %collective-permute-start.2 = (f32[7,32,512]{2,1,0:T(8,128)}, f32[7,32,512]{2,1,0:T(8,128)S(1)}, u32[]{:S(2)}, u32[]{:S(2)}) collective-permute-start(f32[7,32,512]{2,1,0:T(8,128)} %dynamic-slice_bitcast_fusion.2), channel_id=1, source_target_pairs={{0,1},{1,0},{2,3},{3,2},{4,5},{5,4},{6,7},{7,6},{8,9},{9,8},{10,11... | collective-permute-start | bytes 1376264 | tf_op jit(solution)/shard_map/ppermute | solution.py:438
  27.0 0.1 dynamic-slice
  27.1 0.1 broadcast_multiply_fusion
  27.2 0.1 reshape.73
  27.2 0.1 dynamic-slice_convert_fusion
  27.3 0.3 reshape.74.kept
  27.6 3.7 %collective-permute-done.3.before = f32[2,3,32,512]{3,2,1,0:T(8,128)S(1)} collective-permute-done((f32[2,3,32,512]{3,2,1,0:T(8,128)S(1)}, f32[2,3,32,512]{3,2,1,0:T(8,128)S(1)}, u32[]{:S(2)}, u32[]{:S(2)}) %collective-permute-start.3) | collective-permute-done | bytes 393248 | tf_op jit(solution)/shard_map/ppermute | solution.py:461
  31.3 0.0 collective-permute-done.4.after
  31.3 0.1 copy.18.gain
  31.4 0.0 collective-permute-done.beside
  31.5 9.7 %shard_map.93 = (f32[7,32,512]{2,1,0:T(8,128)S(1)}, f32[7,32,512]{2,1,0:T(8,128)S(1)}, f32[2,7,32,512]{3,2,1,0:T(8,128)}) custom-call(s32[2]{0:T(128)S(1)} %pad_add_fusion.place, f32[3,32,32,512]{3,2,1,0:T(8,128)} %field.1, f32[16,32,512]{2,1,0:T(8,128)} %collective-permute-done.beside, f32[7,32,512]{2,1,0:T(8,128)S(1)} %collective-permute-done.2.diagonal, ...), custom_call_target="tpu_custom_call" | custom-call | flops 1 | bytes 1 | tf_op jit(solution)/shard_map/pallas_call | solution.py:248
  41.2 1.3 %collective-permute-start.9 = (f32[2,7,32,512]{3,2,1,0:T(8,128)}, f32[2,7,32,512]{3,2,1,0:T(8,128)}, u32[]{:S(2)}, u32[]{:S(2)}) collective-permute-start(f32[2,7,32,512]{3,2,1,0:T(8,128)} %get-tuple-element.38), channel_id=1, source_target_pairs={{0,2},{2,0},{1,3},{3,1},{4,6},{6,4},{5,7},{7,5},{8,10},{10,8},{9,1... | collective-permute-start | bytes 2752520 | tf_op jit(solution)/shard_map/ppermute | solution.py:438
  42.5 7.0 %collective-permute-done.5.refs_0_ = f32[2,9,32,512]{3,2,1,0:T(8,128)} collective-permute-done((f32[2,9,32,512]{3,2,1,0:T(8,128)}, f32[2,9,32,512]{3,2,1,0:T(8,128)}, u32[]{:S(2)}, u32[]{:S(2)}) %collective-permute-start.5) | collective-permute-done | bytes 1179680 | tf_op jit(solution)/shard_map/ppermute | solution.py:438
  49.4 1.9 %dynamic-slice_bitcast_fusion.1 = f32[9,32,512]{2,1,0:T(8,128)} fusion(f32[2,9,32,512]{3,2,1,0:T(8,128)} %collective-permute-done.5.refs_0_, s32[]{:T(128)S(6)} %select_n.38), kind=kLoop, calls=%fused_computation.1 | loop fusion | bytes 1179652 | tf_op jit(solution)/shard_map/squeeze | solution.py:441
  51.3 2.1 %collective-permute-start.6 = (f32[9,32,512]{2,1,0:T(8,128)}, f32[9,32,512]{2,1,0:T(8,128)S(1)}, u32[]{:S(2)}, u32[]{:S(2)}) collective-permute-start(f32[9,32,512]{2,1,0:T(8,128)} %dynamic-slice_bitcast_fusion.1), channel_id=1, source_target_pairs={{0,1},{1,0},{2,3},{3,2},{4,5},{5,4},{6,7},{7,6},{8,9},{9,8},{10,11... | collective-permute-start | bytes 1769480 | tf_op jit(solution)/shard_map/ppermute | solution.py:438
  53.4 2.1 %collective-permute-done.7.refs_1_ = f32[7,32,512]{2,1,0:T(8,128)S(1)} collective-permute-done((f32[7,32,512]{2,1,0:T(8,128)S(1)}, f32[7,32,512]{2,1,0:T(8,128)S(1)}, u32[]{:S(2)}, u32[]{:S(2)}) %collective-permute-start.7) | collective-permute-done | bytes 458784 | tf_op jit(solution)/shard_map/ppermute | solution.py:438
  55.5 0.1 copy.20.gain
  55.7 0.2 collective-permute-done.6.diagonal
  55.9 0.8 copy-done.3
  56.7 11.4 %shard_map.94 = (f32[9,32,512]{2,1,0:T(8,128)S(1)}, f32[9,32,512]{2,1,0:T(8,128)}, f32[9,32,512]{2,1,0:T(8,128)}, f32[7,32,512]{2,1,0:T(8,128)S(1)}, f32[2,32,512]{2,1,0:T(8,128)S(1)}) custom-call(s32[2]{0:T(128)S(1)} %pad_add_fusion.place, f32[3,32,32,512]{3,2,1,0:T(8,128)} %field.1, f32[16,32,512]{2,1,0:T(8,128)} %collective-permute-done.beside, ...), custom_call_target="tpu_custom_call" | custom-call | flops 1 | bytes 1 | tf_op jit(solution)/shard_map/pallas_call | solution.py:248
  68.1 0.8 copy-done
  68.9 0.4 collective-permute-start.8
  69.3 1.8 %collective-permute-start.11 = (f32[9,32,512]{2,1,0:T(8,128)}, f32[9,32,512]{2,1,0:T(8,128)S(1)}, u32[]{:S(2)}, u32[]{:S(2)}) collective-permute-start(f32[9,32,512]{2,1,0:T(8,128)} %get-tuple-element.40), channel_id=1, source_target_pairs={{0,2},{2,0},{1,3},{3,1},{4,6},{6,4},{5,7},{7,5},{8,10},{10,8},{9,1... | collective-permute-start | bytes 1769480 | tf_op jit(solution)/shard_map/ppermute | solution.py:438
  71.1 2.2 %slice_bitcast_fusion = (f32[7,32,512]{2,1,0:T(8,128)}, f32[7,32,512]{2,1,0:T(8,128)}) fusion(f32[2,7,32,512]{3,2,1,0:T(8,128)} %collective-permute-done.9), kind=kLoop, calls=%fused_computation.2 | loop fusion | bytes 1835008 | tf_op jit(solution)/shard_map/squeeze | solution.py:498
  73.3 0.4 collective-permute-start.10
  73.7 0.1 collective-permute-start.12
  73.8 1.7 %collective-permute-start.13 = (f32[2,32,512]{2,1,0:T(8,128)S(1)}, f32[2,32,512]{2,1,0:T(8,128)S(1)}, u32[]{:S(2)}, u32[]{:S(2)}) collective-permute-start(f32[2,32,512]{2,1,0:T(8,128)S(1)} %get-tuple-element.42), channel_id=1, source_target_pairs={{0,3},{3,0},{1,2},{2,1},{4,7},{7,4},{5,6},{6,5},{8,11},{11,8},{9,1... | collective-permute-start | bytes 393224 | tf_op jit(solution)/shard_map/ppermute | solution.py:438
  75.5 0.1 divide_multiply_fusion.cot
  75.6 8.8 %shard_map.95.base = f32[3,32,32,512]{3,2,1,0:T(8,128)} custom-call(s32[2]{0:T(128)S(1)} %pad_add_fusion.place, f32[3,32,32,512]{3,2,1,0:T(8,128)} %field.1, f32[2,3,32,512]{3,2,1,0:T(8,128)S(1)} %collective-permute-done.3.before, f32[2,3,32,512]{3,2,1,0:T(8,128)S(1)} %collective-permute-done.4.after, f32[32,1,1]{2,1,0:T(1,128)S(1)} %get-tuple-element.45.radius, ...), custom_call_target="tpu_custom_call" | custom-call | flops 1 | bytes 1 | tf_op jit(solution)/shard_map/pallas_call | solution.py:343
  84.4 0.9 dynamic-slice_bitcast_fusion.3.base
  85.4 2.5 %shard_map.96.base = f32[3,32,32,512]{3,2,1,0:T(8,128)} custom-call(s32[2]{0:T(128)S(1)} %pad_add_fusion.place, f32[3,32,32,512]{3,2,1,0:T(8,128)} %shard_map.95.base, f32[9,32,512]{2,1,0:T(8,128)S(1)} %collective-permute-done.11.azim), custom_call_target="tpu_custom_call", output_to_operand_aliasing={{}: (1, {})} | custom-call | flops 1 | bytes 1 | tf_op jit(solution)/shard_map/pallas_call | solution.py:381
  87.8 7.5 %collective-permute-done.12.azim = f32[7,32,512]{2,1,0:T(8,128)S(1)} collective-permute-done((f32[7,32,512]{2,1,0:T(8,128)S(1)}, f32[7,32,512]{2,1,0:T(8,128)S(1)}, u32[]{:S(2)}, u32[]{:S(2)}) %collective-permute-start.12) | collective-permute-done | bytes 458784 | tf_op jit(solution)/shard_map/ppermute | solution.py:438
  95.3 2.4 %shard_map.97.current = f32[3,32,32,512]{3,2,1,0:T(8,128)} custom-call(s32[2]{0:T(128)S(1)} %pad_add_fusion.place, f32[3,32,32,512]{3,2,1,0:T(8,128)} %shard_map.96.base, f32[7,32,512]{2,1,0:T(8,128)S(1)} %collective-permute-done.12.azim), custom_call_target="tpu_custom_call", output_to_operand_aliasing={{}: (1, {})} | custom-call | flops 1 | bytes 1 | tf_op jit(solution)/shard_map/pallas_call | solution.py:381
  97.7 1.2 %shard_map.98 = f32[3,32,32,512]{3,2,1,0:T(8,128)} custom-call(s32[2]{0:T(128)S(1)} %pad_add_fusion.place, f32[3,32,32,512]{3,2,1,0:T(8,128)} %shard_map.97.current, f32[2,32,512]{2,1,0:T(8,128)S(1)} %dynamic-slice_bitcast_fusion.3.base, f32[2,32,512]{2,1,0:T(8,128)S(1)} %collective-permute-done.13.azim), custom_call_target="tpu_custom_call", output_to_operand_aliasing={{}: (1, {})} | custom-call | flops 1 | bytes 1 | tf_op jit(solution)/shard_map/pallas_call | solution.py:407
  (17 shorter events, 0.1 us)
Async XLA Ops:
  1.8 25.4 %copy-start.4 = (s32[256]{0:T(256)S(1)}, s32[256]{0:T(256)}, u32[]{:S(2)}) copy-start(s32[256]{0:T(256)} %param.10) | copy-start | bytes 3076
  1.8 29.6 %copy-start.1 = (f32[1,2048]{1,0:T(1,128)S(1)}, f32[1,2048]{1,0:T(1,128)}, u32[]{:S(2)}) copy-start(f32[1,2048]{1,0:T(1,128)} %constant.85.clone.modes) | copy-start | bytes 24580
  1.8 22.2 %collective-permute-start.1 = (f32[2,7,32,512]{3,2,1,0:T(8,128)S(1)}, f32[2,7,32,512]{3,2,1,0:T(8,128)S(1)}, u32[]{:S(2)}, u32[]{:S(2)}) collective-permute-start(f32[2,7,32,512]{3,2,1,0:T(8,128)S(1)} %shard_map.91), channel_id=1, source_target_pairs={{0,2},{2,0},{1,3},{3,1},{4,6},{6,4},{5,7},{7,5},{8,10},{10,8},{9,1... | collective-permute-start | bytes 2752520 | tf_op jit(solution)/shard_map/ppermute | solution.py:438
  7.9 23.5 %collective-permute-start = (f32[16,32,512]{2,1,0:T(8,128)}, f32[16,32,512]{2,1,0:T(8,128)}, u32[]{:S(2)}, u32[]{:S(2)}) collective-permute-start(f32[16,32,512]{2,1,0:T(8,128)} %dynamic-slice_bitcast_fusion), channel_id=1, source_target_pairs={{0,1},{1,0},{2,3},{3,2},{4,5},{5,4},{6,7},{7,6},{8,9},{9,8},{10,11... | collective-permute-start | bytes 3145736 | tf_op jit(solution)/shard_map/ppermute | solution.py:438
  11.3 38.1 %collective-permute-start.5 = (f32[2,9,32,512]{3,2,1,0:T(8,128)}, f32[2,9,32,512]{3,2,1,0:T(8,128)}, u32[]{:S(2)}, u32[]{:S(2)}) collective-permute-start(f32[2,9,32,512]{3,2,1,0:T(8,128)} %constant_dynamic-slice_fusion), channel_id=1, source_target_pairs={{0,2},{2,0},{1,3},{3,1},{4,6},{6,4},{5,7},{7,5},{8,10},{10,8},{9,1... | collective-permute-start | bytes 3538952 | tf_op jit(solution)/shard_map/ppermute | solution.py:438
  11.3 20.0 %collective-permute-start.3 = (f32[2,3,32,512]{3,2,1,0:T(8,128)S(1)}, f32[2,3,32,512]{3,2,1,0:T(8,128)S(1)}, u32[]{:S(2)}, u32[]{:S(2)}) collective-permute-start(f32[2,3,32,512]{3,2,1,0:T(8,128)S(1)} %get-tuple-element.25), channel_id=1, source_target_pairs={{0,4},{4,8},{8,12},{12,16},{16,20},{20,24},{24,28},{1,5},{5,9},{9,... | collective-permute-start | bytes 1179656 | tf_op jit(solution)/shard_map/ppermute | solution.py:461
  14.7 16.6 %collective-permute-start.4 = (f32[2,3,32,512]{3,2,1,0:T(8,128)S(1)}, f32[2,3,32,512]{3,2,1,0:T(8,128)S(1)}, u32[]{:S(2)}, u32[]{:S(2)}) collective-permute-start(f32[2,3,32,512]{3,2,1,0:T(8,128)S(1)} %get-tuple-element.26), channel_id=1, source_target_pairs={{4,0},{8,4},{12,8},{16,12},{20,16},{24,20},{28,24},{5,1},{9,5},{13... | collective-permute-start | bytes 1179656 | tf_op jit(solution)/shard_map/ppermute | solution.py:461
  24.0 7.4 %copy-start.2 = (f32[2,7,32,512]{3,2,1,0:T(8,128)}, f32[2,7,32,512]{3,2,1,0:T(8,128)S(1)}, u32[]{:S(2)}) copy-start(f32[2,7,32,512]{3,2,1,0:T(8,128)S(1)} %collective-permute-done.1.refs_0_) | copy-start | bytes 2752516
  24.9 6.5 %collective-permute-start.2 = (f32[7,32,512]{2,1,0:T(8,128)}, f32[7,32,512]{2,1,0:T(8,128)S(1)}, u32[]{:S(2)}, u32[]{:S(2)}) collective-permute-start(f32[7,32,512]{2,1,0:T(8,128)} %dynamic-slice_bitcast_fusion.2), channel_id=1, source_target_pairs={{0,1},{1,0},{2,3},{3,2},{4,5},{5,4},{6,7},{7,6},{8,9},{9,8},{10,11... | collective-permute-start | bytes 1376264 | tf_op jit(solution)/shard_map/ppermute | solution.py:438
  41.2 29.9 %collective-permute-start.9 = (f32[2,7,32,512]{3,2,1,0:T(8,128)}, f32[2,7,32,512]{3,2,1,0:T(8,128)}, u32[]{:S(2)}, u32[]{:S(2)}) collective-permute-start(f32[2,7,32,512]{3,2,1,0:T(8,128)} %get-tuple-element.38), channel_id=1, source_target_pairs={{0,2},{2,0},{1,3},{3,1},{4,6},{6,4},{5,7},{7,5},{8,10},{10,8},{9,1... | collective-permute-start | bytes 2752520 | tf_op jit(solution)/shard_map/ppermute | solution.py:438
  51.3 4.6 %collective-permute-start.6 = (f32[9,32,512]{2,1,0:T(8,128)}, f32[9,32,512]{2,1,0:T(8,128)S(1)}, u32[]{:S(2)}, u32[]{:S(2)}) collective-permute-start(f32[9,32,512]{2,1,0:T(8,128)} %dynamic-slice_bitcast_fusion.1), channel_id=1, source_target_pairs={{0,1},{1,0},{2,3},{3,2},{4,5},{5,4},{6,7},{7,6},{8,9},{9,8},{10,11... | collective-permute-start | bytes 1769480 | tf_op jit(solution)/shard_map/ppermute | solution.py:438
  53.4 2.2 %collective-permute-start.7 = (f32[7,32,512]{2,1,0:T(8,128)S(1)}, f32[7,32,512]{2,1,0:T(8,128)S(1)}, u32[]{:S(2)}, u32[]{:S(2)}) collective-permute-start(f32[7,32,512]{2,1,0:T(8,128)S(1)} %get-tuple-element.32), channel_id=1, source_target_pairs={{0,1},{1,0},{2,3},{3,2},{4,5},{5,4},{6,7},{7,6},{8,9},{9,8},{10,11... | collective-permute-start | bytes 1376264 | tf_op jit(solution)/shard_map/ppermute | solution.py:438
  55.9 0.8 copy-start.3
  68.1 0.8 copy-start
  68.9 6.7 %collective-permute-start.8 = (f32[9,32,512]{2,1,0:T(8,128)}, f32[9,32,512]{2,1,0:T(8,128)}, u32[]{:S(2)}, u32[]{:S(2)}) collective-permute-start(f32[9,32,512]{2,1,0:T(8,128)} %get-tuple-element.37), channel_id=1, source_target_pairs={{0,1},{1,0},{2,3},{3,2},{4,5},{5,4},{6,7},{7,6},{8,9},{9,8},{10,11... | collective-permute-start | bytes 1769480 | tf_op jit(solution)/shard_map/ppermute | solution.py:438
  69.3 16.0 %collective-permute-start.11 = (f32[9,32,512]{2,1,0:T(8,128)}, f32[9,32,512]{2,1,0:T(8,128)S(1)}, u32[]{:S(2)}, u32[]{:S(2)}) collective-permute-start(f32[9,32,512]{2,1,0:T(8,128)} %get-tuple-element.40), channel_id=1, source_target_pairs={{0,2},{2,0},{1,3},{3,1},{4,6},{6,4},{5,7},{7,5},{8,10},{10,8},{9,1... | collective-permute-start | bytes 1769480 | tf_op jit(solution)/shard_map/ppermute | solution.py:438
  73.3 2.4 %collective-permute-start.10 = (f32[7,32,512]{2,1,0:T(8,128)}, f32[7,32,512]{2,1,0:T(8,128)}, u32[]{:S(2)}, u32[]{:S(2)}) collective-permute-start(f32[7,32,512]{2,1,0:T(8,128)} %get-tuple-element.43), channel_id=1, source_target_pairs={{0,1},{1,0},{2,3},{3,2},{4,5},{5,4},{6,7},{7,6},{8,9},{9,8},{10,11... | collective-permute-start | bytes 1376264 | tf_op jit(solution)/shard_map/ppermute | solution.py:438
  73.7 21.7 %collective-permute-start.12 = (f32[7,32,512]{2,1,0:T(8,128)S(1)}, f32[7,32,512]{2,1,0:T(8,128)S(1)}, u32[]{:S(2)}, u32[]{:S(2)}) collective-permute-start(f32[7,32,512]{2,1,0:T(8,128)S(1)} %get-tuple-element.41), channel_id=1, source_target_pairs={{0,3},{3,0},{1,2},{2,1},{4,7},{7,4},{5,6},{6,5},{8,11},{11,8},{9,1... | collective-permute-start | bytes 1376264 | tf_op jit(solution)/shard_map/ppermute | solution.py:438
  73.8 23.9 %collective-permute-start.13 = (f32[2,32,512]{2,1,0:T(8,128)S(1)}, f32[2,32,512]{2,1,0:T(8,128)S(1)}, u32[]{:S(2)}, u32[]{:S(2)}) collective-permute-start(f32[2,32,512]{2,1,0:T(8,128)S(1)} %get-tuple-element.42), channel_id=1, source_target_pairs={{0,3},{3,0},{1,2},{2,1},{4,7},{7,4},{5,6},{6,5},{8,11},{11,8},{9,1... | collective-permute-start | bytes 393224 | tf_op jit(solution)/shard_map/ppermute | solution.py:438

commit v6 on v5

--- a/solution.py
+++ b/solution.py
@@ -135,7 +135,7 @@
     return jnp.stack([j_radial, j_polar, j_azim])
 
 
-CHUNKS = ((7,), (9,))
+CHUNKS = (7, 9)
 LAST = (7, 2)
 TO_Y = [(0, 2), (2, 0), (1, 3), (3, 1)]
 TO_C = [(0, 1), (1, 0), (2, 3), (3, 2)]
@@ -173,19 +173,17 @@
     return dot(high, table[0]) + dot(high, table[1]) + dot(low, table[0])
 
 
-def transform_kernel(count, outputs, place, own, beside, diagonal, kept, gain, modes, *refs):
-    across, tables, refs = refs[:count], refs[count : count + 6], refs[count + 6 :]
-    (out_own, out_beside, *outs), held, sems = refs[:outputs], refs[outputs:-1], refs[-1]
+def transform_kernel(place, own, across, beside, diagonal, kept, gain, modes, *refs):
+    tables, (out_own, out_beside, *outs), held, sems = refs[:6], refs[6:-7], refs[-7:-1], refs[-1]
     copies = [pltpu.make_async_copy(table, ref, sems.at[i]) for i, (table, ref) in enumerate(zip(tables, held))]
     for copy in copies:
         copy.start()
     quarter = own.shape[-1]
-    rows = diagonal.shape[0] * diagonal.shape[1]
+    rows = across.shape[0] * across.shape[1]
     sign_y = (1 - 2 * place[0]).astype(jnp.float32)
     sign_c = (1 - 2 * place[1]).astype(jnp.float32)
     first = place[1] == 0
-    a, c, d = (ref[...].reshape(rows, quarter) for ref in (own, beside, diagonal))
-    b = jnp.concatenate([ref[...].reshape(-1, quarter) for ref in across], axis=0)
+    a, b, c, d = (ref[...].reshape(rows, quarter) for ref in (own, across, beside, diagonal))
     near, far = a + b, c + d
     near_odd, far_odd = sign_y * (a - b), sign_y * (c - d)
     odd = jnp.concatenate([jnp.where(first, near_odd, far_odd), jnp.where(first, far_odd, near_odd)], axis=1)
@@ -219,39 +217,44 @@
             at += out.shape[0]
 
 
-def transform(place, magnetic, start, parts, beside, diagonal, row_kept, row_gain, tables, cuts):
-    depth, th_dev, quarter = diagonal.shape
+def transform(place, magnetic, start, across, beside, diagonal, row_kept, row_gain, tables, cuts):
+    depth, th_dev, quarter = across.shape[1:]
     zero, two, odd, mode_ids = tables
     whole = pl.BlockSpec(memory_space=pltpu.VMEM)
     rows = depth * th_dev
     half = magnetic.shape[1] // 2
-    part = (pl.Element(1), pl.Element(depth), pl.Element(th_dev), pl.Element(quarter))
+    shape = (depth, th_dev, quarter)
+    part = tuple(pl.Element(size) for size in shape)
     row_block = pl.BlockSpec((pl.Element(rows), pl.Element(1)), lambda i, p: (start * th_dev, 0))
-    shape = (depth, th_dev, quarter)
     shapes = [shape, shape, (2,) + shape] if cuts is None else [shape] * 3 + [(cut, th_dev, quarter) for cut in cuts]
+    if diagonal is None:
+        diagonal, whole_diagonal = across, pl.BlockSpec((None,) + shape, lambda i, p: (1, 0, 0, 0))
+        across_part = pl.BlockSpec((None,) + shape, lambda i, p: (0, 0, 0, 0))
+    else:
+        whole_diagonal, across_part = whole, pl.BlockSpec((None,) + shape, lambda i, p: (p[1], 0, 0, 0))
     grid_spec = pltpu.PrefetchScalarGridSpec(
         num_scalar_prefetch=1,
         grid=(1,),
         in_specs=[
-            pl.BlockSpec(part, lambda i, p: (p[1], p[0] * half + start, 0, 0)),
-            pl.BlockSpec(part[1:], lambda i, p: (start, 0, 0)),
-            whole,
+            pl.BlockSpec((pl.Element(1),) + part, lambda i, p: (p[1], p[0] * half + start, 0, 0)),
+            across_part,
+            pl.BlockSpec(part, lambda i, p: (start, 0, 0)),
+            whole_diagonal,
             row_block,
             row_block,
             whole,
         ]
-        + [pl.BlockSpec((None,) + value.shape[1:], lambda i, p: (p[1], 0, 0, 0)) for value in parts]
         + [pl.BlockSpec(memory_space=pl.ANY)] * 6,
         out_specs=[whole] * len(shapes),
         scratch_shapes=[pltpu.VMEM(t.shape, jnp.bfloat16) for t in (*zero, *two, *odd)] + [pltpu.SemaphoreType.DMA((6,))],
     )
     return pl.pallas_call(
-        functools.partial(transform_kernel, len(parts), len(shapes)),
+        transform_kernel,
         grid_spec=grid_spec,
         out_shape=[jax.ShapeDtypeStruct(shape, jnp.float32) for shape in shapes],
         compiler_params=pltpu.CompilerParams(vmem_limit_bytes=VMEM),
         cost_estimate=SHORT,
-    )(place, magnetic, beside, diagonal, row_kept, row_gain, mode_ids, *parts, *zero, *two, *odd)
+    )(place, magnetic, across, beside, diagonal, row_kept, row_gain, mode_ids, *zero, *two, *odd)
 
 
 def edge_rows(magnetic):
@@ -427,10 +430,9 @@
 def on_four(magnetic, kept_modes):
     radii, th_dev, ph_dev = (magnetic.shape[1], magnetic.shape[2], magnetic.shape[3])
     half = radii // 2
-    unit = half // sum(map(sum, CHUNKS))
-    pieces = [[unit * piece for piece in chunk] for chunk in CHUNKS]
-    depths = [sum(chunk) for chunk in pieces]
-    last_cuts = [unit * piece for piece in LAST]
+    unit = half // sum(CHUNKS)
+    depths = [unit * part for part in CHUNKS]
+    last_cuts = [unit * part for part in LAST]
     starts = [sum(depths[:k]) for k in range(len(depths))]
     index = lax.axis_index("azim")
     y, c = index // 2, index % 2
@@ -440,28 +442,26 @@
     def cut(source, field, start, length):
         return lax.dynamic_slice(source, (field, start, 0, 0), (1, length, th_dev, ph_dev))[0]
 
-    arrived = []
-    source = magnetic
-    for k, chunk in enumerate(pieces):
-        arrived.append([])
-        for i, depth in enumerate(chunk):
-            at = (1 - y) * half + starts[k] + sum(chunk[:i])
-            if k == 0:
-                both = copy_part(place, source, starts[k] + sum(chunk[:i]), depth)
-            else:
-                both = lax.dynamic_slice(source, (0, at, 0, 0), (2, depth, th_dev, ph_dev))
-            (source,) = after(both, source)
-            arrived[k].append(send(both, TO_Y))
-        if k == 0:
-            lat_size = lax.axis_size("lat")
-            up = [(i, i + 1) for i in range(lat_size - 1)]
-            down = [(i + 1, i) for i in range(lat_size - 1)]
-            last, first = edge_rows(source)
-            (source,) = after((last, first), source)
-            north, south = lax.ppermute(last, "lat", up), lax.ppermute(first, "lat", down)
-            to_c = cut(source, 1 - c, y * half, half)
-            (source,) = after(to_c, source)
-            beside = send(to_c, TO_C)
+    both = copy_part(place, magnetic, 0, depths[0])
+    (source,) = after(both, magnetic)
+    arrived = [send(both, TO_Y)]
+    last, first = edge_rows(source)
+    (source,) = after((last, first), source)
+    crossing = []
+    for start, depth in zip(starts[1:], depths[1:]):
+        to_c = cut(source, 1 - c, (1 - y) * half + start, depth)
+        (source,) = after(to_c, source)
+        crossing.append(send(to_c, TO_C))
+    to_c = cut(source, 1 - c, y * half, half)
+    (source,) = after(to_c, source)
+    beside = send(to_c, TO_C)
+    for start, depth, crossed in zip(starts[1:], depths[1:], crossing):
+        both = jnp.stack([cut(source, c, (1 - y) * half + start, depth), crossed])
+        arrived.append(send(both, TO_Y))
+    lat_size = lax.axis_size("lat")
+    up = [(i, i + 1) for i in range(lat_size - 1)]
+    down = [(i + 1, i) for i in range(lat_size - 1)]
+    north, south = lax.ppermute(last, "lat", up), lax.ppermute(first, "lat", down)
 
     spacing, band_start, colatitude = band_geometry(th_dev)
     radius = (inner_radius + (jnp.arange(radii, dtype=jnp.float32) + 0.5) * spacing)[:, None, None]
@@ -477,16 +477,19 @@
     tables = mode_tables(4 * ph_dev)
     mine, from_c, returned = [], [], []
     for k, start in enumerate(starts):
-        parts = arrived[k]
-        if k > 0:
-            parts = after(mine[-1], *parts)
+        across, diagonal = arrived[k], None
         (row_gain,) = after(from_c[-1] if k > 0 else (north, south), row_gain)
-        diagonal = send(jnp.concatenate([cut(part, 1 - c, 0, part.shape[1]) for part in parts]), TO_C)
+        if k == 0:
+            diagonal = send(cut(across, 1 - c, 0, depths[k]), TO_C)
+        else:
+            (across,) = after(mine[-1], across)
         cuts = None if k + 1 < len(starts) else last_cuts
         out, to_c, to_y, *to_yc = transform(
-            place, magnetic, start, parts, beside, diagonal, row_kept, row_gain, tables, cuts
+            place, magnetic, start, across, beside, diagonal, row_kept, row_gain, tables, cuts
         )
         mine.append(out)
+        if k + 1 < len(starts):
+            (to_c,) = after(arrived[k + 1], to_c)
         from_c.append(send(to_c, TO_C))
         returned.append(send(to_y, TO_Y))
     final = [(returned.pop(), True, starts[-1])]
@@ -511,7 +514,7 @@
 
     def run(magnetic, kept_modes):
         radii, ph_dev = magnetic.shape[1], magnetic.shape[3]
-        four = lax.axis_size("azim") == 4 and radii % (2 * sum(map(sum, CHUNKS))) == 0 and ph_dev % 256 == 0
+        four = lax.axis_size("azim") == 4 and radii % (2 * sum(CHUNKS)) == 0 and ph_dev % 256 == 0
         return (on_four if four else on_device)(magnetic, kept_modes)
 
     return jax.shard_map(

time: 99.6 us -> 97.3 us (0.977)
  waiting for transfers between devices: 28.6 us -> 24.8 us
  other arithmetic: 0.39 us -> 2.64 us
  local copies, waits for them, and re-layouts: 12.9 us -> 10.8 us
  starting transfers between devices: 17.6 us -> 19.2 us
    ppermute x12, waiting for transfers between devices: 24.9 us -> 18.8 us  [on_four(): send = lambda value, pairs: lax.ppermute(value, 'azim', pairs)]
    ppermute x1, waiting for transfers between devices: 3.66 us -> 5.97 us  [on_four(): lax.ppermute(last, 'lat', up)]
    another operation x0 -> x1, other arithmetic: none -> 2.25 us  [on_four(): both = jnp.stack([cut(source, c, (1 - y) * half + start, depth), crossed])]
    ppermute x12, starting transfers between devices: 12.9 us -> 14.5 us  [on_four(): send = lambda value, pairs: lax.ppermute(value, 'azim', pairs)]
    dynamic_slice x1, local copies, waits for them, and re-layouts: 2.41 us -> 1.1 us  [cut(): lax.dynamic_slice(source, (field, start, 0, 0), (1, length, th_dev, ph_dev))]
  transfers between devices with their start and end apart: 14 -> 14, of which waited for: 6 -> 6; matrix products, arithmetic and copies ran while one was open for 12% -> 13% of each run, Pallas kernels for 37% -> 37%
where the time goes in v6:
time: 97.3 us; the launch traced here: 96.7 us
  Pallas kernels  39 us (40%)
  waiting for transfers between devices  24.8 us (25%)
  starting transfers between devices  19.2 us (20%)
  local copies, waits for them, and re-layouts  10.8 us (11%)
  other arithmetic  2.64 us (3%)
    pallas_call x2, Pallas kernels, transform(): pl.pallas_call(transform_kernel, grid_spec=grid_spec, out_shape=[jax.Shap...  20.8 us
    ppermute x12, waiting for transfers between devices, on_four(): send = lambda value, pairs: lax.ppermute(value, 'azim', pairs)  18.8 us
    ppermute x12, starting transfers between devices, on_four(): send = lambda value, pairs: lax.ppermute(value, 'azim', pairs)  14.5 us
    pallas_call x1, Pallas kernels, local_part(): pl.pallas_call(kernel, grid_spec=pltpu.PrefetchScalarGridSpec(num_scalar_...  8.78 us
    squeeze x4, local copies, waits for them, and re-layouts, cut(): lax.dynamic_slice(source, (field, start, 0, 0), (1, length, th_dev, ph_dev))  5.99 us
    ppermute x1, waiting for transfers between devices, on_four(): lax.ppermute(last, 'lat', up)  5.97 us
    pallas_call x2, Pallas kernels, add_one(): pl.pallas_call(kernel, grid_spec=pltpu.PrefetchScalarGridSpec(num_scalar_...  4.86 us
    ppermute x1, starting transfers between devices, on_four(): lax.ppermute(last, 'lat', up)  3.35 us
  transfers between devices with their start and end apart: 14, of which 6 were waited for; matrix products, arithmetic and copies ran while one was open for 13% of the time, Pallas kernels for 37%

profile of v6, /device:TPU:1, one launch (start us, length us, event | category | flops | bytes accessed | tf_op | source)
XLA Modules:
  0.0 96.7 jit_solution(845280117732818799)
XLA Ops:
  0.0 0.1 pad_add_fusion.place
  0.1 1.7 %shard_map.91 = f32[2,7,32,512]{3,2,1,0:T(8,128)S(1)} custom-call(s32[2]{0:T(128)S(1)} %pad_add_fusion.place, f32[3,32,32,512]{3,2,1,0:T(8,128)} %field.1), custom_call_target="tpu_custom_call" | custom-call | flops 1 | bytes 1 | tf_op jit(solution)/shard_map/pallas_call | solution.py:295
  1.8 2.1 %collective-permute-start = (f32[2,7,32,512]{3,2,1,0:T(8,128)S(1)}, f32[2,7,32,512]{3,2,1,0:T(8,128)S(1)}, u32[]{:S(2)}, u32[]{:S(2)}) collective-permute-start(f32[2,7,32,512]{3,2,1,0:T(8,128)S(1)} %shard_map.91), channel_id=1, source_target_pairs={{0,2},{2,0},{1,3},{3,1},{4,6},{6,4},{5,7},{7,5},{8,10},{10,8},{9,1... | collective-permute-start | bytes 2752520 | tf_op jit(solution)/shard_map/ppermute | solution.py:440
  3.9 1.6 %shard_map.92 = (f32[2,3,32,512]{3,2,1,0:T(8,128)S(1)}, f32[2,3,32,512]{3,2,1,0:T(8,128)S(1)}) custom-call(f32[3,32,32,512]{3,2,1,0:T(8,128)} %field.1, f32[3,32,32,512]{3,2,1,0:T(8,128)} %field.1), custom_call_target="tpu_custom_call" | custom-call | flops 1 | bytes 1 | tf_op jit(solution)/shard_map/pallas_call | solution.py:270
  5.6 0.0 copy-start.3
  5.6 0.0 copy-start.1
  5.6 1.9 %dynamic-slice_bitcast_fusion.1 = f32[9,32,512]{2,1,0:T(8,128)} fusion(f32[3,32,32,512]{3,2,1,0:T(8,128)} %field.1, s32[]{:T(128)S(6)} %select_n.38, s32[]{:T(128)S(6)} %select_n.39), kind=kLoop, calls=%fused_computation.2 | loop fusion | bytes 1179656 | tf_op jit(solution)/shard_map/squeeze | solution.py:443
  7.5 1.0 collective-permute-start.5
  8.5 2.3 %dynamic-slice_bitcast_fusion = f32[16,32,512]{2,1,0:T(8,128)} fusion(f32[3,32,32,512]{3,2,1,0:T(8,128)} %field.1, s32[]{:T(128)S(6)} %select_n.38, s32[]{:T(128)S(6)} %select_n.40), kind=kLoop, calls=%fused_computation.1 | loop fusion | bytes 2097160 | tf_op jit(solution)/shard_map/squeeze | solution.py:443
  10.8 0.0 collective-permute-start.1
  10.8 1.1 %constant_dynamic-slice_fusion = f32[1,9,32,512]{3,2,1,0:T(8,128)S(1)} fusion(f32[3,32,32,512]{3,2,1,0:T(8,128)} %field.1, s32[]{:T(128)S(6)} %select_n.43, s32[]{:T(128)S(6)} %select_n.39), kind=kLoop, calls=%fused_computation.11 | loop fusion | bytes 1179656 | tf_op jit(solution)/shard_map/dynamic_slice | solution.py:443
  11.9 2.2 %pad_maximum_fusion = f32[2,9,32,512]{3,2,1,0:T(8,128)} fusion(f32[1,9,32,512]{3,2,1,0:T(8,128)} %bitcast.5, f32[1,9,32,512]{3,2,1,0:T(8,128)S(1)} %constant_dynamic-slice_fusion), kind=kLoop, calls=%fused_computation | loop fusion | flops 294912 | bytes 2359296 | tf_op jit(solution)/shard_map/stack | solution.py:459
  14.2 3.4 %collective-permute-start.3 = (f32[2,3,32,512]{3,2,1,0:T(8,128)S(1)}, f32[2,3,32,512]{3,2,1,0:T(8,128)S(1)}, u32[]{:S(2)}, u32[]{:S(2)}) collective-permute-start(f32[2,3,32,512]{3,2,1,0:T(8,128)S(1)} %get-tuple-element.27), channel_id=1, source_target_pairs={{0,4},{4,8},{8,12},{12,16},{16,20},{20,24},{24,28},{1,5},{5,9},{9,... | collective-permute-start | bytes 1179656 | tf_op jit(solution)/shard_map/ppermute | solution.py:464
  17.5 1.3 %collective-permute-start.4 = (f32[2,3,32,512]{3,2,1,0:T(8,128)S(1)}, f32[2,3,32,512]{3,2,1,0:T(8,128)S(1)}, u32[]{:S(2)}, u32[]{:S(2)}) collective-permute-start(f32[2,3,32,512]{3,2,1,0:T(8,128)S(1)} %get-tuple-element.28), channel_id=1, source_target_pairs={{4,0},{8,4},{12,8},{16,12},{20,16},{24,20},{28,24},{5,1},{9,5},{13... | collective-permute-start | bytes 1179656 | tf_op jit(solution)/shard_map/ppermute | solution.py:464
  18.8 5.2 %collective-permute-done.across = f32[2,7,32,512]{3,2,1,0:T(8,128)S(1)} collective-permute-done((f32[2,7,32,512]{3,2,1,0:T(8,128)S(1)}, f32[2,7,32,512]{3,2,1,0:T(8,128)S(1)}, u32[]{:S(2)}, u32[]{:S(2)}) %collective-permute-start) | collective-permute-done | bytes 917536 | tf_op jit(solution)/shard_map/ppermute | solution.py:440
  24.0 0.9 dynamic-slice_bitcast_fusion.2
  24.9 2.1 %collective-permute-start.2 = (f32[7,32,512]{2,1,0:T(8,128)}, f32[7,32,512]{2,1,0:T(8,128)S(1)}, u32[]{:S(2)}, u32[]{:S(2)}) collective-permute-start(f32[7,32,512]{2,1,0:T(8,128)} %dynamic-slice_bitcast_fusion.2), channel_id=1, source_target_pairs={{0,1},{1,0},{2,3},{3,2},{4,5},{5,4},{6,7},{7,6},{8,9},{9,8},{10,11... | collective-permute-start | bytes 1376264 | tf_op jit(solution)/shard_map/ppermute | solution.py:440
  26.9 0.1 dynamic-slice
  27.1 0.1 broadcast_multiply_fusion
  27.1 0.1 reshape.73
  27.2 0.1 dynamic-slice_convert_fusion
  27.3 0.3 reshape.74.kept
  27.6 6.0 %collective-permute-done.3.before = f32[2,3,32,512]{3,2,1,0:T(8,128)S(1)} collective-permute-done((f32[2,3,32,512]{3,2,1,0:T(8,128)S(1)}, f32[2,3,32,512]{3,2,1,0:T(8,128)S(1)}, u32[]{:S(2)}, u32[]{:S(2)}) %collective-permute-start.3) | collective-permute-done | bytes 393248 | tf_op jit(solution)/shard_map/ppermute | solution.py:464
  33.6 0.0 collective-permute-done.4.after
  33.6 0.1 copy.18.gain
  33.7 0.0 collective-permute-done.1.beside
  33.7 9.7 %shard_map.93 = (f32[7,32,512]{2,1,0:T(8,128)S(1)}, f32[7,32,512]{2,1,0:T(8,128)S(1)}, f32[2,7,32,512]{3,2,1,0:T(8,128)}) custom-call(s32[2]{0:T(128)S(1)} %pad_add_fusion.place, f32[3,32,32,512]{3,2,1,0:T(8,128)} %field.1, f32[2,7,32,512]{3,2,1,0:T(8,128)} %copy-done.2, f32[16,32,512]{2,1,0:T(8,128)} %collective-permute-done.1.beside, ...), custom_call_target="tpu_custom_call" | custom-call | flops 1 | bytes 1 | tf_op jit(solution)/shard_map/pallas_call | solution.py:251
  43.4 1.3 %collective-permute-start.9 = (f32[2,7,32,512]{3,2,1,0:T(8,128)}, f32[2,7,32,512]{3,2,1,0:T(8,128)}, u32[]{:S(2)}, u32[]{:S(2)}) collective-permute-start(f32[2,7,32,512]{3,2,1,0:T(8,128)} %get-tuple-element.42), channel_id=1, source_target_pairs={{0,2},{2,0},{1,3},{3,1},{4,6},{6,4},{5,7},{7,5},{8,10},{10,8},{9,1... | collective-permute-start | bytes 2752520 | tf_op jit(solution)/shard_map/ppermute | solution.py:440
  44.7 4.6 %collective-permute-done.6.across.diagonal = f32[2,9,32,512]{3,2,1,0:T(8,128)} collective-permute-done((f32[2,9,32,512]{3,2,1,0:T(8,128)}, f32[2,9,32,512]{3,2,1,0:T(8,128)}, u32[]{:S(2)}, u32[]{:S(2)}) %collective-permute-start.6) | collective-permute-done | bytes 1179680 | tf_op jit(solution)/shard_map/ppermute | solution.py:440
  49.4 2.1 %collective-permute-start.7 = (f32[7,32,512]{2,1,0:T(8,128)S(1)}, f32[7,32,512]{2,1,0:T(8,128)S(1)}, u32[]{:S(2)}, u32[]{:S(2)}) collective-permute-start(f32[7,32,512]{2,1,0:T(8,128)S(1)} %get-tuple-element.36), channel_id=1, source_target_pairs={{0,1},{1,0},{2,3},{3,2},{4,5},{5,4},{6,7},{7,6},{8,9},{9,8},{10,11... | collective-permute-start | bytes 1376264 | tf_op jit(solution)/shard_map/ppermute | solution.py:440
  51.5 1.4 %collective-permute-done.7.refs_1_ = f32[7,32,512]{2,1,0:T(8,128)S(1)} collective-permute-done((f32[7,32,512]{2,1,0:T(8,128)S(1)}, f32[7,32,512]{2,1,0:T(8,128)S(1)}, u32[]{:S(2)}, u32[]{:S(2)}) %collective-permute-start.7) | collective-permute-done | bytes 458784 | tf_op jit(solution)/shard_map/ppermute | solution.py:440
  52.9 0.1 copy.20.gain
  53.0 11.2 %shard_map.94 = (f32[9,32,512]{2,1,0:T(8,128)S(1)}, f32[9,32,512]{2,1,0:T(8,128)}, f32[9,32,512]{2,1,0:T(8,128)}, f32[7,32,512]{2,1,0:T(8,128)S(1)}, f32[2,32,512]{2,1,0:T(8,128)S(1)}) custom-call(s32[2]{0:T(128)S(1)} %pad_add_fusion.place, f32[3,32,32,512]{3,2,1,0:T(8,128)} %field.1, f32[2,9,32,512]{3,2,1,0:T(8,128)} %collective-permute-done.6.across.diagonal, ...), custom_call_target="tpu_custom_call" | custom-call | flops 1 | bytes 1 | tf_op jit(solution)/shard_map/pallas_call | solution.py:251
  64.2 0.8 copy-done
  65.0 0.4 collective-permute-start.8
  65.4 1.8 %collective-permute-start.11 = (f32[9,32,512]{2,1,0:T(8,128)}, f32[9,32,512]{2,1,0:T(8,128)S(1)}, u32[]{:S(2)}, u32[]{:S(2)}) collective-permute-start(f32[9,32,512]{2,1,0:T(8,128)} %get-tuple-element.44), channel_id=1, source_target_pairs={{0,2},{2,0},{1,3},{3,1},{4,6},{6,4},{5,7},{7,5},{8,10},{10,8},{9,1... | collective-permute-start | bytes 1769480 | tf_op jit(solution)/shard_map/ppermute | solution.py:440
  67.2 1.9 %collective-permute-done.9 = f32[2,7,32,512]{3,2,1,0:T(8,128)} collective-permute-done((f32[2,7,32,512]{3,2,1,0:T(8,128)}, f32[2,7,32,512]{3,2,1,0:T(8,128)}, u32[]{:S(2)}, u32[]{:S(2)}) %collective-permute-start.9) | collective-permute-done | bytes 917536 | tf_op jit(solution)/shard_map/ppermute | solution.py:440
  69.1 2.2 %slice_bitcast_fusion = (f32[7,32,512]{2,1,0:T(8,128)}, f32[7,32,512]{2,1,0:T(8,128)}) fusion(f32[2,7,32,512]{3,2,1,0:T(8,128)} %collective-permute-done.9), kind=kLoop, calls=%fused_computation.3 | loop fusion | bytes 1835008 | tf_op jit(solution)/shard_map/squeeze | solution.py:501
  71.2 2.1 %collective-permute-start.10 = (f32[7,32,512]{2,1,0:T(8,128)}, f32[7,32,512]{2,1,0:T(8,128)}, u32[]{:S(2)}, u32[]{:S(2)}) collective-permute-start(f32[7,32,512]{2,1,0:T(8,128)} %get-tuple-element.47), channel_id=1, source_target_pairs={{0,1},{1,0},{2,3},{3,2},{4,5},{5,4},{6,7},{7,6},{8,9},{9,8},{10,11... | collective-permute-start | bytes 1376264 | tf_op jit(solution)/shard_map/ppermute | solution.py:440
  73.3 1.6 %collective-permute-start.12 = (f32[7,32,512]{2,1,0:T(8,128)S(1)}, f32[7,32,512]{2,1,0:T(8,128)S(1)}, u32[]{:S(2)}, u32[]{:S(2)}) collective-permute-start(f32[7,32,512]{2,1,0:T(8,128)S(1)} %get-tuple-element.45), channel_id=1, source_target_pairs={{0,3},{3,0},{1,2},{2,1},{4,7},{7,4},{5,6},{6,5},{8,11},{11,8},{9,1... | collective-permute-start | bytes 1376264 | tf_op jit(solution)/shard_map/ppermute | solution.py:440
  74.9 0.2 collective-permute-start.13
  75.1 0.1 divide_multiply_fusion.cot
  75.2 8.8 %shard_map.95.base = f32[3,32,32,512]{3,2,1,0:T(8,128)} custom-call(s32[2]{0:T(128)S(1)} %pad_add_fusion.place, f32[3,32,32,512]{3,2,1,0:T(8,128)} %field.1, f32[2,3,32,512]{3,2,1,0:T(8,128)S(1)} %collective-permute-done.3.before, f32[2,3,32,512]{3,2,1,0:T(8,128)S(1)} %collective-permute-done.4.after, f32[32,1,1]{2,1,0:T(1,128)S(1)} %get-tuple-element.49.radius, ...), custom_call_target="tpu_custom_call" | custom-call | flops 1 | bytes 1 | tf_op jit(solution)/shard_map/pallas_call | solution.py:346
  84.0 0.9 dynamic-slice_bitcast_fusion.3.base
  84.9 2.5 %shard_map.96.base = f32[3,32,32,512]{3,2,1,0:T(8,128)} custom-call(s32[2]{0:T(128)S(1)} %pad_add_fusion.place, f32[3,32,32,512]{3,2,1,0:T(8,128)} %shard_map.95.base, f32[9,32,512]{2,1,0:T(8,128)S(1)} %collective-permute-done.11.azim), custom_call_target="tpu_custom_call", output_to_operand_aliasing={{}: (1, {})} | custom-call | flops 1 | bytes 1 | tf_op jit(solution)/shard_map/pallas_call | solution.py:384
  87.4 5.7 %collective-permute-done.12.azim = f32[7,32,512]{2,1,0:T(8,128)S(1)} collective-permute-done((f32[7,32,512]{2,1,0:T(8,128)S(1)}, f32[7,32,512]{2,1,0:T(8,128)S(1)}, u32[]{:S(2)}, u32[]{:S(2)}) %collective-permute-start.12) | collective-permute-done | bytes 458784 | tf_op jit(solution)/shard_map/ppermute | solution.py:440
  93.1 2.4 %shard_map.97.current = f32[3,32,32,512]{3,2,1,0:T(8,128)} custom-call(s32[2]{0:T(128)S(1)} %pad_add_fusion.place, f32[3,32,32,512]{3,2,1,0:T(8,128)} %shard_map.96.base, f32[7,32,512]{2,1,0:T(8,128)S(1)} %collective-permute-done.12.azim), custom_call_target="tpu_custom_call", output_to_operand_aliasing={{}: (1, {})} | custom-call | flops 1 | bytes 1 | tf_op jit(solution)/shard_map/pallas_call | solution.py:384
  95.5 1.2 %shard_map.98 = f32[3,32,32,512]{3,2,1,0:T(8,128)} custom-call(s32[2]{0:T(128)S(1)} %pad_add_fusion.place, f32[3,32,32,512]{3,2,1,0:T(8,128)} %shard_map.97.current, f32[2,32,512]{2,1,0:T(8,128)S(1)} %dynamic-slice_bitcast_fusion.3.base, f32[2,32,512]{2,1,0:T(8,128)S(1)} %collective-permute-done.13.azim), custom_call_target="tpu_custom_call", output_to_operand_aliasing={{}: (1, {})} | custom-call | flops 1 | bytes 1 | tf_op jit(solution)/shard_map/pallas_call | solution.py:410
  (16 shorter events, 0.1 us)
Async XLA Ops:
  1.8 22.2 %collective-permute-start = (f32[2,7,32,512]{3,2,1,0:T(8,128)S(1)}, f32[2,7,32,512]{3,2,1,0:T(8,128)S(1)}, u32[]{:S(2)}, u32[]{:S(2)}) collective-permute-start(f32[2,7,32,512]{3,2,1,0:T(8,128)S(1)} %shard_map.91), channel_id=1, source_target_pairs={{0,2},{2,0},{1,3},{3,1},{4,6},{6,4},{5,7},{7,5},{8,10},{10,8},{9,1... | collective-permute-start | bytes 2752520 | tf_op jit(solution)/shard_map/ppermute | solution.py:440
  5.6 21.7 %copy-start.3 = (s32[256]{0:T(256)S(1)}, s32[256]{0:T(256)}, u32[]{:S(2)}) copy-start(s32[256]{0:T(256)} %param.10) | copy-start | bytes 3076
  5.6 28.2 %copy-start.1 = (f32[1,2048]{1,0:T(1,128)S(1)}, f32[1,2048]{1,0:T(1,128)}, u32[]{:S(2)}) copy-start(f32[1,2048]{1,0:T(1,128)} %constant.85.clone.modes) | copy-start | bytes 24580
  7.5 4.4 %collective-permute-start.5 = (f32[9,32,512]{2,1,0:T(8,128)}, f32[9,32,512]{2,1,0:T(8,128)}, u32[]{:S(2)}, u32[]{:S(2)}) collective-permute-start(f32[9,32,512]{2,1,0:T(8,128)} %dynamic-slice_bitcast_fusion.1), channel_id=1, source_target_pairs={{0,1},{1,0},{2,3},{3,2},{4,5},{5,4},{6,7},{7,6},{8,9},{9,8},{10,11... | collective-permute-start | bytes 1769480 | tf_op jit(solution)/shard_map/ppermute | solution.py:440
  10.8 22.9 %collective-permute-start.1 = (f32[16,32,512]{2,1,0:T(8,128)}, f32[16,32,512]{2,1,0:T(8,128)}, u32[]{:S(2)}, u32[]{:S(2)}) collective-permute-start(f32[16,32,512]{2,1,0:T(8,128)} %dynamic-slice_bitcast_fusion), channel_id=1, source_target_pairs={{0,1},{1,0},{2,3},{3,2},{4,5},{5,4},{6,7},{7,6},{8,9},{9,8},{10,11... | collective-permute-start | bytes 3145736 | tf_op jit(solution)/shard_map/ppermute | solution.py:440
  14.2 35.2 %collective-permute-start.6 = (f32[2,9,32,512]{3,2,1,0:T(8,128)}, f32[2,9,32,512]{3,2,1,0:T(8,128)}, u32[]{:S(2)}, u32[]{:S(2)}) collective-permute-start(f32[2,9,32,512]{3,2,1,0:T(8,128)} %pad_maximum_fusion), channel_id=1, source_target_pairs={{0,2},{2,0},{1,3},{3,1},{4,6},{6,4},{5,7},{7,5},{8,10},{10,8},{9,1... | collective-permute-start | bytes 3538952 | tf_op jit(solution)/shard_map/ppermute | solution.py:440
  14.2 19.4 %collective-permute-start.3 = (f32[2,3,32,512]{3,2,1,0:T(8,128)S(1)}, f32[2,3,32,512]{3,2,1,0:T(8,128)S(1)}, u32[]{:S(2)}, u32[]{:S(2)}) collective-permute-start(f32[2,3,32,512]{3,2,1,0:T(8,128)S(1)} %get-tuple-element.27), channel_id=1, source_target_pairs={{0,4},{4,8},{8,12},{12,16},{16,20},{20,24},{24,28},{1,5},{5,9},{9,... | collective-permute-start | bytes 1179656 | tf_op jit(solution)/shard_map/ppermute | solution.py:464
  17.5 16.0 %collective-permute-start.4 = (f32[2,3,32,512]{3,2,1,0:T(8,128)S(1)}, f32[2,3,32,512]{3,2,1,0:T(8,128)S(1)}, u32[]{:S(2)}, u32[]{:S(2)}) collective-permute-start(f32[2,3,32,512]{3,2,1,0:T(8,128)S(1)} %get-tuple-element.28), channel_id=1, source_target_pairs={{4,0},{8,4},{12,8},{16,12},{20,16},{24,20},{28,24},{5,1},{9,5},{13... | collective-permute-start | bytes 1179656 | tf_op jit(solution)/shard_map/ppermute | solution.py:464
  24.0 9.7 %copy-start.2 = (f32[2,7,32,512]{3,2,1,0:T(8,128)}, f32[2,7,32,512]{3,2,1,0:T(8,128)S(1)}, u32[]{:S(2)}) copy-start(f32[2,7,32,512]{3,2,1,0:T(8,128)S(1)} %collective-permute-done.across) | copy-start | bytes 2752516
  24.9 8.9 %collective-permute-start.2 = (f32[7,32,512]{2,1,0:T(8,128)}, f32[7,32,512]{2,1,0:T(8,128)S(1)}, u32[]{:S(2)}, u32[]{:S(2)}) collective-permute-start(f32[7,32,512]{2,1,0:T(8,128)} %dynamic-slice_bitcast_fusion.2), channel_id=1, source_target_pairs={{0,1},{1,0},{2,3},{3,2},{4,5},{5,4},{6,7},{7,6},{8,9},{9,8},{10,11... | collective-permute-start | bytes 1376264 | tf_op jit(solution)/shard_map/ppermute | solution.py:440
  43.4 25.6 %collective-permute-start.9 = (f32[2,7,32,512]{3,2,1,0:T(8,128)}, f32[2,7,32,512]{3,2,1,0:T(8,128)}, u32[]{:S(2)}, u32[]{:S(2)}) collective-permute-start(f32[2,7,32,512]{3,2,1,0:T(8,128)} %get-tuple-element.42), channel_id=1, source_target_pairs={{0,2},{2,0},{1,3},{3,1},{4,6},{6,4},{5,7},{7,5},{8,10},{10,8},{9,1... | collective-permute-start | bytes 2752520 | tf_op jit(solution)/shard_map/ppermute | solution.py:440
  49.4 3.5 %collective-permute-start.7 = (f32[7,32,512]{2,1,0:T(8,128)S(1)}, f32[7,32,512]{2,1,0:T(8,128)S(1)}, u32[]{:S(2)}, u32[]{:S(2)}) collective-permute-start(f32[7,32,512]{2,1,0:T(8,128)S(1)} %get-tuple-element.36), channel_id=1, source_target_pairs={{0,1},{1,0},{2,3},{3,2},{4,5},{5,4},{6,7},{7,6},{8,9},{9,8},{10,11... | collective-permute-start | bytes 1376264 | tf_op jit(solution)/shard_map/ppermute | solution.py:440
  64.2 0.8 copy-start
  65.0 10.2 %collective-permute-start.8 = (f32[9,32,512]{2,1,0:T(8,128)}, f32[9,32,512]{2,1,0:T(8,128)}, u32[]{:S(2)}, u32[]{:S(2)}) collective-permute-start(f32[9,32,512]{2,1,0:T(8,128)} %get-tuple-element.41), channel_id=1, source_target_pairs={{0,1},{1,0},{2,3},{3,2},{4,5},{5,4},{6,7},{7,6},{8,9},{9,8},{10,11... | collective-permute-start | bytes 1769480 | tf_op jit(solution)/shard_map/ppermute | solution.py:440
  65.4 19.5 %collective-permute-start.11 = (f32[9,32,512]{2,1,0:T(8,128)}, f32[9,32,512]{2,1,0:T(8,128)S(1)}, u32[]{:S(2)}, u32[]{:S(2)}) collective-permute-start(f32[9,32,512]{2,1,0:T(8,128)} %get-tuple-element.44), channel_id=1, source_target_pairs={{0,2},{2,0},{1,3},{3,1},{4,6},{6,4},{5,7},{7,5},{8,10},{10,8},{9,1... | collective-permute-start | bytes 1769480 | tf_op jit(solution)/shard_map/ppermute | solution.py:440
  71.2 4.0 %collective-permute-start.10 = (f32[7,32,512]{2,1,0:T(8,128)}, f32[7,32,512]{2,1,0:T(8,128)}, u32[]{:S(2)}, u32[]{:S(2)}) collective-permute-start(f32[7,32,512]{2,1,0:T(8,128)} %get-tuple-element.47), channel_id=1, source_target_pairs={{0,1},{1,0},{2,3},{3,2},{4,5},{5,4},{6,7},{7,6},{8,9},{9,8},{10,11... | collective-permute-start | bytes 1376264 | tf_op jit(solution)/shard_map/ppermute | solution.py:440
  73.3 19.8 %collective-permute-start.12 = (f32[7,32,512]{2,1,0:T(8,128)S(1)}, f32[7,32,512]{2,1,0:T(8,128)S(1)}, u32[]{:S(2)}, u32[]{:S(2)}) collective-permute-start(f32[7,32,512]{2,1,0:T(8,128)S(1)} %get-tuple-element.45), channel_id=1, source_target_pairs={{0,3},{3,0},{1,2},{2,1},{4,7},{7,4},{5,6},{6,5},{8,11},{11,8},{9,1... | collective-permute-start | bytes 1376264 | tf_op jit(solution)/shard_map/ppermute | solution.py:440
  74.9 20.6 %collective-permute-start.13 = (f32[2,32,512]{2,1,0:T(8,128)S(1)}, f32[2,32,512]{2,1,0:T(8,128)S(1)}, u32[]{:S(2)}, u32[]{:S(2)}) collective-permute-start(f32[2,32,512]{2,1,0:T(8,128)S(1)} %get-tuple-element.46), channel_id=1, source_target_pairs={{0,3},{3,0},{1,2},{2,1},{4,7},{7,4},{5,6},{6,5},{8,11},{11,8},{9,1... | collective-permute-start | bytes 393224 | tf_op jit(solution)/shard_map/ppermute | solution.py:440

commit v7 on v6

--- a/solution.py
+++ b/solution.py
@@ -136,7 +136,7 @@
 
 
 CHUNKS = (7, 9)
-LAST = (7, 2)
+LAST = (6, 3)
 TO_Y = [(0, 2), (2, 0), (1, 3), (3, 1)]
 TO_C = [(0, 1), (1, 0), (2, 3), (3, 2)]
 TO_YC = [(0, 3), (3, 0), (1, 2), (2, 1)]
@@ -513,8 +513,9 @@
     placed = (P(None, None, "lat", "azim"), P())
 
     def run(magnetic, kept_modes):
-        radii, ph_dev = magnetic.shape[1], magnetic.shape[3]
+        radii, th_dev, ph_dev = magnetic.shape[1:]
         four = lax.axis_size("azim") == 4 and radii % (2 * sum(CHUNKS)) == 0 and ph_dev % 256 == 0
+        four = four and th_dev % 8 == 0
         return (on_four if four else on_device)(magnetic, kept_modes)
 
     return jax.shard_map(

time: 97.3 us -> 96.6 us (level)
  transfers between devices with their start and end apart: 14 -> 14, of which waited for: 6 -> 7; matrix products, arithmetic and copies ran while one was open for 13% -> 13% of each run, Pallas kernels for 37% -> 38%
where the time goes in v7:
time: 96.6 us; the launch traced here: 96 us
  Pallas kernels  39 us (40%)
  waiting for transfers between devices  24.1 us (25%)
  starting transfers between devices  19.2 us (20%)
  local copies, waits for them, and re-layouts  10.8 us (11%)
  other arithmetic  2.64 us (3%)
    pallas_call x2, Pallas kernels, transform(): pl.pallas_call(transform_kernel, grid_spec=grid_spec, out_shape=[jax.Shap...  20.8 us
    ppermute x12, waiting for transfers between devices, on_four(): send = lambda value, pairs: lax.ppermute(value, 'azim', pairs)  18.2 us
    ppermute x12, starting transfers between devices, on_four(): send = lambda value, pairs: lax.ppermute(value, 'azim', pairs)  14.5 us
    pallas_call x1, Pallas kernels, local_part(): pl.pallas_call(kernel, grid_spec=pltpu.PrefetchScalarGridSpec(num_scalar_...  8.77 us
    squeeze x4, local copies, waits for them, and re-layouts, cut(): lax.dynamic_slice(source, (field, start, 0, 0), (1, length, th_dev, ph_dev))  6.01 us
    ppermute x1, waiting for transfers between devices, on_four(): lax.ppermute(last, 'lat', up)  5.97 us
    pallas_call x2, Pallas kernels, add_one(): pl.pallas_call(kernel, grid_spec=pltpu.PrefetchScalarGridSpec(num_scalar_...  4.81 us
    ppermute x1, starting transfers between devices, on_four(): lax.ppermute(last, 'lat', up)  3.35 us
  transfers between devices with their start and end apart: 14, of which 7 were waited for; matrix products, arithmetic and copies ran while one was open for 13% of the time, Pallas kernels for 38%

profile of v7, /device:TPU:1, one launch (start us, length us, event | category | flops | bytes accessed | tf_op | source)
XLA Modules:
  0.0 96.0 jit_solution(17995792629484959847)
XLA Ops:
  0.0 0.1 pad_add_fusion.place
  0.1 1.7 %shard_map.91 = f32[2,7,32,512]{3,2,1,0:T(8,128)S(1)} custom-call(s32[2]{0:T(128)S(1)} %pad_add_fusion.place, f32[3,32,32,512]{3,2,1,0:T(8,128)} %field.1), custom_call_target="tpu_custom_call" | custom-call | flops 1 | bytes 1 | tf_op jit(solution)/shard_map/pallas_call | solution.py:295
  1.8 2.1 %collective-permute-start = (f32[2,7,32,512]{3,2,1,0:T(8,128)S(1)}, f32[2,7,32,512]{3,2,1,0:T(8,128)S(1)}, u32[]{:S(2)}, u32[]{:S(2)}) collective-permute-start(f32[2,7,32,512]{3,2,1,0:T(8,128)S(1)} %shard_map.91), channel_id=1, source_target_pairs={{0,2},{2,0},{1,3},{3,1},{4,6},{6,4},{5,7},{7,5},{8,10},{10,8},{9,1... | collective-permute-start | bytes 2752520 | tf_op jit(solution)/shard_map/ppermute | solution.py:440
  3.9 1.6 %shard_map.92 = (f32[2,3,32,512]{3,2,1,0:T(8,128)S(1)}, f32[2,3,32,512]{3,2,1,0:T(8,128)S(1)}) custom-call(f32[3,32,32,512]{3,2,1,0:T(8,128)} %field.1, f32[3,32,32,512]{3,2,1,0:T(8,128)} %field.1), custom_call_target="tpu_custom_call" | custom-call | flops 1 | bytes 1 | tf_op jit(solution)/shard_map/pallas_call | solution.py:270
  5.6 0.0 copy-start.3
  5.6 0.0 copy-start.1
  5.6 1.9 %dynamic-slice_bitcast_fusion.1 = f32[9,32,512]{2,1,0:T(8,128)} fusion(f32[3,32,32,512]{3,2,1,0:T(8,128)} %field.1, s32[]{:T(128)S(6)} %select_n.38, s32[]{:T(128)S(6)} %select_n.39), kind=kLoop, calls=%fused_computation.2 | loop fusion | bytes 1179656 | tf_op jit(solution)/shard_map/squeeze | solution.py:443
  7.5 1.0 collective-permute-start.5
  8.5 2.3 %dynamic-slice_bitcast_fusion = f32[16,32,512]{2,1,0:T(8,128)} fusion(f32[3,32,32,512]{3,2,1,0:T(8,128)} %field.1, s32[]{:T(128)S(6)} %select_n.38, s32[]{:T(128)S(6)} %select_n.40), kind=kLoop, calls=%fused_computation.1 | loop fusion | bytes 2097160 | tf_op jit(solution)/shard_map/squeeze | solution.py:443
  10.8 0.0 collective-permute-start.1
  10.8 1.1 %constant_dynamic-slice_fusion = f32[1,9,32,512]{3,2,1,0:T(8,128)S(1)} fusion(f32[3,32,32,512]{3,2,1,0:T(8,128)} %field.1, s32[]{:T(128)S(6)} %select_n.43, s32[]{:T(128)S(6)} %select_n.39), kind=kLoop, calls=%fused_computation.11 | loop fusion | bytes 1179656 | tf_op jit(solution)/shard_map/dynamic_slice | solution.py:443
  11.9 0.0 collective-permute-done.5
  11.9 2.2 %pad_maximum_fusion = f32[2,9,32,512]{3,2,1,0:T(8,128)} fusion(f32[1,9,32,512]{3,2,1,0:T(8,128)} %bitcast.5, f32[1,9,32,512]{3,2,1,0:T(8,128)S(1)} %constant_dynamic-slice_fusion), kind=kLoop, calls=%fused_computation | loop fusion | flops 294912 | bytes 2359296 | tf_op jit(solution)/shard_map/stack | solution.py:459
  14.2 3.4 %collective-permute-start.3 = (f32[2,3,32,512]{3,2,1,0:T(8,128)S(1)}, f32[2,3,32,512]{3,2,1,0:T(8,128)S(1)}, u32[]{:S(2)}, u32[]{:S(2)}) collective-permute-start(f32[2,3,32,512]{3,2,1,0:T(8,128)S(1)} %get-tuple-element.27), channel_id=1, source_target_pairs={{0,4},{4,8},{8,12},{12,16},{16,20},{20,24},{24,28},{1,5},{5,9},{9,... | collective-permute-start | bytes 1179656 | tf_op jit(solution)/shard_map/ppermute | solution.py:464
  17.5 1.3 %collective-permute-start.4 = (f32[2,3,32,512]{3,2,1,0:T(8,128)S(1)}, f32[2,3,32,512]{3,2,1,0:T(8,128)S(1)}, u32[]{:S(2)}, u32[]{:S(2)}) collective-permute-start(f32[2,3,32,512]{3,2,1,0:T(8,128)S(1)} %get-tuple-element.28), channel_id=1, source_target_pairs={{4,0},{8,4},{12,8},{16,12},{20,16},{24,20},{28,24},{5,1},{9,5},{13... | collective-permute-start | bytes 1179656 | tf_op jit(solution)/shard_map/ppermute | solution.py:464
  18.8 5.2 %collective-permute-done.across = f32[2,7,32,512]{3,2,1,0:T(8,128)S(1)} collective-permute-done((f32[2,7,32,512]{3,2,1,0:T(8,128)S(1)}, f32[2,7,32,512]{3,2,1,0:T(8,128)S(1)}, u32[]{:S(2)}, u32[]{:S(2)}) %collective-permute-start) | collective-permute-done | bytes 917536 | tf_op jit(solution)/shard_map/ppermute | solution.py:440
  24.0 0.9 dynamic-slice_bitcast_fusion.2
  24.9 2.1 %collective-permute-start.2 = (f32[7,32,512]{2,1,0:T(8,128)}, f32[7,32,512]{2,1,0:T(8,128)S(1)}, u32[]{:S(2)}, u32[]{:S(2)}) collective-permute-start(f32[7,32,512]{2,1,0:T(8,128)} %dynamic-slice_bitcast_fusion.2), channel_id=1, source_target_pairs={{0,1},{1,0},{2,3},{3,2},{4,5},{5,4},{6,7},{7,6},{8,9},{9,8},{10,11... | collective-permute-start | bytes 1376264 | tf_op jit(solution)/shard_map/ppermute | solution.py:440
  26.9 0.1 dynamic-slice
  27.1 0.1 broadcast_multiply_fusion
  27.1 0.1 reshape.73
  27.2 0.1 dynamic-slice_convert_fusion
  27.3 0.3 reshape.74.kept
  27.6 6.0 %collective-permute-done.3.before = f32[2,3,32,512]{3,2,1,0:T(8,128)S(1)} collective-permute-done((f32[2,3,32,512]{3,2,1,0:T(8,128)S(1)}, f32[2,3,32,512]{3,2,1,0:T(8,128)S(1)}, u32[]{:S(2)}, u32[]{:S(2)}) %collective-permute-start.3) | collective-permute-done | bytes 393248 | tf_op jit(solution)/shard_map/ppermute | solution.py:464
  33.6 0.1 copy.18.gain
  33.7 9.7 %shard_map.93 = (f32[7,32,512]{2,1,0:T(8,128)S(1)}, f32[7,32,512]{2,1,0:T(8,128)S(1)}, f32[2,7,32,512]{3,2,1,0:T(8,128)}) custom-call(s32[2]{0:T(128)S(1)} %pad_add_fusion.place, f32[3,32,32,512]{3,2,1,0:T(8,128)} %field.1, f32[2,7,32,512]{3,2,1,0:T(8,128)} %copy-done.2, f32[16,32,512]{2,1,0:T(8,128)} %collective-permute-done.1.beside, ...), custom_call_target="tpu_custom_call" | custom-call | flops 1 | bytes 1 | tf_op jit(solution)/shard_map/pallas_call | solution.py:251
  43.4 1.3 %collective-permute-start.9 = (f32[2,7,32,512]{3,2,1,0:T(8,128)}, f32[2,7,32,512]{3,2,1,0:T(8,128)}, u32[]{:S(2)}, u32[]{:S(2)}) collective-permute-start(f32[2,7,32,512]{3,2,1,0:T(8,128)} %get-tuple-element.42), channel_id=1, source_target_pairs={{0,2},{2,0},{1,3},{3,1},{4,6},{6,4},{5,7},{7,5},{8,10},{10,8},{9,1... | collective-permute-start | bytes 2752520 | tf_op jit(solution)/shard_map/ppermute | solution.py:440
  44.7 4.6 %collective-permute-done.6.across.diagonal = f32[2,9,32,512]{3,2,1,0:T(8,128)} collective-permute-done((f32[2,9,32,512]{3,2,1,0:T(8,128)}, f32[2,9,32,512]{3,2,1,0:T(8,128)}, u32[]{:S(2)}, u32[]{:S(2)}) %collective-permute-start.6) | collective-permute-done | bytes 1179680 | tf_op jit(solution)/shard_map/ppermute | solution.py:440
  49.4 2.1 %collective-permute-start.7 = (f32[7,32,512]{2,1,0:T(8,128)S(1)}, f32[7,32,512]{2,1,0:T(8,128)S(1)}, u32[]{:S(2)}, u32[]{:S(2)}) collective-permute-start(f32[7,32,512]{2,1,0:T(8,128)S(1)} %get-tuple-element.36), channel_id=1, source_target_pairs={{0,1},{1,0},{2,3},{3,2},{4,5},{5,4},{6,7},{7,6},{8,9},{9,8},{10,11... | collective-permute-start | bytes 1376264 | tf_op jit(solution)/shard_map/ppermute | solution.py:440
  51.5 1.4 %collective-permute-done.7.refs_1_ = f32[7,32,512]{2,1,0:T(8,128)S(1)} collective-permute-done((f32[7,32,512]{2,1,0:T(8,128)S(1)}, f32[7,32,512]{2,1,0:T(8,128)S(1)}, u32[]{:S(2)}, u32[]{:S(2)}) %collective-permute-start.7) | collective-permute-done | bytes 458784 | tf_op jit(solution)/shard_map/ppermute | solution.py:440
  52.9 0.1 copy.20.gain
  53.0 11.2 %shard_map.94 = (f32[9,32,512]{2,1,0:T(8,128)S(1)}, f32[9,32,512]{2,1,0:T(8,128)}, f32[9,32,512]{2,1,0:T(8,128)}, f32[6,32,512]{2,1,0:T(8,128)S(1)}, f32[3,32,512]{2,1,0:T(8,128)S(1)}) custom-call(s32[2]{0:T(128)S(1)} %pad_add_fusion.place, f32[3,32,32,512]{3,2,1,0:T(8,128)} %field.1, f32[2,9,32,512]{3,2,1,0:T(8,128)} %collective-permute-done.6.across.diagonal, ...), custom_call_target="tpu_custom_call" | custom-call | flops 1 | bytes 1 | tf_op jit(solution)/shard_map/pallas_call | solution.py:251
  64.2 0.8 copy-done
  65.0 0.4 collective-permute-start.8
  65.4 1.8 %collective-permute-start.11 = (f32[9,32,512]{2,1,0:T(8,128)}, f32[9,32,512]{2,1,0:T(8,128)S(1)}, u32[]{:S(2)}, u32[]{:S(2)}) collective-permute-start(f32[9,32,512]{2,1,0:T(8,128)} %get-tuple-element.44), channel_id=1, source_target_pairs={{0,2},{2,0},{1,3},{3,1},{4,6},{6,4},{5,7},{7,5},{8,10},{10,8},{9,1... | collective-permute-start | bytes 1769480 | tf_op jit(solution)/shard_map/ppermute | solution.py:440
  67.2 1.9 %collective-permute-done.9 = f32[2,7,32,512]{3,2,1,0:T(8,128)} collective-permute-done((f32[2,7,32,512]{3,2,1,0:T(8,128)}, f32[2,7,32,512]{3,2,1,0:T(8,128)}, u32[]{:S(2)}, u32[]{:S(2)}) %collective-permute-start.9) | collective-permute-done | bytes 917536 | tf_op jit(solution)/shard_map/ppermute | solution.py:440
  69.1 2.2 %slice_bitcast_fusion = (f32[7,32,512]{2,1,0:T(8,128)}, f32[7,32,512]{2,1,0:T(8,128)}) fusion(f32[2,7,32,512]{3,2,1,0:T(8,128)} %collective-permute-done.9), kind=kLoop, calls=%fused_computation.3 | loop fusion | bytes 1835008 | tf_op jit(solution)/shard_map/squeeze | solution.py:501
  71.2 2.1 %collective-permute-start.10 = (f32[7,32,512]{2,1,0:T(8,128)}, f32[7,32,512]{2,1,0:T(8,128)}, u32[]{:S(2)}, u32[]{:S(2)}) collective-permute-start(f32[7,32,512]{2,1,0:T(8,128)} %get-tuple-element.47), channel_id=1, source_target_pairs={{0,1},{1,0},{2,3},{3,2},{4,5},{5,4},{6,7},{7,6},{8,9},{9,8},{10,11... | collective-permute-start | bytes 1376264 | tf_op jit(solution)/shard_map/ppermute | solution.py:440
  73.3 1.6 %collective-permute-start.12 = (f32[6,32,512]{2,1,0:T(8,128)S(1)}, f32[6,32,512]{2,1,0:T(8,128)S(1)}, u32[]{:S(2)}, u32[]{:S(2)}) collective-permute-start(f32[6,32,512]{2,1,0:T(8,128)S(1)} %get-tuple-element.45), channel_id=1, source_target_pairs={{0,3},{3,0},{1,2},{2,1},{4,7},{7,4},{5,6},{6,5},{8,11},{11,8},{9,1... | collective-permute-start | bytes 1179656 | tf_op jit(solution)/shard_map/ppermute | solution.py:440
  74.9 0.2 collective-permute-start.13
  75.1 0.1 divide_multiply_fusion.cot
  75.2 8.8 %shard_map.95.base = f32[3,32,32,512]{3,2,1,0:T(8,128)} custom-call(s32[2]{0:T(128)S(1)} %pad_add_fusion.place, f32[3,32,32,512]{3,2,1,0:T(8,128)} %field.1, f32[2,3,32,512]{3,2,1,0:T(8,128)S(1)} %collective-permute-done.3.before, f32[2,3,32,512]{3,2,1,0:T(8,128)S(1)} %collective-permute-done.4.after, f32[32,1,1]{2,1,0:T(1,128)S(1)} %get-tuple-element.49.radius, ...), custom_call_target="tpu_custom_call" | custom-call | flops 1 | bytes 1 | tf_op jit(solution)/shard_map/pallas_call | solution.py:346
  84.0 0.9 dynamic-slice_bitcast_fusion.3.base
  84.9 2.5 %shard_map.96.base = f32[3,32,32,512]{3,2,1,0:T(8,128)} custom-call(s32[2]{0:T(128)S(1)} %pad_add_fusion.place, f32[3,32,32,512]{3,2,1,0:T(8,128)} %shard_map.95.base, f32[9,32,512]{2,1,0:T(8,128)S(1)} %collective-permute-done.11.azim), custom_call_target="tpu_custom_call", output_to_operand_aliasing={{}: (1, {})} | custom-call | flops 1 | bytes 1 | tf_op jit(solution)/shard_map/pallas_call | solution.py:384
  87.4 4.3 %collective-permute-done.12.azim = f32[6,32,512]{2,1,0:T(8,128)S(1)} collective-permute-done((f32[6,32,512]{2,1,0:T(8,128)S(1)}, f32[6,32,512]{2,1,0:T(8,128)S(1)}, u32[]{:S(2)}, u32[]{:S(2)}) %collective-permute-start.12) | collective-permute-done | bytes 393248 | tf_op jit(solution)/shard_map/ppermute | solution.py:440
  91.7 2.3 %shard_map.97.current = f32[3,32,32,512]{3,2,1,0:T(8,128)} custom-call(s32[2]{0:T(128)S(1)} %pad_add_fusion.place, f32[3,32,32,512]{3,2,1,0:T(8,128)} %shard_map.96.base, f32[6,32,512]{2,1,0:T(8,128)S(1)} %collective-permute-done.12.azim), custom_call_target="tpu_custom_call", output_to_operand_aliasing={{}: (1, {})} | custom-call | flops 1 | bytes 1 | tf_op jit(solution)/shard_map/pallas_call | solution.py:384
  94.0 0.8 collective-permute-done.13.azim
  94.8 1.2 %shard_map.98 = f32[3,32,32,512]{3,2,1,0:T(8,128)} custom-call(s32[2]{0:T(128)S(1)} %pad_add_fusion.place, f32[3,32,32,512]{3,2,1,0:T(8,128)} %shard_map.97.current, f32[3,32,512]{2,1,0:T(8,128)S(1)} %dynamic-slice_bitcast_fusion.3.base, f32[3,32,512]{2,1,0:T(8,128)S(1)} %collective-permute-done.13.azim), custom_call_target="tpu_custom_call", output_to_operand_aliasing={{}: (1, {})} | custom-call | flops 1 | bytes 1 | tf_op jit(solution)/shard_map/pallas_call | solution.py:410
  (16 shorter events, 0.1 us)
Async XLA Ops:
  1.8 22.2 %collective-permute-start = (f32[2,7,32,512]{3,2,1,0:T(8,128)S(1)}, f32[2,7,32,512]{3,2,1,0:T(8,128)S(1)}, u32[]{:S(2)}, u32[]{:S(2)}) collective-permute-start(f32[2,7,32,512]{3,2,1,0:T(8,128)S(1)} %shard_map.91), channel_id=1, source_target_pairs={{0,2},{2,0},{1,3},{3,1},{4,6},{6,4},{5,7},{7,5},{8,10},{10,8},{9,1... | collective-permute-start | bytes 2752520 | tf_op jit(solution)/shard_map/ppermute | solution.py:440
  5.6 21.7 %copy-start.3 = (s32[256]{0:T(256)S(1)}, s32[256]{0:T(256)}, u32[]{:S(2)}) copy-start(s32[256]{0:T(256)} %param.10) | copy-start | bytes 3076
  5.6 28.2 %copy-start.1 = (f32[1,2048]{1,0:T(1,128)S(1)}, f32[1,2048]{1,0:T(1,128)}, u32[]{:S(2)}) copy-start(f32[1,2048]{1,0:T(1,128)} %constant.85.clone.modes) | copy-start | bytes 24580
  7.5 4.4 %collective-permute-start.5 = (f32[9,32,512]{2,1,0:T(8,128)}, f32[9,32,512]{2,1,0:T(8,128)}, u32[]{:S(2)}, u32[]{:S(2)}) collective-permute-start(f32[9,32,512]{2,1,0:T(8,128)} %dynamic-slice_bitcast_fusion.1), channel_id=1, source_target_pairs={{0,1},{1,0},{2,3},{3,2},{4,5},{5,4},{6,7},{7,6},{8,9},{9,8},{10,11... | collective-permute-start | bytes 1769480 | tf_op jit(solution)/shard_map/ppermute | solution.py:440
  10.8 22.9 %collective-permute-start.1 = (f32[16,32,512]{2,1,0:T(8,128)}, f32[16,32,512]{2,1,0:T(8,128)}, u32[]{:S(2)}, u32[]{:S(2)}) collective-permute-start(f32[16,32,512]{2,1,0:T(8,128)} %dynamic-slice_bitcast_fusion), channel_id=1, source_target_pairs={{0,1},{1,0},{2,3},{3,2},{4,5},{5,4},{6,7},{7,6},{8,9},{9,8},{10,11... | collective-permute-start | bytes 3145736 | tf_op jit(solution)/shard_map/ppermute | solution.py:440
  14.2 35.2 %collective-permute-start.6 = (f32[2,9,32,512]{3,2,1,0:T(8,128)}, f32[2,9,32,512]{3,2,1,0:T(8,128)}, u32[]{:S(2)}, u32[]{:S(2)}) collective-permute-start(f32[2,9,32,512]{3,2,1,0:T(8,128)} %pad_maximum_fusion), channel_id=1, source_target_pairs={{0,2},{2,0},{1,3},{3,1},{4,6},{6,4},{5,7},{7,5},{8,10},{10,8},{9,1... | collective-permute-start | bytes 3538952 | tf_op jit(solution)/shard_map/ppermute | solution.py:440
  14.2 19.4 %collective-permute-start.3 = (f32[2,3,32,512]{3,2,1,0:T(8,128)S(1)}, f32[2,3,32,512]{3,2,1,0:T(8,128)S(1)}, u32[]{:S(2)}, u32[]{:S(2)}) collective-permute-start(f32[2,3,32,512]{3,2,1,0:T(8,128)S(1)} %get-tuple-element.27), channel_id=1, source_target_pairs={{0,4},{4,8},{8,12},{12,16},{16,20},{20,24},{24,28},{1,5},{5,9},{9,... | collective-permute-start | bytes 1179656 | tf_op jit(solution)/shard_map/ppermute | solution.py:464
  17.5 16.0 %collective-permute-start.4 = (f32[2,3,32,512]{3,2,1,0:T(8,128)S(1)}, f32[2,3,32,512]{3,2,1,0:T(8,128)S(1)}, u32[]{:S(2)}, u32[]{:S(2)}) collective-permute-start(f32[2,3,32,512]{3,2,1,0:T(8,128)S(1)} %get-tuple-element.28), channel_id=1, source_target_pairs={{4,0},{8,4},{12,8},{16,12},{20,16},{24,20},{28,24},{5,1},{9,5},{13... | collective-permute-start | bytes 1179656 | tf_op jit(solution)/shard_map/ppermute | solution.py:464
  24.0 9.7 %copy-start.2 = (f32[2,7,32,512]{3,2,1,0:T(8,128)}, f32[2,7,32,512]{3,2,1,0:T(8,128)S(1)}, u32[]{:S(2)}) copy-start(f32[2,7,32,512]{3,2,1,0:T(8,128)S(1)} %collective-permute-done.across) | copy-start | bytes 2752516
  24.9 8.9 %collective-permute-start.2 = (f32[7,32,512]{2,1,0:T(8,128)}, f32[7,32,512]{2,1,0:T(8,128)S(1)}, u32[]{:S(2)}, u32[]{:S(2)}) collective-permute-start(f32[7,32,512]{2,1,0:T(8,128)} %dynamic-slice_bitcast_fusion.2), channel_id=1, source_target_pairs={{0,1},{1,0},{2,3},{3,2},{4,5},{5,4},{6,7},{7,6},{8,9},{9,8},{10,11... | collective-permute-start | bytes 1376264 | tf_op jit(solution)/shard_map/ppermute | solution.py:440
  43.4 25.6 %collective-permute-start.9 = (f32[2,7,32,512]{3,2,1,0:T(8,128)}, f32[2,7,32,512]{3,2,1,0:T(8,128)}, u32[]{:S(2)}, u32[]{:S(2)}) collective-permute-start(f32[2,7,32,512]{3,2,1,0:T(8,128)} %get-tuple-element.42), channel_id=1, source_target_pairs={{0,2},{2,0},{1,3},{3,1},{4,6},{6,4},{5,7},{7,5},{8,10},{10,8},{9,1... | collective-permute-start | bytes 2752520 | tf_op jit(solution)/shard_map/ppermute | solution.py:440
  49.4 3.5 %collective-permute-start.7 = (f32[7,32,512]{2,1,0:T(8,128)S(1)}, f32[7,32,512]{2,1,0:T(8,128)S(1)}, u32[]{:S(2)}, u32[]{:S(2)}) collective-permute-start(f32[7,32,512]{2,1,0:T(8,128)S(1)} %get-tuple-element.36), channel_id=1, source_target_pairs={{0,1},{1,0},{2,3},{3,2},{4,5},{5,4},{6,7},{7,6},{8,9},{9,8},{10,11... | collective-permute-start | bytes 1376264 | tf_op jit(solution)/shard_map/ppermute | solution.py:440
  64.2 0.8 copy-start
  65.0 10.2 %collective-permute-start.8 = (f32[9,32,512]{2,1,0:T(8,128)}, f32[9,32,512]{2,1,0:T(8,128)}, u32[]{:S(2)}, u32[]{:S(2)}) collective-permute-start(f32[9,32,512]{2,1,0:T(8,128)} %get-tuple-element.41), channel_id=1, source_target_pairs={{0,1},{1,0},{2,3},{3,2},{4,5},{5,4},{6,7},{7,6},{8,9},{9,8},{10,11... | collective-permute-start | bytes 1769480 | tf_op jit(solution)/shard_map/ppermute | solution.py:440
  65.4 19.5 %collective-permute-start.11 = (f32[9,32,512]{2,1,0:T(8,128)}, f32[9,32,512]{2,1,0:T(8,128)S(1)}, u32[]{:S(2)}, u32[]{:S(2)}) collective-permute-start(f32[9,32,512]{2,1,0:T(8,128)} %get-tuple-element.44), channel_id=1, source_target_pairs={{0,2},{2,0},{1,3},{3,1},{4,6},{6,4},{5,7},{7,5},{8,10},{10,8},{9,1... | collective-permute-start | bytes 1769480 | tf_op jit(solution)/shard_map/ppermute | solution.py:440
  71.2 4.0 %collective-permute-start.10 = (f32[7,32,512]{2,1,0:T(8,128)}, f32[7,32,512]{2,1,0:T(8,128)}, u32[]{:S(2)}, u32[]{:S(2)}) collective-permute-start(f32[7,32,512]{2,1,0:T(8,128)} %get-tuple-element.47), channel_id=1, source_target_pairs={{0,1},{1,0},{2,3},{3,2},{4,5},{5,4},{6,7},{7,6},{8,9},{9,8},{10,11... | collective-permute-start | bytes 1376264 | tf_op jit(solution)/shard_map/ppermute | solution.py:440
  73.3 18.4 %collective-permute-start.12 = (f32[6,32,512]{2,1,0:T(8,128)S(1)}, f32[6,32,512]{2,1,0:T(8,128)S(1)}, u32[]{:S(2)}, u32[]{:S(2)}) collective-permute-start(f32[6,32,512]{2,1,0:T(8,128)S(1)} %get-tuple-element.45), channel_id=1, source_target_pairs={{0,3},{3,0},{1,2},{2,1},{4,7},{7,4},{5,6},{6,5},{8,11},{11,8},{9,1... | collective-permute-start | bytes 1179656 | tf_op jit(solution)/shard_map/ppermute | solution.py:440
  74.9 19.9 %collective-permute-start.13 = (f32[3,32,512]{2,1,0:T(8,128)S(1)}, f32[3,32,512]{2,1,0:T(8,128)S(1)}, u32[]{:S(2)}, u32[]{:S(2)}) collective-permute-start(f32[3,32,512]{2,1,0:T(8,128)S(1)} %get-tuple-element.46), channel_id=1, source_target_pairs={{0,3},{3,0},{1,2},{2,1},{4,7},{7,4},{5,6},{6,5},{8,11},{11,8},{9,1... | collective-permute-start | bytes 589832 | tf_op jit(solution)/shard_map/ppermute | solution.py:440

commit v8 on v7

--- a/solution.py
+++ b/solution.py
@@ -144,10 +144,12 @@
 SHORT = pl.CostEstimate(flops=1, bytes_accessed=1, transcendentals=0)
 
 
-def halves(table):
-    high = table.astype(jnp.bfloat16)
-    low = (table - high.astype(np.float64)).astype(jnp.bfloat16)
-    return np.stack([high, low])
+def split_table(table, count):
+    parts = []
+    for _ in range(count):
+        parts.append(table.astype(jnp.bfloat16))
+        table = table - parts[-1].astype(np.float64)
+    return np.stack(parts)
 
 
 def mode_tables(lon_total):
@@ -157,7 +159,7 @@
         phase = (np.arange(length)[:, None] * modes[None, :] % lon_total) * (2.0 * np.pi / lon_total)
         forward = np.concatenate([np.cos(phase), np.sin(phase)], axis=1)
         inverse = np.concatenate([-np.sin(phase), np.cos(phase)], axis=1).T
-        return halves(forward), halves(inverse)
+        return split_table(forward, 3), split_table(inverse, 2)
 
     zero = 4 * np.arange(quarter // 2)
     two = zero + 2
@@ -166,11 +168,18 @@
     return pair(zero, quarter), pair(two, quarter), pair(odd, 2 * quarter), mode_ids
 
 
-def triple_dot(value, table):
-    high = value.astype(jnp.bfloat16)
-    low = (value - high.astype(jnp.float32)).astype(jnp.bfloat16)
-    dot = functools.partial(jnp.dot, preferred_element_type=jnp.float32)
-    return dot(high, table[0]) + dot(high, table[1]) + dot(low, table[0])
+def split_dot(value, table):
+    count = table.shape[0]
+    parts = []
+    for _ in range(count):
+        parts.append(value.astype(jnp.bfloat16))
+        value = value - parts[-1].astype(jnp.float32)
+    total = None
+    for order in reversed(range(count)):
+        for i in range(order + 1):
+            term = jnp.dot(parts[i], table[order - i], preferred_element_type=jnp.float32)
+            total = term if total is None else total + term
+    return total
 
 
 def transform_kernel(place, own, across, beside, diagonal, kept, gain, modes, *refs):
@@ -193,9 +202,9 @@
 
     def filtered(value, which, start):
         copies[2 * which].wait()
-        spectrum = triple_dot(value, held[2 * which])
+        spectrum = split_dot(value, held[2 * which])
         copies[2 * which + 1].wait()
-        return triple_dot(spectrum * weight[:, start : start + spectrum.shape[1]], held[2 * which + 1])
+        return split_dot(spectrum * weight[:, start : start + spectrum.shape[1]], held[2 * which + 1])
 
     even0 = filtered(near + far, 0, 0)
     even2 = sign_c * filtered(sign_c * (near - far), 1, quarter)

time: 96.6 us -> 99.1 us (1.026)
  Pallas kernels: 39 us -> 44.5 us
  waiting for transfers between devices: 24.1 us -> 22.3 us
  starting transfers between devices: 19.2 us -> 17.6 us
    pallas_call x2, Pallas kernels: 20.8 us -> 26.3 us  [transform(): pl.pallas_call(transform_kernel, grid_spec=grid_spec, out_shape=[jax.Shap...]
    ppermute x12, waiting for transfers between devices: 18.2 us -> 16.3 us  [on_four(): send = lambda value, pairs: lax.ppermute(value, 'azim', pairs)]
    ppermute x12, starting transfers between devices: 14.5 us -> 12.9 us  [on_four(): send = lambda value, pairs: lax.ppermute(value, 'azim', pairs)]
  transfers between devices with their start and end apart: 14 -> 14, of which waited for: 7 -> 6; matrix products, arithmetic and copies ran while one was open for 13% -> 13% of each run, Pallas kernels for 38% -> 42%
where the time goes in v8:
time: 99.1 us; the launch traced here: 98.2 us
  Pallas kernels  44.5 us (45%)
  waiting for transfers between devices  22.3 us (23%)
  starting transfers between devices  17.6 us (18%)
  local copies, waits for them, and re-layouts  10.8 us (11%)
  other arithmetic  2.64 us (3%)
    pallas_call x2, Pallas kernels, transform(): pl.pallas_call(transform_kernel, grid_spec=grid_spec, out_shape=[jax.Shap...  26.3 us
    ppermute x12, waiting for transfers between devices, on_four(): send = lambda value, pairs: lax.ppermute(value, 'azim', pairs)  16.3 us
    ppermute x12, starting transfers between devices, on_four(): send = lambda value, pairs: lax.ppermute(value, 'azim', pairs)  12.9 us
    pallas_call x1, Pallas kernels, local_part(): pl.pallas_call(kernel, grid_spec=pltpu.PrefetchScalarGridSpec(num_scalar_...  8.77 us
    squeeze x4, local copies, waits for them, and re-layouts, cut(): lax.dynamic_slice(source, (field, start, 0, 0), (1, length, th_dev, ph_dev))  6.01 us
    ppermute x1, waiting for transfers between devices, on_four(): lax.ppermute(last, 'lat', up)  5.97 us
    pallas_call x2, Pallas kernels, add_one(): pl.pallas_call(kernel, grid_spec=pltpu.PrefetchScalarGridSpec(num_scalar_...  4.81 us
    ppermute x1, starting transfers between devices, on_four(): lax.ppermute(last, 'lat', up)  3.35 us
  transfers between devices with their start and end apart: 14, of which 6 were waited for; matrix products, arithmetic and copies ran while one was open for 13% of the time, Pallas kernels for 42%

profile of v8, /device:TPU:1, one launch (start us, length us, event | category | flops | bytes accessed | tf_op | source)
XLA Modules:
  0.0 98.2 jit_solution(4726663281743508191)
XLA Ops:
  0.0 0.1 pad_add_fusion.place
  0.1 1.7 %shard_map.91 = f32[2,7,32,512]{3,2,1,0:T(8,128)S(1)} custom-call(s32[2]{0:T(128)S(1)} %pad_add_fusion.place, f32[3,32,32,512]{3,2,1,0:T(8,128)} %field.1), custom_call_target="tpu_custom_call" | custom-call | flops 1 | bytes 1 | tf_op jit(solution)/shard_map/pallas_call | solution.py:304
  1.8 2.1 %collective-permute-start = (f32[2,7,32,512]{3,2,1,0:T(8,128)S(1)}, f32[2,7,32,512]{3,2,1,0:T(8,128)S(1)}, u32[]{:S(2)}, u32[]{:S(2)}) collective-permute-start(f32[2,7,32,512]{3,2,1,0:T(8,128)S(1)} %shard_map.91), channel_id=1, source_target_pairs={{0,2},{2,0},{1,3},{3,1},{4,6},{6,4},{5,7},{7,5},{8,10},{10,8},{9,1... | collective-permute-start | bytes 2752520 | tf_op jit(solution)/shard_map/ppermute | solution.py:449
  3.9 1.6 %shard_map.92 = (f32[2,3,32,512]{3,2,1,0:T(8,128)S(1)}, f32[2,3,32,512]{3,2,1,0:T(8,128)S(1)}) custom-call(f32[3,32,32,512]{3,2,1,0:T(8,128)} %field.1, f32[3,32,32,512]{3,2,1,0:T(8,128)} %field.1), custom_call_target="tpu_custom_call" | custom-call | flops 1 | bytes 1 | tf_op jit(solution)/shard_map/pallas_call | solution.py:279
  5.6 0.0 copy-start.3
  5.6 0.0 copy-start.1
  5.6 1.9 %dynamic-slice_bitcast_fusion.1 = f32[9,32,512]{2,1,0:T(8,128)} fusion(f32[3,32,32,512]{3,2,1,0:T(8,128)} %field.1, s32[]{:T(128)S(6)} %select_n.38, s32[]{:T(128)S(6)} %select_n.39), kind=kLoop, calls=%fused_computation.2 | loop fusion | bytes 1179656 | tf_op jit(solution)/shard_map/squeeze | solution.py:452
  7.5 1.0 collective-permute-start.5
  8.5 2.3 %dynamic-slice_bitcast_fusion = f32[16,32,512]{2,1,0:T(8,128)} fusion(f32[3,32,32,512]{3,2,1,0:T(8,128)} %field.1, s32[]{:T(128)S(6)} %select_n.38, s32[]{:T(128)S(6)} %select_n.40), kind=kLoop, calls=%fused_computation.1 | loop fusion | bytes 2097160 | tf_op jit(solution)/shard_map/squeeze | solution.py:452
  10.8 0.0 collective-permute-start.1
  10.8 1.1 %constant_dynamic-slice_fusion = f32[1,9,32,512]{3,2,1,0:T(8,128)S(1)} fusion(f32[3,32,32,512]{3,2,1,0:T(8,128)} %field.1, s32[]{:T(128)S(6)} %select_n.43, s32[]{:T(128)S(6)} %select_n.39), kind=kLoop, calls=%fused_computation.11 | loop fusion | bytes 1179656 | tf_op jit(solution)/shard_map/dynamic_slice | solution.py:452
  11.9 2.2 %pad_maximum_fusion = f32[2,9,32,512]{3,2,1,0:T(8,128)} fusion(f32[1,9,32,512]{3,2,1,0:T(8,128)} %bitcast.5, f32[1,9,32,512]{3,2,1,0:T(8,128)S(1)} %constant_dynamic-slice_fusion), kind=kLoop, calls=%fused_computation | loop fusion | flops 294912 | bytes 2359296 | tf_op jit(solution)/shard_map/stack | solution.py:468
  14.2 3.4 %collective-permute-start.3 = (f32[2,3,32,512]{3,2,1,0:T(8,128)S(1)}, f32[2,3,32,512]{3,2,1,0:T(8,128)S(1)}, u32[]{:S(2)}, u32[]{:S(2)}) collective-permute-start(f32[2,3,32,512]{3,2,1,0:T(8,128)S(1)} %get-tuple-element.27), channel_id=1, source_target_pairs={{0,4},{4,8},{8,12},{12,16},{16,20},{20,24},{24,28},{1,5},{5,9},{9,... | collective-permute-start | bytes 1179656 | tf_op jit(solution)/shard_map/ppermute | solution.py:473
  17.5 1.3 %collective-permute-start.4 = (f32[2,3,32,512]{3,2,1,0:T(8,128)S(1)}, f32[2,3,32,512]{3,2,1,0:T(8,128)S(1)}, u32[]{:S(2)}, u32[]{:S(2)}) collective-permute-start(f32[2,3,32,512]{3,2,1,0:T(8,128)S(1)} %get-tuple-element.28), channel_id=1, source_target_pairs={{4,0},{8,4},{12,8},{16,12},{20,16},{24,20},{28,24},{5,1},{9,5},{13... | collective-permute-start | bytes 1179656 | tf_op jit(solution)/shard_map/ppermute | solution.py:473
  18.8 5.2 %collective-permute-done.across = f32[2,7,32,512]{3,2,1,0:T(8,128)S(1)} collective-permute-done((f32[2,7,32,512]{3,2,1,0:T(8,128)S(1)}, f32[2,7,32,512]{3,2,1,0:T(8,128)S(1)}, u32[]{:S(2)}, u32[]{:S(2)}) %collective-permute-start) | collective-permute-done | bytes 917536 | tf_op jit(solution)/shard_map/ppermute | solution.py:449
  24.0 0.9 dynamic-slice_bitcast_fusion.2
  24.9 2.1 %collective-permute-start.2 = (f32[7,32,512]{2,1,0:T(8,128)}, f32[7,32,512]{2,1,0:T(8,128)S(1)}, u32[]{:S(2)}, u32[]{:S(2)}) collective-permute-start(f32[7,32,512]{2,1,0:T(8,128)} %dynamic-slice_bitcast_fusion.2), channel_id=1, source_target_pairs={{0,1},{1,0},{2,3},{3,2},{4,5},{5,4},{6,7},{7,6},{8,9},{9,8},{10,11... | collective-permute-start | bytes 1376264 | tf_op jit(solution)/shard_map/ppermute | solution.py:449
  26.9 0.1 dynamic-slice
  27.1 0.1 broadcast_multiply_fusion
  27.1 0.1 reshape.73
  27.2 0.1 dynamic-slice_convert_fusion
  27.3 0.3 reshape.74.kept
  27.6 6.0 %collective-permute-done.3.before = f32[2,3,32,512]{3,2,1,0:T(8,128)S(1)} collective-permute-done((f32[2,3,32,512]{3,2,1,0:T(8,128)S(1)}, f32[2,3,32,512]{3,2,1,0:T(8,128)S(1)}, u32[]{:S(2)}, u32[]{:S(2)}) %collective-permute-start.3) | collective-permute-done | bytes 393248 | tf_op jit(solution)/shard_map/ppermute | solution.py:473
  33.6 0.0 collective-permute-done.4.after
  33.6 0.1 copy.18.gain
  33.7 12.0 %shard_map.93 = (f32[7,32,512]{2,1,0:T(8,128)S(1)}, f32[7,32,512]{2,1,0:T(8,128)S(1)}, f32[2,7,32,512]{3,2,1,0:T(8,128)}) custom-call(s32[2]{0:T(128)S(1)} %pad_add_fusion.place, f32[3,32,32,512]{3,2,1,0:T(8,128)} %field.1, f32[2,7,32,512]{3,2,1,0:T(8,128)} %copy-done.2, f32[16,32,512]{2,1,0:T(8,128)} %collective-permute-done.1.beside, ...), custom_call_target="tpu_custom_call" | custom-call | flops 1 | bytes 1 | tf_op jit(solution)/shard_map/pallas_call | solution.py:260
  45.8 1.3 %collective-permute-start.9 = (f32[2,7,32,512]{3,2,1,0:T(8,128)}, f32[2,7,32,512]{3,2,1,0:T(8,128)}, u32[]{:S(2)}, u32[]{:S(2)}) collective-permute-start(f32[2,7,32,512]{3,2,1,0:T(8,128)} %get-tuple-element.42), channel_id=1, source_target_pairs={{0,2},{2,0},{1,3},{3,1},{4,6},{6,4},{5,7},{7,5},{8,10},{10,8},{9,1... | collective-permute-start | bytes 2752520 | tf_op jit(solution)/shard_map/ppermute | solution.py:449
  47.1 2.3 %collective-permute-done.6.across.diagonal = f32[2,9,32,512]{3,2,1,0:T(8,128)} collective-permute-done((f32[2,9,32,512]{3,2,1,0:T(8,128)}, f32[2,9,32,512]{3,2,1,0:T(8,128)}, u32[]{:S(2)}, u32[]{:S(2)}) %collective-permute-start.6) | collective-permute-done | bytes 1179680 | tf_op jit(solution)/shard_map/ppermute | solution.py:449
  49.4 2.1 %collective-permute-start.7 = (f32[7,32,512]{2,1,0:T(8,128)S(1)}, f32[7,32,512]{2,1,0:T(8,128)S(1)}, u32[]{:S(2)}, u32[]{:S(2)}) collective-permute-start(f32[7,32,512]{2,1,0:T(8,128)S(1)} %get-tuple-element.36), channel_id=1, source_target_pairs={{0,1},{1,0},{2,3},{3,2},{4,5},{5,4},{6,7},{7,6},{8,9},{9,8},{10,11... | collective-permute-start | bytes 1376264 | tf_op jit(solution)/shard_map/ppermute | solution.py:449
  51.5 1.4 %collective-permute-done.7.refs_1_ = f32[7,32,512]{2,1,0:T(8,128)S(1)} collective-permute-done((f32[7,32,512]{2,1,0:T(8,128)S(1)}, f32[7,32,512]{2,1,0:T(8,128)S(1)}, u32[]{:S(2)}, u32[]{:S(2)}) %collective-permute-start.7) | collective-permute-done | bytes 458784 | tf_op jit(solution)/shard_map/ppermute | solution.py:449
  52.9 0.1 copy.20.gain
  53.0 14.3 %shard_map.94 = (f32[9,32,512]{2,1,0:T(8,128)S(1)}, f32[9,32,512]{2,1,0:T(8,128)}, f32[9,32,512]{2,1,0:T(8,128)}, f32[6,32,512]{2,1,0:T(8,128)S(1)}, f32[3,32,512]{2,1,0:T(8,128)S(1)}) custom-call(s32[2]{0:T(128)S(1)} %pad_add_fusion.place, f32[3,32,32,512]{3,2,1,0:T(8,128)} %field.1, f32[2,9,32,512]{3,2,1,0:T(8,128)} %collective-permute-done.6.across.diagonal, ...), custom_call_target="tpu_custom_call" | custom-call | flops 1 | bytes 1 | tf_op jit(solution)/shard_map/pallas_call | solution.py:260
  67.4 0.8 copy-done
  68.2 0.4 collective-permute-start.8
  68.5 1.8 %collective-permute-start.11 = (f32[9,32,512]{2,1,0:T(8,128)}, f32[9,32,512]{2,1,0:T(8,128)S(1)}, u32[]{:S(2)}, u32[]{:S(2)}) collective-permute-start(f32[9,32,512]{2,1,0:T(8,128)} %get-tuple-element.44), channel_id=1, source_target_pairs={{0,2},{2,0},{1,3},{3,1},{4,6},{6,4},{5,7},{7,5},{8,10},{10,8},{9,1... | collective-permute-start | bytes 1769480 | tf_op jit(solution)/shard_map/ppermute | solution.py:449
  70.3 2.2 %slice_bitcast_fusion = (f32[7,32,512]{2,1,0:T(8,128)}, f32[7,32,512]{2,1,0:T(8,128)}) fusion(f32[2,7,32,512]{3,2,1,0:T(8,128)} %collective-permute-done.9), kind=kLoop, calls=%fused_computation.3 | loop fusion | bytes 1835008 | tf_op jit(solution)/shard_map/squeeze | solution.py:510
  72.5 0.4 collective-permute-start.10
  72.9 0.9 collective-permute-start.12
  73.8 0.9 collective-permute-start.13
  74.8 0.1 divide_multiply_fusion.cot
  74.8 0.0 collective-permute-done.10.refs_5_
  74.9 8.8 %shard_map.95.base = f32[3,32,32,512]{3,2,1,0:T(8,128)} custom-call(s32[2]{0:T(128)S(1)} %pad_add_fusion.place, f32[3,32,32,512]{3,2,1,0:T(8,128)} %field.1, f32[2,3,32,512]{3,2,1,0:T(8,128)S(1)} %collective-permute-done.3.before, f32[2,3,32,512]{3,2,1,0:T(8,128)S(1)} %collective-permute-done.4.after, f32[32,1,1]{2,1,0:T(1,128)S(1)} %get-tuple-element.49.radius, ...), custom_call_target="tpu_custom_call" | custom-call | flops 1 | bytes 1 | tf_op jit(solution)/shard_map/pallas_call | solution.py:355
  83.6 0.9 dynamic-slice_bitcast_fusion.3.base
  84.6 2.5 %shard_map.96.base = f32[3,32,32,512]{3,2,1,0:T(8,128)} custom-call(s32[2]{0:T(128)S(1)} %pad_add_fusion.place, f32[3,32,32,512]{3,2,1,0:T(8,128)} %shard_map.95.base, f32[9,32,512]{2,1,0:T(8,128)S(1)} %collective-permute-done.11.azim), custom_call_target="tpu_custom_call", output_to_operand_aliasing={{}: (1, {})} | custom-call | flops 1 | bytes 1 | tf_op jit(solution)/shard_map/pallas_call | solution.py:393
  87.1 6.1 %collective-permute-done.12.azim = f32[6,32,512]{2,1,0:T(8,128)S(1)} collective-permute-done((f32[6,32,512]{2,1,0:T(8,128)S(1)}, f32[6,32,512]{2,1,0:T(8,128)S(1)}, u32[]{:S(2)}, u32[]{:S(2)}) %collective-permute-start.12) | collective-permute-done | bytes 393248 | tf_op jit(solution)/shard_map/ppermute | solution.py:449
  93.1 2.3 %shard_map.97.current = f32[3,32,32,512]{3,2,1,0:T(8,128)} custom-call(s32[2]{0:T(128)S(1)} %pad_add_fusion.place, f32[3,32,32,512]{3,2,1,0:T(8,128)} %shard_map.96.base, f32[6,32,512]{2,1,0:T(8,128)S(1)} %collective-permute-done.12.azim), custom_call_target="tpu_custom_call", output_to_operand_aliasing={{}: (1, {})} | custom-call | flops 1 | bytes 1 | tf_op jit(solution)/shard_map/pallas_call | solution.py:393
  95.5 1.3 %collective-permute-done.13.azim = f32[3,32,512]{2,1,0:T(8,128)S(1)} collective-permute-done((f32[3,32,512]{2,1,0:T(8,128)S(1)}, f32[3,32,512]{2,1,0:T(8,128)S(1)}, u32[]{:S(2)}, u32[]{:S(2)}) %collective-permute-start.13) | collective-permute-done | bytes 196640 | tf_op jit(solution)/shard_map/ppermute | solution.py:449
  96.8 1.2 %shard_map.98 = f32[3,32,32,512]{3,2,1,0:T(8,128)} custom-call(s32[2]{0:T(128)S(1)} %pad_add_fusion.place, f32[3,32,32,512]{3,2,1,0:T(8,128)} %shard_map.97.current, f32[3,32,512]{2,1,0:T(8,128)S(1)} %dynamic-slice_bitcast_fusion.3.base, f32[3,32,512]{2,1,0:T(8,128)S(1)} %collective-permute-done.13.azim), custom_call_target="tpu_custom_call", output_to_operand_aliasing={{}: (1, {})} | custom-call | flops 1 | bytes 1 | tf_op jit(solution)/shard_map/pallas_call | solution.py:419
  (16 shorter events, 0.1 us)
Async XLA Ops:
  1.8 22.2 %collective-permute-start = (f32[2,7,32,512]{3,2,1,0:T(8,128)S(1)}, f32[2,7,32,512]{3,2,1,0:T(8,128)S(1)}, u32[]{:S(2)}, u32[]{:S(2)}) collective-permute-start(f32[2,7,32,512]{3,2,1,0:T(8,128)S(1)} %shard_map.91), channel_id=1, source_target_pairs={{0,2},{2,0},{1,3},{3,1},{4,6},{6,4},{5,7},{7,5},{8,10},{10,8},{9,1... | collective-permute-start | bytes 2752520 | tf_op jit(solution)/shard_map/ppermute | solution.py:449
  5.6 21.7 %copy-start.3 = (s32[256]{0:T(256)S(1)}, s32[256]{0:T(256)}, u32[]{:S(2)}) copy-start(s32[256]{0:T(256)} %param.10) | copy-start | bytes 3076
  5.6 28.2 %copy-start.1 = (f32[1,2048]{1,0:T(1,128)S(1)}, f32[1,2048]{1,0:T(1,128)}, u32[]{:S(2)}) copy-start(f32[1,2048]{1,0:T(1,128)} %constant.85.clone.modes) | copy-start | bytes 24580
  7.5 4.4 %collective-permute-start.5 = (f32[9,32,512]{2,1,0:T(8,128)}, f32[9,32,512]{2,1,0:T(8,128)}, u32[]{:S(2)}, u32[]{:S(2)}) collective-permute-start(f32[9,32,512]{2,1,0:T(8,128)} %dynamic-slice_bitcast_fusion.1), channel_id=1, source_target_pairs={{0,1},{1,0},{2,3},{3,2},{4,5},{5,4},{6,7},{7,6},{8,9},{9,8},{10,11... | collective-permute-start | bytes 1769480 | tf_op jit(solution)/shard_map/ppermute | solution.py:449
  10.8 22.9 %collective-permute-start.1 = (f32[16,32,512]{2,1,0:T(8,128)}, f32[16,32,512]{2,1,0:T(8,128)}, u32[]{:S(2)}, u32[]{:S(2)}) collective-permute-start(f32[16,32,512]{2,1,0:T(8,128)} %dynamic-slice_bitcast_fusion), channel_id=1, source_target_pairs={{0,1},{1,0},{2,3},{3,2},{4,5},{5,4},{6,7},{7,6},{8,9},{9,8},{10,11... | collective-permute-start | bytes 3145736 | tf_op jit(solution)/shard_map/ppermute | solution.py:449
  14.2 35.2 %collective-permute-start.6 = (f32[2,9,32,512]{3,2,1,0:T(8,128)}, f32[2,9,32,512]{3,2,1,0:T(8,128)}, u32[]{:S(2)}, u32[]{:S(2)}) collective-permute-start(f32[2,9,32,512]{3,2,1,0:T(8,128)} %pad_maximum_fusion), channel_id=1, source_target_pairs={{0,2},{2,0},{1,3},{3,1},{4,6},{6,4},{5,7},{7,5},{8,10},{10,8},{9,1... | collective-permute-start | bytes 3538952 | tf_op jit(solution)/shard_map/ppermute | solution.py:449
  14.2 19.4 %collective-permute-start.3 = (f32[2,3,32,512]{3,2,1,0:T(8,128)S(1)}, f32[2,3,32,512]{3,2,1,0:T(8,128)S(1)}, u32[]{:S(2)}, u32[]{:S(2)}) collective-permute-start(f32[2,3,32,512]{3,2,1,0:T(8,128)S(1)} %get-tuple-element.27), channel_id=1, source_target_pairs={{0,4},{4,8},{8,12},{12,16},{16,20},{20,24},{24,28},{1,5},{5,9},{9,... | collective-permute-start | bytes 1179656 | tf_op jit(solution)/shard_map/ppermute | solution.py:473
  17.5 16.0 %collective-permute-start.4 = (f32[2,3,32,512]{3,2,1,0:T(8,128)S(1)}, f32[2,3,32,512]{3,2,1,0:T(8,128)S(1)}, u32[]{:S(2)}, u32[]{:S(2)}) collective-permute-start(f32[2,3,32,512]{3,2,1,0:T(8,128)S(1)} %get-tuple-element.28), channel_id=1, source_target_pairs={{4,0},{8,4},{12,8},{16,12},{20,16},{24,20},{28,24},{5,1},{9,5},{13... | collective-permute-start | bytes 1179656 | tf_op jit(solution)/shard_map/ppermute | solution.py:473
  24.0 9.7 %copy-start.2 = (f32[2,7,32,512]{3,2,1,0:T(8,128)}, f32[2,7,32,512]{3,2,1,0:T(8,128)S(1)}, u32[]{:S(2)}) copy-start(f32[2,7,32,512]{3,2,1,0:T(8,128)S(1)} %collective-permute-done.across) | copy-start | bytes 2752516
  24.9 8.9 %collective-permute-start.2 = (f32[7,32,512]{2,1,0:T(8,128)}, f32[7,32,512]{2,1,0:T(8,128)S(1)}, u32[]{:S(2)}, u32[]{:S(2)}) collective-permute-start(f32[7,32,512]{2,1,0:T(8,128)} %dynamic-slice_bitcast_fusion.2), channel_id=1, source_target_pairs={{0,1},{1,0},{2,3},{3,2},{4,5},{5,4},{6,7},{7,6},{8,9},{9,8},{10,11... | collective-permute-start | bytes 1376264 | tf_op jit(solution)/shard_map/ppermute | solution.py:449
  45.8 24.5 %collective-permute-start.9 = (f32[2,7,32,512]{3,2,1,0:T(8,128)}, f32[2,7,32,512]{3,2,1,0:T(8,128)}, u32[]{:S(2)}, u32[]{:S(2)}) collective-permute-start(f32[2,7,32,512]{3,2,1,0:T(8,128)} %get-tuple-element.42), channel_id=1, source_target_pairs={{0,2},{2,0},{1,3},{3,1},{4,6},{6,4},{5,7},{7,5},{8,10},{10,8},{9,1... | collective-permute-start | bytes 2752520 | tf_op jit(solution)/shard_map/ppermute | solution.py:449
  49.4 3.5 %collective-permute-start.7 = (f32[7,32,512]{2,1,0:T(8,128)S(1)}, f32[7,32,512]{2,1,0:T(8,128)S(1)}, u32[]{:S(2)}, u32[]{:S(2)}) collective-permute-start(f32[7,32,512]{2,1,0:T(8,128)S(1)} %get-tuple-element.36), channel_id=1, source_target_pairs={{0,1},{1,0},{2,3},{3,2},{4,5},{5,4},{6,7},{7,6},{8,9},{9,8},{10,11... | collective-permute-start | bytes 1376264 | tf_op jit(solution)/shard_map/ppermute | solution.py:449
  67.3 0.8 copy-start
  68.2 6.7 %collective-permute-start.8 = (f32[9,32,512]{2,1,0:T(8,128)}, f32[9,32,512]{2,1,0:T(8,128)}, u32[]{:S(2)}, u32[]{:S(2)}) collective-permute-start(f32[9,32,512]{2,1,0:T(8,128)} %get-tuple-element.41), channel_id=1, source_target_pairs={{0,1},{1,0},{2,3},{3,2},{4,5},{5,4},{6,7},{7,6},{8,9},{9,8},{10,11... | collective-permute-start | bytes 1769480 | tf_op jit(solution)/shard_map/ppermute | solution.py:449
  68.5 16.1 %collective-permute-start.11 = (f32[9,32,512]{2,1,0:T(8,128)}, f32[9,32,512]{2,1,0:T(8,128)S(1)}, u32[]{:S(2)}, u32[]{:S(2)}) collective-permute-start(f32[9,32,512]{2,1,0:T(8,128)} %get-tuple-element.44), channel_id=1, source_target_pairs={{0,2},{2,0},{1,3},{3,1},{4,6},{6,4},{5,7},{7,5},{8,10},{10,8},{9,1... | collective-permute-start | bytes 1769480 | tf_op jit(solution)/shard_map/ppermute | solution.py:449
  72.5 2.4 %collective-permute-start.10 = (f32[7,32,512]{2,1,0:T(8,128)}, f32[7,32,512]{2,1,0:T(8,128)}, u32[]{:S(2)}, u32[]{:S(2)}) collective-permute-start(f32[7,32,512]{2,1,0:T(8,128)} %get-tuple-element.47), channel_id=1, source_target_pairs={{0,1},{1,0},{2,3},{3,2},{4,5},{5,4},{6,7},{7,6},{8,9},{9,8},{10,11... | collective-permute-start | bytes 1376264 | tf_op jit(solution)/shard_map/ppermute | solution.py:449
  72.9 20.2 %collective-permute-start.12 = (f32[6,32,512]{2,1,0:T(8,128)S(1)}, f32[6,32,512]{2,1,0:T(8,128)S(1)}, u32[]{:S(2)}, u32[]{:S(2)}) collective-permute-start(f32[6,32,512]{2,1,0:T(8,128)S(1)} %get-tuple-element.45), channel_id=1, source_target_pairs={{0,3},{3,0},{1,2},{2,1},{4,7},{7,4},{5,6},{6,5},{8,11},{11,8},{9,1... | collective-permute-start | bytes 1179656 | tf_op jit(solution)/shard_map/ppermute | solution.py:449
  73.8 22.9 %collective-permute-start.13 = (f32[3,32,512]{2,1,0:T(8,128)S(1)}, f32[3,32,512]{2,1,0:T(8,128)S(1)}, u32[]{:S(2)}, u32[]{:S(2)}) collective-permute-start(f32[3,32,512]{2,1,0:T(8,128)S(1)} %get-tuple-element.46), channel_id=1, source_target_pairs={{0,3},{3,0},{1,2},{2,1},{4,7},{7,4},{5,6},{6,5},{8,11},{11,8},{9,1... | collective-permute-start | bytes 589832 | tf_op jit(solution)/shard_map/ppermute | solution.py:449

commit v9 on v8

--- a/solution.py
+++ b/solution.py
@@ -140,7 +140,7 @@
 TO_Y = [(0, 2), (2, 0), (1, 3), (3, 1)]
 TO_C = [(0, 1), (1, 0), (2, 3), (3, 2)]
 TO_YC = [(0, 3), (3, 0), (1, 2), (2, 1)]
-VMEM = 52 * 1024 * 1024
+VMEM = 50 * 1024 * 1024
 SHORT = pl.CostEstimate(flops=1, bytes_accessed=1, transcendentals=0)
 
 
@@ -149,7 +149,7 @@
     for _ in range(count):
         parts.append(table.astype(jnp.bfloat16))
         table = table - parts[-1].astype(np.float64)
-    return np.stack(parts)
+    return np.concatenate(parts)
 
 
 def mode_tables(lon_total):
@@ -161,29 +161,31 @@
         inverse = np.concatenate([-np.sin(phase), np.cos(phase)], axis=1).T
         return split_table(forward, 3), split_table(inverse, 2)
 
-    zero = 4 * np.arange(quarter // 2)
-    two = zero + 2
+    zero = 8 * np.arange(quarter // 4)
+    four = zero + 4
+    two = 4 * np.arange(quarter // 2) + 2
     odd = 2 * np.arange(quarter) + 1
-    mode_ids = np.concatenate([zero, zero, two, two, odd, odd]).astype(np.float32)[None, :]
-    return pair(zero, quarter), pair(two, quarter), pair(odd, 2 * quarter), mode_ids
+    mode_ids = np.concatenate([zero, zero, four, four, two, two, odd, odd]).astype(np.float32)[None, :]
+    return pair(zero, quarter // 2), pair(four, quarter // 2), pair(two, quarter), pair(odd, 2 * quarter), mode_ids
 
 
 def split_dot(value, table):
-    count = table.shape[0]
+    depth = value.shape[1]
+    count = table.shape[0] // depth
     parts = []
     for _ in range(count):
         parts.append(value.astype(jnp.bfloat16))
         value = value - parts[-1].astype(jnp.float32)
     total = None
     for order in reversed(range(count)):
-        for i in range(order + 1):
-            term = jnp.dot(parts[i], table[order - i], preferred_element_type=jnp.float32)
-            total = term if total is None else total + term
+        row = jnp.concatenate(parts[order::-1], axis=1)
+        term = jnp.dot(row, table[: (order + 1) * depth], preferred_element_type=jnp.float32)
+        total = term if total is None else total + term
     return total
 
 
 def transform_kernel(place, own, across, beside, diagonal, kept, gain, modes, *refs):
-    tables, (out_own, out_beside, *outs), held, sems = refs[:6], refs[6:-7], refs[-7:-1], refs[-1]
+    tables, (out_own, out_beside, *outs), held, sems = refs[:8], refs[8:-9], refs[-9:-1], refs[-1]
     copies = [pltpu.make_async_copy(table, ref, sems.at[i]) for i, (table, ref) in enumerate(zip(tables, held))]
     for copy in copies:
         copy.start()
@@ -206,9 +208,11 @@
         copies[2 * which + 1].wait()
         return split_dot(spectrum * weight[:, start : start + spectrum.shape[1]], held[2 * which + 1])
 
-    even0 = filtered(near + far, 0, 0)
-    even2 = sign_c * filtered(sign_c * (near - far), 1, quarter)
-    odd_out = sign_y * filtered(odd, 2, 2 * quarter)
+    lower, upper = (near + far)[:, : quarter // 2], (near + far)[:, quarter // 2 :]
+    zero, four = filtered(lower + upper, 0, 0), filtered(lower - upper, 1, quarter // 2)
+    even0 = jnp.concatenate([zero + four, zero - four], axis=1)
+    even2 = sign_c * filtered(sign_c * (near - far), 2, quarter)
+    odd_out = sign_y * filtered(odd, 3, 2 * quarter)
     left, right = odd_out[:, :quarter], odd_out[:, quarter:]
     odd_near, odd_far = jnp.where(first, left, right), jnp.where(first, right, left)
     even_near, even_far = even0 + even2, even0 - even2
@@ -228,7 +232,8 @@
 
 def transform(place, magnetic, start, across, beside, diagonal, row_kept, row_gain, tables, cuts):
     depth, th_dev, quarter = across.shape[1:]
-    zero, two, odd, mode_ids = tables
+    *pairs, mode_ids = tables
+    flat = [table for pair in pairs for table in pair]
     whole = pl.BlockSpec(memory_space=pltpu.VMEM)
     rows = depth * th_dev
     half = magnetic.shape[1] // 2
@@ -253,9 +258,9 @@
             row_block,
             whole,
         ]
-        + [pl.BlockSpec(memory_space=pl.ANY)] * 6,
+        + [pl.BlockSpec(memory_space=pl.ANY)] * len(flat),
         out_specs=[whole] * len(shapes),
-        scratch_shapes=[pltpu.VMEM(t.shape, jnp.bfloat16) for t in (*zero, *two, *odd)] + [pltpu.SemaphoreType.DMA((6,))],
+        scratch_shapes=[pltpu.VMEM(t.shape, jnp.bfloat16) for t in flat] + [pltpu.SemaphoreType.DMA((len(flat),))],
     )
     return pl.pallas_call(
         transform_kernel,
@@ -263,7 +268,7 @@
         out_shape=[jax.ShapeDtypeStruct(shape, jnp.float32) for shape in shapes],
         compiler_params=pltpu.CompilerParams(vmem_limit_bytes=VMEM),
         cost_estimate=SHORT,
-    )(place, magnetic, across, beside, diagonal, row_kept, row_gain, mode_ids, *zero, *two, *odd)
+    )(place, magnetic, across, beside, diagonal, row_kept, row_gain, mode_ids, *flat)
 
 
 def edge_rows(magnetic):

time: 99.1 us -> 98 us (0.989)
  waiting for transfers between devices: 22.3 us -> 18.8 us
  local copies, waits for them, and re-layouts: 10.8 us -> 12.2 us
    ppermute x12, waiting for transfers between devices: 16.3 us -> 12.7 us  [on_four(): send = lambda value, pairs: lax.ppermute(value, 'azim', pairs)]
    unnamed x8 -> x22, local copies, waits for them, and re-layouts: 0.83 us -> 2.79 us
  transfers between devices with their start and end apart: 14 -> 14, of which waited for: 6 -> 6; matrix products, arithmetic and copies ran while one was open for 13% -> 12% of each run, Pallas kernels for 42% -> 43%
where the time goes in v9:
time: 98 us; the launch traced here: 96.9 us
  Pallas kernels  44.9 us (46%)
  waiting for transfers between devices  18.8 us (19%)
  starting transfers between devices  17.9 us (18%)
  local copies, waits for them, and re-layouts  12.2 us (12%)
  other arithmetic  2.67 us (3%)
    pallas_call x2, Pallas kernels, transform(): pl.pallas_call(transform_kernel, grid_spec=grid_spec, out_shape=[jax.Shap...  26.2 us
    ppermute x12, starting transfers between devices, on_four(): send = lambda value, pairs: lax.ppermute(value, 'azim', pairs)  13.2 us
    ppermute x12, waiting for transfers between devices, on_four(): send = lambda value, pairs: lax.ppermute(value, 'azim', pairs)  12.7 us
    pallas_call x1, Pallas kernels, local_part(): pl.pallas_call(kernel, grid_spec=pltpu.PrefetchScalarGridSpec(num_scalar_...  8.51 us
    ppermute x1, waiting for transfers between devices, on_four(): lax.ppermute(last, 'lat', up)  6.14 us
    squeeze x4, local copies, waits for them, and re-layouts, cut(): lax.dynamic_slice(source, (field, start, 0, 0), (1, length, th_dev, ph_dev))  5.61 us
    pallas_call x2, Pallas kernels, add_one(): pl.pallas_call(kernel, grid_spec=pltpu.PrefetchScalarGridSpec(num_scalar_...  4.98 us
    ppermute x1, starting transfers between devices, on_four(): lax.ppermute(last, 'lat', up)  3.35 us
  transfers between devices with their start and end apart: 14, of which 6 were waited for; matrix products, arithmetic and copies ran while one was open for 12% of the time, Pallas kernels for 43%

profile of v9, /device:TPU:1, one launch (start us, length us, event | category | flops | bytes accessed | tf_op | source)
XLA Modules:
  0.0 96.9 jit_solution(4949475120111558634)
XLA Ops:
  0.0 0.1 pad_add_fusion.place
  0.1 1.7 %shard_map.109 = f32[2,7,32,512]{3,2,1,0:T(8,128)S(1)} custom-call(s32[2]{0:T(128)S(1)} %pad_add_fusion.place, f32[3,32,32,512]{3,2,1,0:T(8,128)} %field.1), custom_call_target="tpu_custom_call" | custom-call | flops 1 | bytes 1 | tf_op jit(solution)/shard_map/pallas_call | solution.py:309
  1.8 2.1 %collective-permute-start = (f32[2,7,32,512]{3,2,1,0:T(8,128)S(1)}, f32[2,7,32,512]{3,2,1,0:T(8,128)}, u32[]{:S(2)}, u32[]{:S(2)}) collective-permute-start(f32[2,7,32,512]{3,2,1,0:T(8,128)S(1)} %shard_map.109), channel_id=1, source_target_pairs={{0,2},{2,0},{1,3},{3,1},{4,6},{6,4},{5,7},{7,5},{8,10},{10,8},{9,1... | collective-permute-start | bytes 2752520 | tf_op jit(solution)/shard_map/ppermute | solution.py:454
  3.9 2.3 %shard_map.110 = (f32[2,3,32,512]{3,2,1,0:T(8,128)}, f32[2,3,32,512]{3,2,1,0:T(8,128)S(1)}) custom-call(f32[3,32,32,512]{3,2,1,0:T(8,128)} %field.1, f32[3,32,32,512]{3,2,1,0:T(8,128)} %field.1), custom_call_target="tpu_custom_call" | custom-call | flops 1 | bytes 1 | tf_op jit(solution)/shard_map/pallas_call | solution.py:284
  6.2 0.0 copy-start.1
  6.2 0.0 copy-start.2
  6.3 1.3 %dynamic-slice_bitcast_fusion.1 = f32[9,32,512]{2,1,0:T(8,128)S(1)} fusion(f32[3,32,32,512]{3,2,1,0:T(8,128)} %field.1, s32[]{:T(128)S(6)} %select_n.38, s32[]{:T(128)S(6)} %select_n.39), kind=kLoop, calls=%fused_computation.2 | loop fusion | bytes 1179656 | tf_op jit(solution)/shard_map/squeeze | solution.py:457
  7.6 1.0 %collective-permute-start.5 = (f32[9,32,512]{2,1,0:T(8,128)S(1)}, f32[9,32,512]{2,1,0:T(8,128)}, u32[]{:S(2)}, u32[]{:S(2)}) collective-permute-start(f32[9,32,512]{2,1,0:T(8,128)S(1)} %dynamic-slice_bitcast_fusion.1), channel_id=1, source_target_pairs={{0,1},{1,0},{2,3},{3,2},{4,5},{5,4},{6,7},{7,6},{8,9},{9,8},{10,11... | collective-permute-start | bytes 1769480 | tf_op jit(solution)/shard_map/ppermute | solution.py:454
  8.6 2.3 %dynamic-slice_bitcast_fusion = f32[16,32,512]{2,1,0:T(8,128)} fusion(f32[3,32,32,512]{3,2,1,0:T(8,128)} %field.1, s32[]{:T(128)S(6)} %select_n.38, s32[]{:T(128)S(6)} %select_n.40), kind=kLoop, calls=%fused_computation.1 | loop fusion | bytes 2097160 | tf_op jit(solution)/shard_map/squeeze | solution.py:457
  10.9 0.0 collective-permute-start.1
  10.9 1.1 %constant_dynamic-slice_fusion = f32[1,9,32,512]{3,2,1,0:T(8,128)S(1)} fusion(f32[3,32,32,512]{3,2,1,0:T(8,128)} %field.1, s32[]{:T(128)S(6)} %select_n.43, s32[]{:T(128)S(6)} %select_n.39), kind=kLoop, calls=%fused_computation.11 | loop fusion | bytes 1179656 | tf_op jit(solution)/shard_map/dynamic_slice | solution.py:457
  12.1 2.3 %pad_maximum_fusion = f32[2,9,32,512]{3,2,1,0:T(8,128)} fusion(f32[1,9,32,512]{3,2,1,0:T(8,128)} %bitcast.5, f32[1,9,32,512]{3,2,1,0:T(8,128)S(1)} %constant_dynamic-slice_fusion), kind=kLoop, calls=%fused_computation | loop fusion | flops 294912 | bytes 2359296 | tf_op jit(solution)/shard_map/stack | solution.py:473
  14.3 3.4 %collective-permute-start.3 = (f32[2,3,32,512]{3,2,1,0:T(8,128)}, f32[2,3,32,512]{3,2,1,0:T(8,128)S(1)}, u32[]{:S(2)}, u32[]{:S(2)}) collective-permute-start(f32[2,3,32,512]{3,2,1,0:T(8,128)} %get-tuple-element.27), channel_id=1, source_target_pairs={{0,4},{4,8},{8,12},{12,16},{16,20},{20,24},{24,28},{1,5},{5,9},{9,... | collective-permute-start | bytes 1179656 | tf_op jit(solution)/shard_map/ppermute | solution.py:478
  17.7 1.3 %collective-permute-start.4 = (f32[2,3,32,512]{3,2,1,0:T(8,128)}, f32[2,3,32,512]{3,2,1,0:T(8,128)S(1)}, u32[]{:S(2)}, u32[]{:S(2)}) collective-permute-start(f32[2,3,32,512]{3,2,1,0:T(8,128)} %copy-done.9), channel_id=1, source_target_pairs={{4,0},{8,4},{12,8},{16,12},{20,16},{24,20},{28,24},{5,1},{9,5},{13... | collective-permute-start | bytes 1179656 | tf_op jit(solution)/shard_map/ppermute | solution.py:478
  19.0 5.1 %collective-permute-done.across = f32[2,7,32,512]{3,2,1,0:T(8,128)} collective-permute-done((f32[2,7,32,512]{3,2,1,0:T(8,128)S(1)}, f32[2,7,32,512]{3,2,1,0:T(8,128)}, u32[]{:S(2)}, u32[]{:S(2)}) %collective-permute-start) | collective-permute-done | bytes 917536 | tf_op jit(solution)/shard_map/ppermute | solution.py:454
  24.1 1.0 %dynamic-slice_bitcast_fusion.2 = f32[7,32,512]{2,1,0:T(8,128)S(1)} fusion(f32[2,7,32,512]{3,2,1,0:T(8,128)} %collective-permute-done.across, s32[]{:T(128)S(6)} %select_n.41), kind=kLoop, calls=%fused_computation.5 | loop fusion | bytes 917508 | tf_op jit(solution)/shard_map/squeeze | solution.py:457
  25.2 2.1 %collective-permute-start.2 = (f32[7,32,512]{2,1,0:T(8,128)S(1)}, f32[7,32,512]{2,1,0:T(8,128)S(1)}, u32[]{:S(2)}, u32[]{:S(2)}) collective-permute-start(f32[7,32,512]{2,1,0:T(8,128)S(1)} %dynamic-slice_bitcast_fusion.2), channel_id=1, source_target_pairs={{0,1},{1,0},{2,3},{3,2},{4,5},{5,4},{6,7},{7,6},{8,9},{9,8},{10,11... | collective-permute-start | bytes 1376264 | tf_op jit(solution)/shard_map/ppermute | solution.py:454
  27.3 0.1 dynamic-slice
  27.4 0.1 broadcast_multiply_fusion
  27.5 0.1 reshape.73
  27.6 0.1 dynamic-slice_convert_fusion
  27.7 0.3 reshape.74.kept
  27.9 6.1 %collective-permute-done.3.before = f32[2,3,32,512]{3,2,1,0:T(8,128)S(1)} collective-permute-done((f32[2,3,32,512]{3,2,1,0:T(8,128)}, f32[2,3,32,512]{3,2,1,0:T(8,128)S(1)}, u32[]{:S(2)}, u32[]{:S(2)}) %collective-permute-start.3) | collective-permute-done | bytes 393248 | tf_op jit(solution)/shard_map/ppermute | solution.py:478
  34.1 0.8 copy-done.4
  34.9 0.1 copy.20.gain
  35.1 11.7 %shard_map.111 = (f32[7,32,512]{2,1,0:T(8,128)S(1)}, f32[7,32,512]{2,1,0:T(8,128)S(1)}, f32[2,7,32,512]{3,2,1,0:T(8,128)}) custom-call(s32[2]{0:T(128)S(1)} %pad_add_fusion.place, f32[3,32,32,512]{3,2,1,0:T(8,128)} %field.1, f32[2,7,32,512]{3,2,1,0:T(8,128)} %collective-permute-done.across, f32[16,32,512]{2,1,0:T(8,128)} %collective-permute-done.1.beside, ...), custom_call_target="tpu_custom_call" | custom-call | flops 1 | bytes 1 | tf_op jit(solution)/shard_map/pallas_call | solution.py:265
  46.8 1.3 %collective-permute-start.9 = (f32[2,7,32,512]{3,2,1,0:T(8,128)}, f32[2,7,32,512]{3,2,1,0:T(8,128)}, u32[]{:S(2)}, u32[]{:S(2)}) collective-permute-start(f32[2,7,32,512]{3,2,1,0:T(8,128)} %get-tuple-element.42), channel_id=1, source_target_pairs={{0,2},{2,0},{1,3},{3,1},{4,6},{6,4},{5,7},{7,5},{8,10},{10,8},{9,1... | collective-permute-start | bytes 2752520 | tf_op jit(solution)/shard_map/ppermute | solution.py:454
  48.1 1.3 %collective-permute-done.6.across.diagonal = f32[2,9,32,512]{3,2,1,0:T(8,128)} collective-permute-done((f32[2,9,32,512]{3,2,1,0:T(8,128)}, f32[2,9,32,512]{3,2,1,0:T(8,128)}, u32[]{:S(2)}, u32[]{:S(2)}) %collective-permute-start.6) | collective-permute-done | bytes 1179680 | tf_op jit(solution)/shard_map/ppermute | solution.py:454
  49.4 1.5 %collective-permute-start.7 = (f32[7,32,512]{2,1,0:T(8,128)S(1)}, f32[7,32,512]{2,1,0:T(8,128)S(1)}, u32[]{:S(2)}, u32[]{:S(2)}) collective-permute-start(f32[7,32,512]{2,1,0:T(8,128)S(1)} %get-tuple-element.36), channel_id=1, source_target_pairs={{0,1},{1,0},{2,3},{3,2},{4,5},{5,4},{6,7},{7,6},{8,9},{9,8},{10,11... | collective-permute-start | bytes 1376264 | tf_op jit(solution)/shard_map/ppermute | solution.py:454
  50.9 1.4 %collective-permute-done.7.refs_1_ = f32[7,32,512]{2,1,0:T(8,128)S(1)} collective-permute-done((f32[7,32,512]{2,1,0:T(8,128)S(1)}, f32[7,32,512]{2,1,0:T(8,128)S(1)}, u32[]{:S(2)}, u32[]{:S(2)}) %collective-permute-start.7) | collective-permute-done | bytes 458784 | tf_op jit(solution)/shard_map/ppermute | solution.py:454
  52.3 0.1 copy.22.gain
  52.5 14.5 %shard_map.112 = (f32[9,32,512]{2,1,0:T(8,128)S(1)}, f32[9,32,512]{2,1,0:T(8,128)}, f32[9,32,512]{2,1,0:T(8,128)}, f32[6,32,512]{2,1,0:T(8,128)}, f32[3,32,512]{2,1,0:T(8,128)S(1)}) custom-call(s32[2]{0:T(128)S(1)} %pad_add_fusion.place, f32[3,32,32,512]{3,2,1,0:T(8,128)} %field.1, f32[2,9,32,512]{3,2,1,0:T(8,128)} %collective-permute-done.6.across.diagonal, ...), custom_call_target="tpu_custom_call" | custom-call | flops 1 | bytes 1 | tf_op jit(solution)/shard_map/pallas_call | solution.py:265
  67.0 0.4 collective-permute-start.8
  67.4 1.7 %collective-permute-start.11 = (f32[9,32,512]{2,1,0:T(8,128)}, f32[9,32,512]{2,1,0:T(8,128)S(1)}, u32[]{:S(2)}, u32[]{:S(2)}) collective-permute-start(f32[9,32,512]{2,1,0:T(8,128)} %get-tuple-element.44), channel_id=1, source_target_pairs={{0,2},{2,0},{1,3},{3,1},{4,6},{6,4},{5,7},{7,5},{8,10},{10,8},{9,1... | collective-permute-start | bytes 1769480 | tf_op jit(solution)/shard_map/ppermute | solution.py:454
  69.1 2.0 %slice_bitcast_fusion = (f32[7,32,512]{2,1,0:T(8,128)}, f32[7,32,512]{2,1,0:T(8,128)S(1)}) fusion(f32[2,7,32,512]{3,2,1,0:T(8,128)} %collective-permute-done.9), kind=kLoop, calls=%fused_computation.3 | loop fusion | bytes 1835008 | tf_op jit(solution)/shard_map/squeeze | solution.py:515
  71.1 1.2 %collective-permute-start.10 = (f32[7,32,512]{2,1,0:T(8,128)}, f32[7,32,512]{2,1,0:T(8,128)}, u32[]{:S(2)}, u32[]{:S(2)}) collective-permute-start(f32[7,32,512]{2,1,0:T(8,128)} %get-tuple-element.47), channel_id=1, source_target_pairs={{0,1},{1,0},{2,3},{3,2},{4,5},{5,4},{6,7},{7,6},{8,9},{9,8},{10,11... | collective-permute-start | bytes 1376264 | tf_op jit(solution)/shard_map/ppermute | solution.py:454
  72.3 1.3 %collective-permute-start.12 = (f32[6,32,512]{2,1,0:T(8,128)}, f32[6,32,512]{2,1,0:T(8,128)}, u32[]{:S(2)}, u32[]{:S(2)}) collective-permute-start(f32[6,32,512]{2,1,0:T(8,128)} %get-tuple-element.45), channel_id=1, source_target_pairs={{0,3},{3,0},{1,2},{2,1},{4,7},{7,4},{5,6},{6,5},{8,11},{11,8},{9,1... | collective-permute-start | bytes 1179656 | tf_op jit(solution)/shard_map/ppermute | solution.py:454
  73.6 0.5 collective-permute-start.13
  74.1 0.1 divide_multiply_fusion.cot
  74.2 1.0 %copy-done.5 = f32[2,3,32,512]{3,2,1,0:T(8,128)S(1)} copy-done((f32[2,3,32,512]{3,2,1,0:T(8,128)S(1)}, f32[2,3,32,512]{3,2,1,0:T(8,128)}, u32[]{:S(2)}) %copy-start.5) | copy-done | bytes 393240
  75.2 1.0 %copy-done.7 = f32[2,3,32,512]{3,2,1,0:T(8,128)S(1)} copy-done((f32[2,3,32,512]{3,2,1,0:T(8,128)S(1)}, f32[2,3,32,512]{3,2,1,0:T(8,128)}, u32[]{:S(2)}) %copy-start.7) | copy-done | bytes 393240
  76.2 8.5 %shard_map.113.base = f32[3,32,32,512]{3,2,1,0:T(8,128)} custom-call(s32[2]{0:T(128)S(1)} %pad_add_fusion.place, f32[3,32,32,512]{3,2,1,0:T(8,128)} %field.1, f32[2,3,32,512]{3,2,1,0:T(8,128)S(1)} %copy-done.5, f32[2,3,32,512]{3,2,1,0:T(8,128)S(1)} %copy-done.7, f32[32,1,1]{2,1,0:T(1,128)S(1)} %get-tuple-element.49.radius, ...), custom_call_target="tpu_custom_call" | custom-call | flops 1 | bytes 1 | tf_op jit(solution)/shard_map/pallas_call | solution.py:360
  84.7 0.9 dynamic-slice_bitcast_fusion.3.base
  85.7 2.5 %shard_map.114.base = f32[3,32,32,512]{3,2,1,0:T(8,128)} custom-call(s32[2]{0:T(128)S(1)} %pad_add_fusion.place, f32[3,32,32,512]{3,2,1,0:T(8,128)} %shard_map.113.base, f32[9,32,512]{2,1,0:T(8,128)S(1)} %collective-permute-done.11.azim), custom_call_target="tpu_custom_call", output_to_operand_aliasing={{}: (1, {})} | custom-call | flops 1 | bytes 1 | tf_op jit(solution)/shard_map/pallas_call | solution.py:398
  88.2 3.7 %collective-permute-done.12.azim = f32[6,32,512]{2,1,0:T(8,128)} collective-permute-done((f32[6,32,512]{2,1,0:T(8,128)}, f32[6,32,512]{2,1,0:T(8,128)}, u32[]{:S(2)}, u32[]{:S(2)}) %collective-permute-start.12) | collective-permute-done | bytes 393248 | tf_op jit(solution)/shard_map/ppermute | solution.py:454
  91.9 2.4 %shard_map.115.current = f32[3,32,32,512]{3,2,1,0:T(8,128)} custom-call(s32[2]{0:T(128)S(1)} %pad_add_fusion.place, f32[3,32,32,512]{3,2,1,0:T(8,128)} %shard_map.114.base, f32[6,32,512]{2,1,0:T(8,128)} %collective-permute-done.12.azim), custom_call_target="tpu_custom_call", output_to_operand_aliasing={{}: (1, {})} | custom-call | flops 1 | bytes 1 | tf_op jit(solution)/shard_map/pallas_call | solution.py:398
  94.3 1.2 %collective-permute-done.13.azim = f32[3,32,512]{2,1,0:T(8,128)S(1)} collective-permute-done((f32[3,32,512]{2,1,0:T(8,128)S(1)}, f32[3,32,512]{2,1,0:T(8,128)S(1)}, u32[]{:S(2)}, u32[]{:S(2)}) %collective-permute-start.13) | collective-permute-done | bytes 196640 | tf_op jit(solution)/shard_map/ppermute | solution.py:454
  95.5 1.2 %shard_map.116 = f32[3,32,32,512]{3,2,1,0:T(8,128)} custom-call(s32[2]{0:T(128)S(1)} %pad_add_fusion.place, f32[3,32,32,512]{3,2,1,0:T(8,128)} %shard_map.115.current, f32[3,32,512]{2,1,0:T(8,128)S(1)} %dynamic-slice_bitcast_fusion.3.base, f32[3,32,512]{2,1,0:T(8,128)S(1)} %collective-permute-done.13.azim), custom_call_target="tpu_custom_call", output_to_operand_aliasing={{}: (1, {})} | custom-call | flops 1 | bytes 1 | tf_op jit(solution)/shard_map/pallas_call | solution.py:424
  (30 shorter events, 0.1 us)
Async XLA Ops:
  1.8 22.3 %collective-permute-start = (f32[2,7,32,512]{3,2,1,0:T(8,128)S(1)}, f32[2,7,32,512]{3,2,1,0:T(8,128)}, u32[]{:S(2)}, u32[]{:S(2)}) collective-permute-start(f32[2,7,32,512]{3,2,1,0:T(8,128)S(1)} %shard_map.109), channel_id=1, source_target_pairs={{0,2},{2,0},{1,3},{3,1},{4,6},{6,4},{5,7},{7,5},{8,10},{10,8},{9,1... | collective-permute-start | bytes 2752520 | tf_op jit(solution)/shard_map/ppermute | solution.py:454
  6.2 8.2 %copy-start.9 = (f32[2,3,32,512]{3,2,1,0:T(8,128)}, f32[2,3,32,512]{3,2,1,0:T(8,128)S(1)}, u32[]{:S(2)}) copy-start(f32[2,3,32,512]{3,2,1,0:T(8,128)S(1)} %get-tuple-element.28) | copy-start | bytes 1179652
  6.2 21.4 %copy-start.10 = (s32[256]{0:T(256)S(1)}, s32[256]{0:T(256)}, u32[]{:S(2)}) copy-start(s32[256]{0:T(256)} %param.12) | copy-start | bytes 3076
  6.2 28.8 %copy-start = (bf16[768,256]{1,0:T(8,128)(2,1)S(1)}, bf16[768,256]{1,0:T(8,128)(2,1)}, u32[]{:S(2)}) copy-start(bf16[768,256]{1,0:T(8,128)(2,1)} %constant.92.clone.refs_2_) | copy-start | bytes 1179652
  6.2 28.8 %copy-start.1 = (bf16[768,256]{1,0:T(8,128)(2,1)S(1)}, bf16[768,256]{1,0:T(8,128)(2,1)}, u32[]{:S(2)}) copy-start(bf16[768,256]{1,0:T(8,128)(2,1)} %constant.90.clone.refs_0_) | copy-start | bytes 1179652
  6.2 28.8 %copy-start.2 = (bf16[512,256]{1,0:T(8,128)(2,1)S(1)}, bf16[512,256]{1,0:T(8,128)(2,1)}, u32[]{:S(2)}) copy-start(bf16[512,256]{1,0:T(8,128)(2,1)} %constant.93.clone.refs_3_) | copy-start | bytes 786436
  6.2 28.8 %copy-start.3 = (bf16[512,256]{1,0:T(8,128)(2,1)S(1)}, bf16[512,256]{1,0:T(8,128)(2,1)}, u32[]{:S(2)}) copy-start(bf16[512,256]{1,0:T(8,128)(2,1)} %constant.91.clone.refs_1_) | copy-start | bytes 786436
  6.2 28.8 %copy-start.8 = (f32[1,2048]{1,0:T(1,128)S(1)}, f32[1,2048]{1,0:T(1,128)}, u32[]{:S(2)}) copy-start(f32[1,2048]{1,0:T(1,128)} %constant.89.clone.modes) | copy-start | bytes 24580
  7.6 4.5 %collective-permute-start.5 = (f32[9,32,512]{2,1,0:T(8,128)S(1)}, f32[9,32,512]{2,1,0:T(8,128)}, u32[]{:S(2)}, u32[]{:S(2)}) collective-permute-start(f32[9,32,512]{2,1,0:T(8,128)S(1)} %dynamic-slice_bitcast_fusion.1), channel_id=1, source_target_pairs={{0,1},{1,0},{2,3},{3,2},{4,5},{5,4},{6,7},{7,6},{8,9},{9,8},{10,11... | collective-permute-start | bytes 1769480 | tf_op jit(solution)/shard_map/ppermute | solution.py:454
  10.9 24.1 %collective-permute-start.1 = (f32[16,32,512]{2,1,0:T(8,128)}, f32[16,32,512]{2,1,0:T(8,128)}, u32[]{:S(2)}, u32[]{:S(2)}) collective-permute-start(f32[16,32,512]{2,1,0:T(8,128)} %dynamic-slice_bitcast_fusion), channel_id=1, source_target_pairs={{0,1},{1,0},{2,3},{3,2},{4,5},{5,4},{6,7},{7,6},{8,9},{9,8},{10,11... | collective-permute-start | bytes 3145736 | tf_op jit(solution)/shard_map/ppermute | solution.py:454
  14.3 35.1 %collective-permute-start.6 = (f32[2,9,32,512]{3,2,1,0:T(8,128)}, f32[2,9,32,512]{3,2,1,0:T(8,128)}, u32[]{:S(2)}, u32[]{:S(2)}) collective-permute-start(f32[2,9,32,512]{3,2,1,0:T(8,128)} %pad_maximum_fusion), channel_id=1, source_target_pairs={{0,2},{2,0},{1,3},{3,1},{4,6},{6,4},{5,7},{7,5},{8,10},{10,8},{9,1... | collective-permute-start | bytes 3538952 | tf_op jit(solution)/shard_map/ppermute | solution.py:454
  14.3 19.7 %collective-permute-start.3 = (f32[2,3,32,512]{3,2,1,0:T(8,128)}, f32[2,3,32,512]{3,2,1,0:T(8,128)S(1)}, u32[]{:S(2)}, u32[]{:S(2)}) collective-permute-start(f32[2,3,32,512]{3,2,1,0:T(8,128)} %get-tuple-element.27), channel_id=1, source_target_pairs={{0,4},{4,8},{8,12},{12,16},{16,20},{20,24},{24,28},{1,5},{5,9},{9,... | collective-permute-start | bytes 1179656 | tf_op jit(solution)/shard_map/ppermute | solution.py:478
  17.7 17.2 %collective-permute-start.4 = (f32[2,3,32,512]{3,2,1,0:T(8,128)}, f32[2,3,32,512]{3,2,1,0:T(8,128)S(1)}, u32[]{:S(2)}, u32[]{:S(2)}) collective-permute-start(f32[2,3,32,512]{3,2,1,0:T(8,128)} %copy-done.9), channel_id=1, source_target_pairs={{4,0},{8,4},{12,8},{16,12},{20,16},{24,20},{28,24},{5,1},{9,5},{13... | collective-permute-start | bytes 1179656 | tf_op jit(solution)/shard_map/ppermute | solution.py:478
  25.2 9.9 %collective-permute-start.2 = (f32[7,32,512]{2,1,0:T(8,128)S(1)}, f32[7,32,512]{2,1,0:T(8,128)S(1)}, u32[]{:S(2)}, u32[]{:S(2)}) collective-permute-start(f32[7,32,512]{2,1,0:T(8,128)S(1)} %dynamic-slice_bitcast_fusion.2), channel_id=1, source_target_pairs={{0,1},{1,0},{2,3},{3,2},{4,5},{5,4},{6,7},{7,6},{8,9},{9,8},{10,11... | collective-permute-start | bytes 1376264 | tf_op jit(solution)/shard_map/ppermute | solution.py:454
  34.1 0.8 copy-start.4
  34.9 12.0 %copy-start.6 = (f32[2,3,32,512]{3,2,1,0:T(8,128)}, f32[2,3,32,512]{3,2,1,0:T(8,128)S(1)}, u32[]{:S(2)}) copy-start(f32[2,3,32,512]{3,2,1,0:T(8,128)S(1)} %collective-permute-done.4.after) | copy-start | bytes 1179652
  46.8 22.2 %collective-permute-start.9 = (f32[2,7,32,512]{3,2,1,0:T(8,128)}, f32[2,7,32,512]{3,2,1,0:T(8,128)}, u32[]{:S(2)}, u32[]{:S(2)}) collective-permute-start(f32[2,7,32,512]{3,2,1,0:T(8,128)} %get-tuple-element.42), channel_id=1, source_target_pairs={{0,2},{2,0},{1,3},{3,1},{4,6},{6,4},{5,7},{7,5},{8,10},{10,8},{9,1... | collective-permute-start | bytes 2752520 | tf_op jit(solution)/shard_map/ppermute | solution.py:454
  49.4 2.9 %collective-permute-start.7 = (f32[7,32,512]{2,1,0:T(8,128)S(1)}, f32[7,32,512]{2,1,0:T(8,128)S(1)}, u32[]{:S(2)}, u32[]{:S(2)}) collective-permute-start(f32[7,32,512]{2,1,0:T(8,128)S(1)} %get-tuple-element.36), channel_id=1, source_target_pairs={{0,1},{1,0},{2,3},{3,2},{4,5},{5,4},{6,7},{7,6},{8,9},{9,8},{10,11... | collective-permute-start | bytes 1376264 | tf_op jit(solution)/shard_map/ppermute | solution.py:454
  67.0 7.2 %collective-permute-start.8 = (f32[9,32,512]{2,1,0:T(8,128)}, f32[9,32,512]{2,1,0:T(8,128)S(1)}, u32[]{:S(2)}, u32[]{:S(2)}) collective-permute-start(f32[9,32,512]{2,1,0:T(8,128)} %get-tuple-element.41), channel_id=1, source_target_pairs={{0,1},{1,0},{2,3},{3,2},{4,5},{5,4},{6,7},{7,6},{8,9},{9,8},{10,11... | collective-permute-start | bytes 1769480 | tf_op jit(solution)/shard_map/ppermute | solution.py:454
  67.4 18.3 %collective-permute-start.11 = (f32[9,32,512]{2,1,0:T(8,128)}, f32[9,32,512]{2,1,0:T(8,128)S(1)}, u32[]{:S(2)}, u32[]{:S(2)}) collective-permute-start(f32[9,32,512]{2,1,0:T(8,128)} %get-tuple-element.44), channel_id=1, source_target_pairs={{0,2},{2,0},{1,3},{3,1},{4,6},{6,4},{5,7},{7,5},{8,10},{10,8},{9,1... | collective-permute-start | bytes 1769480 | tf_op jit(solution)/shard_map/ppermute | solution.py:454
  71.1 3.1 %collective-permute-start.10 = (f32[7,32,512]{2,1,0:T(8,128)}, f32[7,32,512]{2,1,0:T(8,128)}, u32[]{:S(2)}, u32[]{:S(2)}) collective-permute-start(f32[7,32,512]{2,1,0:T(8,128)} %get-tuple-element.47), channel_id=1, source_target_pairs={{0,1},{1,0},{2,3},{3,2},{4,5},{5,4},{6,7},{7,6},{8,9},{9,8},{10,11... | collective-permute-start | bytes 1376264 | tf_op jit(solution)/shard_map/ppermute | solution.py:454
  72.3 19.6 %collective-permute-start.12 = (f32[6,32,512]{2,1,0:T(8,128)}, f32[6,32,512]{2,1,0:T(8,128)}, u32[]{:S(2)}, u32[]{:S(2)}) collective-permute-start(f32[6,32,512]{2,1,0:T(8,128)} %get-tuple-element.45), channel_id=1, source_target_pairs={{0,3},{3,0},{1,2},{2,1},{4,7},{7,4},{5,6},{6,5},{8,11},{11,8},{9,1... | collective-permute-start | bytes 1179656 | tf_op jit(solution)/shard_map/ppermute | solution.py:454
  73.6 21.9 %collective-permute-start.13 = (f32[3,32,512]{2,1,0:T(8,128)S(1)}, f32[3,32,512]{2,1,0:T(8,128)S(1)}, u32[]{:S(2)}, u32[]{:S(2)}) collective-permute-start(f32[3,32,512]{2,1,0:T(8,128)S(1)} %get-tuple-element.46), channel_id=1, source_target_pairs={{0,3},{3,0},{1,2},{2,1},{4,7},{7,4},{5,6},{6,5},{8,11},{11,8},{9,1... | collective-permute-start | bytes 589832 | tf_op jit(solution)/shard_map/ppermute | solution.py:454
  74.2 1.0 %copy-start.5 = (f32[2,3,32,512]{3,2,1,0:T(8,128)S(1)}, f32[2,3,32,512]{3,2,1,0:T(8,128)}, u32[]{:S(2)}) copy-start(f32[2,3,32,512]{3,2,1,0:T(8,128)} %copy-done.4) | copy-start | bytes 1179652
  75.2 1.0 %copy-start.7 = (f32[2,3,32,512]{3,2,1,0:T(8,128)S(1)}, f32[2,3,32,512]{3,2,1,0:T(8,128)}, u32[]{:S(2)}) copy-start(f32[2,3,32,512]{3,2,1,0:T(8,128)} %copy-done.6) | copy-start | bytes 1179652
